TPU v7x, 128 devices: a whole 4x4x4 slice. The times are simulated.
128 devices in a mesh: dp: 16 (over y, x), serve: 8 (over z, core).
Axes of the slice: x: 4, y: 4, z: 4, core: 2. Of those that a mesh axis runs over, the one named last changes fastest.
Arguments:
- inputs: bfloat16 [16384, 8192], P('dp', 'serve'), may hold values from -6 to 6
- cotangent: bfloat16 [16384, 4608], P('dp'), may hold values from -0.046875 to 0.046875
- master: float32 [8, 576, 128, 128], P('serve', 'dp'), may hold values from -0.12 to 0.12
- moment: float32 [8, 576, 128, 128], P('serve', 'dp'), may hold values from -1.8 to 1.8
- variance: float32 [8, 576, 128, 128], P('serve', 'dp'), may hold values from 0.01 to 1
- slice_start: int32 [16], replicated, may hold values from 0 to 279, as said below
- block_owner: int32 [36], replicated, may hold values from 0 to 7, as said below
- group_heads: int32 [32], replicated, may hold values from 0 to 31, each once
Outputs:
- new_master: float32 [8, 576, 128, 128], P('serve', 'dp')
- new_moment: float32 [8, 576, 128, 128], P('serve', 'dp')
- new_variance: float32 [8, 576, 128, 128], P('serve', 'dp')
- served_blocks: bfloat16 [8, 9, 8192, 128], P('serve', None, 'dp')
- served_scales: bfloat16 [8, 9, 64], P('serve', None, 'dp')
Inputs may be any that keep to these rules, and one draw needn't show every extreme that they name: Starts never fall; slice_start[0] = 0; every slice_start[i] lies within 9 blocks of i * 18, so a slice holds at most 36 blocks, and some rank's slice holds exactly 36. `block_owner`: each serving rank owns at most 9 packed column blocks, and some rank owns exactly 9.
All inputs are finite; a program needn't handle non-finite values.
Results may differ from a plain program's by a relative error of at most 0.024.
Values may be sent and summed in bfloat16 or wider, within the bound.
No kernel may reach another device: no remote copies, remote signals or barrier semaphores. Data moves between devices by JAX's collectives and lax.ppermute only.
A program may use at most 128 MiB of HBM per device.

v0:
```python
import jax
import jax.numpy as jnp
from jax import lax
from jax.sharding import PartitionSpec as P

QPER = 16
GROUPS = 2


first_bias = 1.0 - 0.9**10
second_bias = 1.0 - 0.95**10


def lookup(entries, indices):
    matches = indices[..., None] == jnp.arange(entries.shape[0], dtype=jnp.int32)
    return jnp.sum(jnp.where(matches, entries, 0), axis=-1)


def bucket_position(target, valid_mask, groups):
    matches = (target[..., None] == jnp.arange(groups, dtype=jnp.int32)) & valid_mask[..., None]
    running = jnp.cumsum(matches.astype(jnp.int32), axis=-2)
    return jnp.sum(jnp.where(matches, running, 0), axis=-1) - 1


def shards(inputs, cotangent, master, moment, variance, slice_start, block_owner, group_heads):
    data_ranks = lax.axis_size("dp")
    serve_ranks = lax.axis_size("serve")
    my_rank = lax.axis_index("dp")
    my_shard = lax.axis_index("serve")
    tokens_dev = inputs.shape[0]
    rows_shard = inputs.shape[1]
    tile_edge = master.shape[2]
    capacity = master.shape[1]
    col_blocks = block_owner.shape[0]
    row_blocks = rows_shard // tile_edge
    flat_count = row_blocks * col_blocks
    slice_len = flat_count // data_ranks
    owner_cap = 2 * col_blocks // serve_ranks
    pair_cap = min(capacity, owner_cap * ((2 * slice_len - 2) // col_blocks + 2))
    band_blocks = row_blocks * serve_ranks // data_ranks
    query_heads = group_heads.shape[0]
    per_group = col_blocks // GROUPS
    grad_flat = jnp.einsum(
        "tra,tcb->rcab",
        inputs.reshape(tokens_dev, row_blocks, tile_edge),
        cotangent.reshape(tokens_dev, col_blocks, tile_edge),
        preferred_element_type=jnp.float32,
    ).astype(jnp.bfloat16)
    grad_flat = grad_flat.reshape(flat_count, tile_edge, tile_edge)
    slice_ends = jnp.concatenate([slice_start[1:], jnp.full((1,), flat_count, jnp.int32)])
    counts = slice_ends - slice_start
    my_count = lookup(counts, my_rank)
    slot_index = jnp.arange(capacity, dtype=jnp.int32)
    my_valid = slot_index < my_count
    row_ids = jnp.arange(lax.axis_size("dp") * capacity, dtype=jnp.int32)
    owner_rank = row_ids // capacity
    offset = row_ids % capacity
    flat_ids = lookup(slice_start, owner_rank) + offset
    live_mask = offset < lookup(counts, owner_rank)
    picked = jnp.take(grad_flat, jnp.minimum(flat_ids, flat_count - 1), axis=0).astype(jnp.float32)
    slot_grad = lax.psum_scatter(
        jnp.where(live_mask[:, None, None], picked, jnp.float32(0.0)).astype(jnp.bfloat16),
        "dp",
        scatter_dimension=0,
        tiled=True,
    ).astype(jnp.float32)
    new_moment = 0.9 * moment + 0.1 * slot_grad[None]
    new_variance = 0.95 * variance + 0.05 * (slot_grad * slot_grad)[None]
    new_master = master - 0.02 * (
        new_moment / first_bias / (jnp.sqrt(new_variance / second_bias) + 1e-08) + 0.1 * master
    )
    peak_abs = jnp.max(jnp.abs(new_master[0]), axis=(1, 2))
    slot_scale = (peak_abs + 1e-06).astype(jnp.bfloat16)
    slot_code = (new_master[0] / slot_scale.astype(jnp.float32)[:, None, None]).astype(jnp.bfloat16)
    packed = jnp.arange(col_blocks, dtype=jnp.int32)
    groups_of = packed // per_group
    within = packed % per_group
    head_ids = lookup(group_heads, groups_of * QPER + jnp.minimum(within, QPER - 1))
    train_col = jnp.where(
        within < QPER,
        head_ids,
        jnp.where(within == QPER, query_heads + groups_of, query_heads + GROUPS + groups_of),
    )
    packed_of = jnp.sum(
        jnp.where(train_col[None, :] == packed[:, None], packed[None, :], 0), axis=1
    )
    earlier = (block_owner[None, :] == block_owner[:, None]) & (packed[None, :] < packed[:, None])
    slot_of = jnp.sum(earlier.astype(jnp.int32), axis=1)
    rank_grid = jnp.arange(data_ranks, dtype=jnp.int32)[:, None, None]
    shard_grid = jnp.arange(serve_ranks, dtype=jnp.int32)[None, :, None]
    offset_grid = slot_index[None, None, :]
    live_grid = offset_grid < counts[:, None, None]
    flat_grid = jnp.minimum(slice_start[:, None, None] + offset_grid, flat_count - 1)
    row_grid = shard_grid * row_blocks + flat_grid // col_blocks
    pack_grid = lookup(packed_of, flat_grid % col_blocks)
    dest_grid = lookup(block_owner, pack_grid)
    pos_grid = bucket_position(dest_grid, live_grid, serve_ranks)
    code_grid = jnp.where(live_grid, row_grid * col_blocks + pack_grid + 1, 0)
    my_dest = lax.dynamic_index_in_dim(dest_grid, my_rank, 0, keepdims=False)[0]
    my_pos = lax.dynamic_index_in_dim(pos_grid, my_rank, 0, keepdims=False)[0]
    target = jnp.where(my_valid, my_dest * pair_cap + my_pos, serve_ranks * pair_cap)
    send_codes = (
        jnp.zeros((serve_ranks * pair_cap, tile_edge, tile_edge), jnp.bfloat16)
        .at[target]
        .set(slot_code, mode="drop")
    )
    send_scales = (
        jnp.zeros((serve_ranks * pair_cap,), jnp.bfloat16).at[target].set(slot_scale, mode="drop")
    )
    got_codes, got_scales = (
        lax.all_to_all(
            send_codes.reshape(serve_ranks, pair_cap, tile_edge, tile_edge),
            "serve",
            split_axis=0,
            concat_axis=0,
            tiled=True,
        ),
        lax.all_to_all(
            send_scales.reshape(serve_ranks, pair_cap),
            "serve",
            split_axis=0,
            concat_axis=0,
            tiled=True,
        ),
    )
    total_items = serve_ranks * pair_cap
    mine = live_grid & (dest_grid == my_shard)
    item_index = jnp.where(
        mine, rank_grid * total_items + shard_grid * pair_cap + pos_grid, data_ranks * total_items
    )
    item_code = (
        jnp.zeros((data_ranks * total_items,), jnp.int32)
        .at[item_index.reshape(-1)]
        .set(code_grid.reshape(-1), mode="drop")
        .reshape(data_ranks, total_items)
    )
    item_live = item_code > 0
    band_dest = (item_code - 1) // col_blocks // band_blocks
    band_pos = bucket_position(band_dest, item_live, data_ranks)
    my_band = lax.dynamic_index_in_dim(band_dest, my_rank, 0, keepdims=False)
    my_band_pos = lax.dynamic_index_in_dim(band_pos, my_rank, 0, keepdims=False)
    my_items = lax.dynamic_index_in_dim(item_live, my_rank, 0, keepdims=False)
    target_band = jnp.where(my_items, my_band * pair_cap + my_band_pos, data_ranks * pair_cap)
    band_codes = (
        jnp.zeros((data_ranks * pair_cap, tile_edge, tile_edge), jnp.bfloat16)
        .at[target_band]
        .set(got_codes.reshape(total_items, tile_edge, tile_edge), mode="drop")
    )
    band_scales = (
        jnp.zeros((data_ranks * pair_cap,), jnp.bfloat16)
        .at[target_band]
        .set(got_scales.reshape(total_items), mode="drop")
    )
    final_codes, final_scales = (
        lax.all_to_all(
            band_codes.reshape(data_ranks, pair_cap, tile_edge, tile_edge),
            "dp",
            split_axis=0,
            concat_axis=0,
            tiled=True,
        ),
        lax.all_to_all(
            band_scales.reshape(data_ranks, pair_cap), "dp", split_axis=0, concat_axis=0, tiled=True
        ),
    )
    arrive = item_live & (band_dest == my_rank)
    source_rows = jnp.arange(data_ranks, dtype=jnp.int32)[:, None]
    arrive_index = jnp.where(arrive, source_rows * pair_cap + band_pos, data_ranks * pair_cap)
    arrive_code = (
        jnp.zeros((data_ranks * pair_cap,), jnp.int32)
        .at[arrive_index.reshape(-1)]
        .set(item_code.reshape(-1), mode="drop")
    )
    arrived = arrive_code > 0
    row_global = (arrive_code - 1) // col_blocks
    pack_ids = (arrive_code - 1) % col_blocks
    place_ids = lookup(slot_of, pack_ids) * band_blocks + row_global % band_blocks
    place_ids = jnp.where(arrived, place_ids, owner_cap * band_blocks)
    served = (
        jnp.zeros((owner_cap * band_blocks, tile_edge, tile_edge), jnp.bfloat16)
        .at[place_ids]
        .set(final_codes.reshape(data_ranks * pair_cap, tile_edge, tile_edge), mode="drop")
    )
    served_blocks = served.reshape(1, owner_cap, band_blocks * tile_edge, tile_edge)
    served_scales = (
        jnp.zeros((owner_cap * band_blocks,), jnp.bfloat16)
        .at[place_ids]
        .set(final_scales.reshape(-1), mode="drop")
        .reshape(1, owner_cap, band_blocks)
    )
    return (new_master, new_moment, new_variance, served_blocks, served_scales)


def solution(mesh):
    placed = (
        P("dp", "serve"),
        P("dp", None),
        P("serve", "dp", None, None),
        P("serve", "dp", None, None),
        P("serve", "dp", None, None),
        P(),
        P(),
        P(),
    )
    return jax.shard_map(
        shards,
        mesh=mesh,
        in_specs=placed,
        out_specs=(
            P("serve", "dp", None, None),
            P("serve", "dp", None, None),
            P("serve", "dp", None, None),
            P("serve", None, "dp", None),
            P("serve", None, "dp"),
        ),
        check_vma=False,
    )
```

profile of v0, /device:TPU:0, one launch (start us, length us, event | category | flops | bytes accessed | tf_op | source)
XLA Modules:
  0.0 514.4 jit_solution(6126189417811752300)
XLA Ops:
  7.3 0.9 slice.12
  8.1 1.4 fusion.49
  9.5 0.7 select_reduce_fusion.4
  10.3 12.7 %copy.73 = bf16[1024,4608]{0,1:T(8,128)(2,1)} copy(bf16[1024,4608]{1,0:T(8,128)(2,1)} %param.9) | data formatting | bytes 18874368 | tf_op args[1]
  23.0 15.7 %convert_bitcast_fusion = bf16[8,36,128,128]{2,3,0,1:T(8,128)(2,1)} fusion(bf16[1024,36,128,1]{0,2,3,1:T(8,128)(2,1)} %bitcast.69, bf16[1024,1024]{1,0:T(8,128)(2,1)S(1)} %copy-done), kind=kOutput, calls=%fused_computation.10 | convolution fusion | flops 9668395008 | bytes 20971520 | tf_op jit(solution)/shard_map/tra,tcb->rcab/dot_general | solution.py:43
  38.7 12.7 %copy.75 = bf16[8,36,128,128]{3,2,1,0:T(8,128)(2,1)} copy(bf16[8,36,128,128]{2,3,0,1:T(8,128)(2,1)} %convert_bitcast_fusion) | data formatting | bytes 18874368 | tf_op jit(solution)/shard_map/convert_element_type | solution.py:48
  51.4 19.7 %gather_fusion = bf16[576,128,128]{2,1,0:T(8,128)(2,1)} fusion(bf16[288,128,128]{2,1,0:T(8,128)(2,1)} %bitcast.66, s32[1024]{0:T(1024)S(1)} %pad_clamp_fusion), kind=kCustom, calls=%fused_computation | custom fusion | bytes 37751040 | tf_op jit(solution)/shard_map/jit(_take)/gather | solution.py:60
  71.1 20.5 %select_convert_fusion = bf16[576,128,128]{2,1,0:T(8,128)(2,1)} fusion(bf16[576,128,128]{2,1,0:T(8,128)(2,1)} %gather_fusion, pred[576]{0:T(1024)(128)(4,1)S(1)} %get-tuple-element.54, pred[576]{0:T(1024)(128)(4,1)S(1)} %get-tuple-element.53), kind=kLoop, calls=%fused_computation.9 | loop fusion | flops 37748736 | bytes 37749888 | tf_op jit(solution)/shard_map/convert_element_type | solution.py:62
  91.6 0.6 copy-done.5
  92.2 0.1 select_reduce_fusion.6
  92.3 0.1 select_reduce_fusion.5
  92.5 0.8 select_reduce_fusion.1
  93.2 0.8 select_reduce_fusion
  94.0 0.1 copy.76
  94.1 0.1 compare_and_fusion
  94.2 0.1 copy.77
  94.3 1.0 fusion.60
  95.3 0.2 add_reduce_fusion
  95.5 0.7 fusion.52
  96.2 119.1 %reduce-scatter.2.cloned.1.call-done = bf16[36,128,128]{2,1,0:T(8,128)(2,1)} async-done(((bf16[576,128,128]{2,1,0:T(8,128)(2,1)}), bf16[36,128,128]{2,1,0:T(8,128)(2,1)}) %reduce-scatter.2.cloned.1.call-update) | async-done | bytes 1179664 | tf_op jit(solution)/shard_map/reduce_scatter | solution.py:61
  215.3 8.6 %fusion.5 = (f32[36]{0:T(128)S(1)}, f32[1,36,128,128]{3,2,1,0:T(8,128)}, f32[1,36,128,128]{3,2,1,0:T(8,128)}, f32[1,36,128,128]{3,2,1,0:T(8,128)}) fusion(f32[1,36,128,128]{3,2,1,0:T(8,128)} %param.10, bf16[36,128,128]{2,1,0:T(8,128)(2,1)} %reduce-scatter.2.cloned.1.call-done, f32[1,36,128,128]{3,2,1,0:T(8,128)} %param.11, f32[1,36,128,128]{3,2,1,0:T(8,128)} %param.12), kind=kLoop, calls=%fused_computation.20 | loop fusion | flops 10616796 | bytes 15335568 | tf_op jit(solution)/shard_map/reduce_max | solution.py:72
  223.9 1.0 scatter_custom_fusion.5
  224.9 0.7 all_to_all.24
  225.5 4.4 all-to-all-start.2
  230.0 2.0 fusion.6
  232.0 3.3 broadcast_in_dim.226
  235.3 6.3 %scatter_fusion = bf16[144,128,128]{2,1,0:T(8,128)(2,1)} fusion(bf16[144,128,128]{2,1,0:T(8,128)(2,1)} %broadcast_in_dim.226, s32[36]{0:T(128)S(1)} %fusion.52, bf16[36,128,128]{2,1,0:T(8,128)(2,1)S(1)} %fusion.6), kind=kCustom, calls=%fused_computation.3 | custom fusion | bytes 3539088 | tf_op jit(solution)/shard_map/scatter | solution.py:105
  241.6 4.8 all-to-all-start
  246.4 0.1 copy.78
  246.5 0.1 copy.80
  246.6 0.1 copy.79
  246.7 0.1 add_select_fusion
  246.8 0.1 select_n.348
  246.9 0.1 reshape.668
  247.1 17.4 %scatter_custom_fusion = s32[2304]{0:T(1024)S(1)} fusion(s32[4608]{0:T(1024)S(1)} %fusion.22, s32[4608]{0:T(1024)S(1)} %reshape.668, s32[]{:T(128)} %constant.109.clone.1), kind=kCustom, calls=%fused_computation.104 | custom fusion | bytes 9220 | tf_op jit(solution)/shard_map/scatter | solution.py:134
  264.5 0.1 and.191
  264.7 0.1 div.113
  264.7 0.1 gt.19
  265.0 9.1 %reduce-window.6 = s32[16,16,2,128]{3,1,2,0:T(8,128)S(1)} reduce-window(s32[16,16,2,128]{3,1,2,0:T(8,128)S(1)} %copy_bitcast_fusion, s32[]{:T(128)} %constant.109.clone.1), window={size=1x1x1x128 pad=0_0x0_0x0_0x127_0}, to_apply=%region_10.11 | reduce-window | flops 8323072 | bytes 524292 | tf_op jit(solution)/shard_map/reduce-window
  274.0 0.1 slice.18
  274.2 0.3 copy.82
  274.5 0.1 bitcast_bitcast_fusion.2
  274.7 0.1 fusion.11
  274.8 0.1 broadcast_add_fusion.1
  274.9 0.1 reshape.716
  275.0 1.5 scatter_custom_fusion.6
  276.5 0.7 all_to_all.25
  277.1 24.7 %all-to-all-done = bf16[8,18,128,128]{3,2,1,0:T(8,128)(2,1)} async-done(((bf16[8,18,128,128]{3,2,1,0:T(8,128)(2,1)}), bf16[8,18,128,128]{3,2,1,0:T(8,128)(2,1)}, u32[]{:S(2)}, u32[]{:S(2)}) %all-to-all-start) | async-done | bytes 4718624 | tf_op jit(solution)/shard_map/all_to_all | solution.py:111
  301.8 4.9 all-to-all-start.3
  306.7 6.0 %broadcast_in_dim.223 = bf16[288,128,128]{2,1,0:T(8,128)(2,1)} broadcast(bf16[]{:T(256)} %constant.191.clone.1), dimensions={} | broadcast | bytes 9437186 | tf_op jit(solution)/shard_map/broadcast_in_dim | solution.py:145
  312.8 21.2 %scatter_fusion.1 = bf16[288,128,128]{2,1,0:T(8,128)(2,1)} fusion(bf16[288,128,128]{2,1,0:T(8,128)(2,1)} %broadcast_in_dim.223, s32[144]{0:T(256)S(1)} %bitcast.71, bf16[144,128,128]{2,1,0:T(8,128)(2,1)} %bitcast.15), kind=kCustom, calls=%fused_computation.4 | custom fusion | bytes 14156352 | tf_op jit(solution)/shard_map/scatter | solution.py:147
  333.9 6.8 %all-to-all-start.1 = ((bf16[16,18,128,128]{3,2,1,0:T(8,128)(2,1)}), bf16[16,18,128,128]{3,2,1,0:T(8,128)(2,1)}, u32[]{:S(2)}, u32[]{:S(2)}) async-start(bf16[16,18,128,128]{3,2,1,0:T(8,128)(2,1)} %bitcast.67), calls=%async_computation.2 | async-start | bytes 18874368 | tf_op jit(solution)/shard_map/all_to_all | solution.py:155
  340.8 0.1 add.432
  340.9 9.0 %scatter_custom_fusion.1 = s32[288]{0:T(512)S(1)} fusion(s32[2304]{0:T(1024)S(1)} %compare_select_fusion.1, s32[2304]{0:T(1024)S(1)} %scatter_custom_fusion, s32[]{:T(128)} %constant.109.clone.1), kind=kCustom, calls=%fused_computation.147 | custom fusion | bytes 1156 | tf_op jit(solution)/shard_map/scatter | solution.py:172
  349.9 0.2 convert_reduce_fusion
  350.0 0.1 select_reduce_fusion.2
  350.2 0.1 reshape.724
  350.3 2.4 scatter_custom_fusion.7
  352.7 0.1 reshape.652
  352.8 0.7 copy.87
  353.4 124.6 %all-to-all-done.1 = bf16[16,18,128,128]{3,2,1,0:T(8,128)(2,1)} async-done(((bf16[16,18,128,128]{3,2,1,0:T(8,128)(2,1)}), bf16[16,18,128,128]{3,2,1,0:T(8,128)(2,1)}, u32[]{:S(2)}, u32[]{:S(2)}) %all-to-all-start.1) | async-done | bytes 9437216 | tf_op jit(solution)/shard_map/all_to_all | solution.py:155
  478.1 0.3 broadcast_in_dim.201
  478.3 28.2 %scatter_fusion.2 = bf16[36,128,128]{2,1,0:T(8,128)(2,1)S(1)} fusion(bf16[36,128,128]{2,1,0:T(8,128)(2,1)S(1)} %broadcast_in_dim.201, s32[288]{0:T(512)S(1)} %compare_select_fusion.5, bf16[288,128,128]{2,1,0:T(8,128)(2,1)} %bitcast.17), kind=kCustom, calls=%fused_computation.5 | custom fusion | bytes 28312704 | tf_op jit(solution)/shard_map/scatter | solution.py:182
  506.6 1.0 copy-done.2
  (43 shorter events, 0.7 us)
Async XLA Ops:
  7.2 15.8 %copy-start = (bf16[1024,1024]{1,0:T(8,128)(2,1)S(1)}, bf16[1024,1024]{1,0:T(8,128)(2,1)}, u32[]{:S(2)}) copy-start(bf16[1024,1024]{1,0:T(8,128)(2,1)} %param.8) | copy-start | bytes 6291460
  7.2 208.1 %reduce-scatter.2.cloned.1.call-start = ((), (), s32[]{:S(2)}) async-start(), calls=%async_computation.5 | async-start | bytes 20054016 | tf_op jit(solution)/shard_map/reduce_scatter | solution.py:61
  91.5 0.7 copy-start.5
  91.5 0.9 copy-start.3
  91.5 1.7 copy-start.4
  225.5 16.1 %all-to-all-start.2 = ((bf16[8,1,18]{2,1,0:T(2,128)(2,1)}), bf16[8,1,18]{2,1,0:T(2,128)(2,1)S(1)}, u32[]{:S(2)}, u32[]{:S(2)}) async-start(bf16[8,1,18]{2,1,0:T(2,128)(2,1)} %all_to_all.24), calls=%async_computation.3 | async-start | bytes 8192 | tf_op jit(solution)/shard_map/all_to_all | solution.py:118
  241.6 60.2 %all-to-all-start = ((bf16[8,18,128,128]{3,2,1,0:T(8,128)(2,1)}), bf16[8,18,128,128]{3,2,1,0:T(8,128)(2,1)}, u32[]{:S(2)}, u32[]{:S(2)}) async-start(bf16[8,18,128,128]{3,2,1,0:T(8,128)(2,1)} %bitcast.68), calls=%async_computation.1 | async-start | bytes 9437184 | tf_op jit(solution)/shard_map/all_to_all | solution.py:111
  301.8 32.1 %all-to-all-start.3 = ((bf16[16,1,18]{2,1,0:T(2,128)(2,1)}), bf16[16,1,18]{2,1,0:T(2,128)(2,1)S(1)}, u32[]{:S(2)}, u32[]{:S(2)}) async-start(bf16[16,1,18]{2,1,0:T(2,128)(2,1)} %all_to_all.25), calls=%async_computation.4 | async-start | bytes 16384 | tf_op jit(solution)/shard_map/all_to_all | solution.py:162
  333.9 144.1 %all-to-all-start.1 = ((bf16[16,18,128,128]{3,2,1,0:T(8,128)(2,1)}), bf16[16,18,128,128]{3,2,1,0:T(8,128)(2,1)}, u32[]{:S(2)}, u32[]{:S(2)}) async-start(bf16[16,18,128,128]{3,2,1,0:T(8,128)(2,1)} %bitcast.67), calls=%async_computation.2 | async-start | bytes 18874368 | tf_op jit(solution)/shard_map/all_to_all | solution.py:155
  478.3 29.2 %copy-start.1 = (bf16[1024,1024]{1,0:T(8,128)(2,1)S(1)}, bf16[1024,1024]{1,0:T(8,128)(2,1)}, u32[]{:S(2)}) copy-start(bf16[1024,1024]{1,0:T(8,128)(2,1)} %param.8) | copy-start | bytes 6291460
  506.5 1.0 copy-start.2
Sparse Core Ops, SparseCore 0:
  91.7 123.5 reduce-scatter.1
where the time goes:
time: 517 us; the launch traced here: 514 us
  waiting for transfers between devices  268 us (52%)
  local copies, waits for them, and re-layouts  148 us (29%)
  other arithmetic  47.2 us (9%)
  starting transfers between devices  21 us (4%)
  matrix products  15.7 us (3%)
  between operations  14.4 us (3%)
    all_to_all x1, waiting for transfers between devices, shards(): lax.all_to_all(band_codes.reshape(data_ranks, pair_cap, tile_edge, tile_e...  125 us
    reduce_scatter x1, waiting for transfers between devices, shards(): lax.psum_scatter(jnp.where(live_mask[:, None, None], picked, jnp.float32(...  119 us
    scatter x1, local copies, waits for them, and re-layouts, shards(): served = jnp.zeros((owner_cap * band_blocks, tile_edge, tile_edge), jnp.b...  28.2 us
    all_to_all x1, waiting for transfers between devices, shards(): lax.all_to_all(send_codes.reshape(serve_ranks, pair_cap, tile_edge, tile_...  24.7 us
    scatter x1, local copies, waits for them, and re-layouts, shards(): band_codes = jnp.zeros((data_ranks * pair_cap, tile_edge, tile_edge), jnp...  21.2 us
    convert_element_type x1, other arithmetic, shards(): jnp.where(live_mask[:, None, None], picked, jnp.float32(0.0))  20.5 us
    gather x1, local copies, waits for them, and re-layouts, shards(): jnp.take(grad_flat, jnp.minimum(flat_ids, flat_count - 1), axis=0)  19.7 us
    scatter x1, local copies, waits for them, and re-layouts, shards(): item_code = jnp.zeros((data_ranks * total_items,), jnp.int32).at[item_ind...  17.4 us
  transfers between devices with their start and end apart: 5, of which 3 were waited for; matrix products, arithmetic and copies ran while one was open for 17% of the time, Pallas kernels for 0%

commit v1 on v0

v1 whole, which is shorter than its diff:
```python
import jax
import jax.numpy as jnp
from jax import lax
from jax.experimental import pallas as pl
from jax.experimental.pallas import tpu as pltpu
from jax.sharding import PartitionSpec as P

QPER = 16
GROUPS = 2
BLK = 128
HALF = 64
UNIT = 9
WIDE = UNIT * BLK
CAP = 36
COLS = 36
SCAP = 9
MSG = SCAP * HALF + 16

first_bias = 1.0 - 0.9**10
second_bias = 1.0 - 0.95**10

BF = jnp.bfloat16
F32 = jnp.float32


def cost(flops, nbytes):
    return pl.CostEstimate(flops=flops, bytes_accessed=nbytes, transcendentals=0)


def params(mib=48):
    return pltpu.CompilerParams(vmem_limit_bytes=mib * 1024 * 1024)


def mm_body(table, left_a, left_b, right, out):
    left = jnp.concatenate([left_a[...], left_b[...]], axis=1)
    prod = lax.dot_general(
        left, right[...], (((0,), (0,)), ((), ())), preferred_element_type=F32
    )
    out[0] = prod[:BLK].astype(BF)
    out[1] = prod[BLK:].astype(BF)


def mm(table, inputs, cotangent):
    n = table.shape[1]
    tok = inputs.shape[0]
    return pl.pallas_call(
        mm_body,
        grid_spec=pltpu.PrefetchScalarGridSpec(
            num_scalar_prefetch=1,
            grid=(n,),
            in_specs=[
                pl.BlockSpec((tok, BLK), lambda g, t: (0, t[0, g])),
                pl.BlockSpec((tok, BLK), lambda g, t: (0, t[1, g])),
                pl.BlockSpec((tok, WIDE), lambda g, t: (0, t[2, g])),
            ],
            out_specs=pl.BlockSpec((2, BLK, WIDE), lambda g, t: (g, 0, 0)),
        ),
        out_shape=jax.ShapeDtypeStruct((2 * n, BLK, WIDE), BF),
        compiler_params=params(),
        cost_estimate=cost(
            2 * n * 256 * WIDE * tok, n * tok * (WIDE + 256) * 2 + n * 256 * WIDE * 2
        ),
        name="gradient_pieces",
    )(table, inputs, inputs, cotangent)


def adam_body(
    info, halo_b, grad_a, grad_b, halo_a, master, moment, variance,
    new_master, new_moment, new_variance, send3, send1, keep1, keep3,
    window, mine, other, scales,
):
    step = pl.program_id(0)
    off, length, odd = info[0], info[1], info[2]

    @pl.when(step == 0)
    def _():
        window[0] = halo_b[...]
        window[1] = grad_a[...]
        window[2] = grad_b[...]
        window[3] = halo_a[...]

    for n in range(4):
        slot = step * 4 + n
        place = off + slot
        place = jnp.where(place >= CAP, place - CAP, place)
        unit = lax.div(place, UNIT)
        lanes = pl.ds(pl.multiple_of((place - unit * UNIT) * BLK, BLK), BLK)
        live = slot < length
        grad = jnp.where(live, window[unit, :, lanes].astype(F32), 0.0)
        mom = 0.9 * moment[0, n] + 0.1 * grad
        var = 0.95 * variance[0, n] + 0.05 * (grad * grad)
        old = master[0, n]
        new = old - 0.02 * (
            (mom * (1.0 / first_bias)) / (jnp.sqrt(var * (1.0 / second_bias)) + 1e-08) + 0.1 * old
        )
        new_master[0, n] = new
        new_moment[0, n] = mom
        new_variance[0, n] = var
        peak = jnp.max(jnp.abs(new), axis=(0, 1), keepdims=True)
        scale = (peak + 1e-06).astype(BF).astype(F32)
        code = jnp.where(live, new * (1.0 / scale), 0.0).astype(BF)
        spot = jnp.where(odd == 1, unit, lax.rem(unit + 3, 4))
        top, low = code[:HALF], code[HALF:]
        mine[spot, :, lanes] = jnp.where(odd == 1, low, top)
        other[spot, :, lanes] = jnp.where(odd == 1, top, low)
        scales[spot, :, lanes] = jnp.broadcast_to(jnp.where(live, scale, 0.0), (8, BLK))

    @pl.when(step == pl.num_programs(0) - 1)
    def _():
        tail = jnp.concatenate(
            [scales[q, 0:1] for q in range(4)] + [jnp.zeros((12, WIDE), F32)], axis=0
        ).astype(BF)
        for q in range(3):
            send3[q * HALF : (q + 1) * HALF] = other[q]
            keep3[q * HALF : (q + 1) * HALF] = mine[q]
        send3[3 * HALF :] = tail
        keep3[3 * HALF :] = tail
        send1[:HALF] = other[3]
        send1[HALF:] = tail
        keep1[:HALF] = mine[3]
        keep1[HALF:] = tail


def adam(info, halo_b, grad_a, grad_b, halo_a, master, moment, variance):
    whole = lambda rows: pl.BlockSpec((rows, WIDE), lambda s, t: (0, 0))
    state = pl.BlockSpec((1, 4, BLK, BLK), lambda s, t: (0, s, 0, 0))
    wide = lambda rows: jax.ShapeDtypeStruct((rows, WIDE), BF)
    slots = jax.ShapeDtypeStruct(master.shape, F32)
    return pl.pallas_call(
        adam_body,
        grid_spec=pltpu.PrefetchScalarGridSpec(
            num_scalar_prefetch=1,
            grid=(CAP // 4,),
            in_specs=[whole(BLK)] * 4 + [state] * 3,
            out_specs=[state] * 3
            + [whole(3 * HALF + 16), whole(HALF + 16), whole(HALF + 16), whole(3 * HALF + 16)],
            scratch_shapes=[
                pltpu.VMEM((4, BLK, WIDE), BF),
                pltpu.VMEM((4, HALF, WIDE), BF),
                pltpu.VMEM((4, HALF, WIDE), BF),
                pltpu.VMEM((4, 8, WIDE), F32),
            ],
        ),
        out_shape=[slots] * 3
        + [wide(3 * HALF + 16), wide(HALF + 16), wide(HALF + 16), wide(3 * HALF + 16)],
        compiler_params=params(),
        cost_estimate=cost(36 * 16384 * 20, 36 * 16384 * 28),
        name="adam_slots",
    )(info, halo_b, grad_a, grad_b, halo_a, master, moment, variance)


def pack_body(info, keep3, got3, got1, got2, out, row, tails):
    odd = info[0]

    def take(ref, q):
        return ref[q * HALF : (q + 1) * HALF]

    def tail(ref, n):
        return ref[n * HALF :].astype(F32)

    @pl.when(odd == 0)
    def _():
        row[0] = take(keep3, 0) + got1[:HALF]
        row[1] = take(keep3, 1) + take(got3, 0)
        row[2] = take(keep3, 2) + take(got3, 1)
        row[3] = take(got3, 2) + got2[:HALF]
        own, pair, near, far = tail(keep3, 3), tail(got3, 3), tail(got1, 1), tail(got2, 1)
        tails[0, 0:1] = own[0:1] + near[3:4]
        tails[1, 0:1] = own[1:2] + pair[0:1]
        tails[2, 0:1] = own[2:3] + pair[1:2]
        tails[3, 0:1] = pair[2:3] + far[3:4]

    @pl.when(odd == 1)
    def _():
        row[0] = take(got3, 0) + got2[:HALF]
        row[1] = take(keep3, 0) + take(got3, 1)
        row[2] = take(keep3, 1) + take(got3, 2)
        row[3] = take(keep3, 2) + got1[:HALF]
        own, pair, near, far = tail(keep3, 3), tail(got3, 3), tail(got1, 1), tail(got2, 1)
        tails[0, 0:1] = pair[0:1] + far[3:4]
        tails[1, 0:1] = own[0:1] + pair[1:2]
        tails[2, 0:1] = own[1:2] + pair[2:3]
        tails[3, 0:1] = own[2:3] + near[3:4]

    def owner(o, carry):
        rows = []
        for t in range(SCAP):
            col = info[1 + o * SCAP + t]
            held = jnp.maximum(col, 0)
            unit = lax.div(held, UNIT)
            lanes = pl.ds(pl.multiple_of((held - unit * UNIT) * BLK, BLK), BLK)
            piece = row[unit, :, lanes]
            out[o, t * HALF : (t + 1) * HALF] = jnp.where(col >= 0, piece, jnp.zeros_like(piece))
            rows.append(jnp.where(col >= 0, tails[unit, :, lanes][0:1], 0.0))
        rows.append(jnp.zeros((16 - SCAP, BLK), F32))
        out[o, SCAP * HALF :] = jnp.concatenate(rows, axis=0).astype(BF)
        return carry

    lax.fori_loop(0, 8, owner, 0)


def pack(info, keep3, got3, got1, got2):
    return pl.pallas_call(
        pack_body,
        grid_spec=pltpu.PrefetchScalarGridSpec(
            num_scalar_prefetch=1,
            grid=(1,),
            in_specs=[
                pl.BlockSpec(a.shape, lambda s, t: (0, 0)) for a in (keep3, got3, got1, got2)
            ],
            out_specs=pl.BlockSpec((8, MSG, BLK), lambda s, t: (0, 0, 0)),
            scratch_shapes=[pltpu.VMEM((4, HALF, WIDE), BF), pltpu.VMEM((4, 8, WIDE), F32)],
        ),
        out_shape=jax.ShapeDtypeStruct((8, MSG, BLK), BF),
        compiler_params=params(),
        cost_estimate=cost(0, 3 * 8 * MSG * BLK * 2),
        name="pack_by_owner",
    )(info, keep3, got3, got1, got2)


def split_body(info, got, *outs):
    for j, out in enumerate(outs):
        out[...] = got[info[j]]


def split(info, got):
    return pl.pallas_call(
        split_body,
        grid_spec=pltpu.PrefetchScalarGridSpec(
            num_scalar_prefetch=1,
            grid=(1,),
            in_specs=[pl.BlockSpec(got.shape, lambda s, t: (0, 0, 0))],
            out_specs=[pl.BlockSpec(got.shape[1:], lambda s, t: (0, 0))] * 8,
        ),
        out_shape=[jax.ShapeDtypeStruct(got.shape[1:], BF)] * 8,
        compiler_params=params(),
        cost_estimate=cost(0, 2 * 8 * MSG * BLK * 2),
        name="split_by_band",
    )(info, got)


def place_body(info, *refs):
    out, tails = refs[8], refs[9]
    for j in range(8):
        at = info[j]
        for t in range(SCAP):
            out[0, t, pl.ds(pl.multiple_of(at * HALF, HALF), HALF)] = refs[j][
                t * HALF : (t + 1) * HALF
            ]
        tails[at] = refs[j][SCAP * HALF :]


def place(info, pieces):
    return pl.pallas_call(
        place_body,
        grid_spec=pltpu.PrefetchScalarGridSpec(
            num_scalar_prefetch=1,
            grid=(1,),
            in_specs=[pl.BlockSpec((MSG, BLK), lambda s, t: (0, 0))] * 8,
            out_specs=[
                pl.BlockSpec((1, SCAP, 8 * HALF, BLK), lambda s, t: (0, 0, 0, 0)),
                pl.BlockSpec((8, 16, BLK), lambda s, t: (0, 0, 0)),
            ],
        ),
        out_shape=[
            jax.ShapeDtypeStruct((1, SCAP, 8 * HALF, BLK), BF),
            jax.ShapeDtypeStruct((8, 16, BLK), BF),
        ],
        compiler_params=params(),
        cost_estimate=cost(0, 2 * 8 * MSG * BLK * 2),
        name="place_served",
    )(info, *pieces)


def add(*parts):
    total = parts[0].astype(F32)
    for part in parts[1:]:
        total = total + part.astype(F32)
    return total.astype(BF)


def shards(inputs, cotangent, master, moment, variance, slice_start, block_owner, group_heads):
    me = lax.axis_index("dp").astype(jnp.int32)
    shard = lax.axis_index("serve").astype(jnp.int32)
    y, x = me // 4, me % 4
    ranks = range(16)

    def along_x(k):
        return [(i, i // 4 * 4 + (i + k) % 4) for i in ranks]

    def along_y(k):
        return [(i, (i + 4 * k) % 16) for i in ranks]

    def send(v, pairs):
        return lax.ppermute(v, "dp", pairs)

    def first(k, half):
        to_x = (x + k) % 4
        rows = [2 * ((y + j) % 4) + to_x // 2 for j in ((0, 2) if half == 0 else (1, 3))]
        return rows[0], rows[1], (to_x % 2) * 2

    def last(k, half):
        to_y = (y + k) % 4
        tos = [(x + j) % 4 for j in ((0, 2) if half == 0 else (1, 3))]
        return 2 * to_y + tos[0] // 2, 2 * to_y + tos[1] // 2, (tos[0] % 2) * 2 + 1

    def pieces(groups):
        table = jnp.stack([jnp.stack([g[n] for g in groups]) for n in range(3)])
        return mm(table.astype(jnp.int32), inputs, cotangent)

    def long_send(which, along):
        fwd = pieces([which(2, 0), which(1, 1)])
        got_fwd = send(fwd, along(1))
        bwd = pieces([which(2, 1), which(3, 0)])
        got_bwd = send(bwd, along(-1))
        return got_fwd, got_bwd

    a_fwd, a_bwd = long_send(first, along_x)
    b_fwd, b_bwd = long_send(last, along_y)
    rest_a = pieces([first(1, 0), first(3, 1), first(0, 0), first(0, 1)])
    rest_b = pieces([last(1, 0), last(3, 1), last(0, 0), last(0, 1)])

    def long_end(rest, fwd, bwd, along):
        fwd2 = send(add(rest[0:2], fwd[0:2]), along(1))
        bwd2 = send(add(rest[2:4], bwd[0:2]), along(-1))
        even = add(rest[4:6], fwd2, bwd[2:4])
        odd = add(rest[6:8], bwd2, fwd[2:4])
        return even[0], odd[0], even[1], odd[1]

    part_a = long_end(rest_a, a_fwd, a_bwd, along_x)
    part_b = long_end(rest_b, b_fwd, b_bwd, along_y)

    def short(parts, along):
        got = [send(parts[k], along(k)) for k in (2, 1, 3)]
        return add(parts[0], *got)

    grad_a = short(part_a, along_y)
    grad_b = short(part_b, along_x)
    halo_a = send(grad_a, [(i + 1, i) for i in range(15)])
    halo_b = send(grad_b, [(i, i + 1) for i in range(15)])

    flat = 16 * 18
    ends = jnp.concatenate([slice_start[1:], jnp.full((1,), flat, jnp.int32)])
    is_me = jnp.arange(16, dtype=jnp.int32) == me
    start = jnp.sum(jnp.where(is_me, slice_start, 0))
    end = jnp.sum(jnp.where(is_me, ends, 0))
    odd = x % 2
    info = jnp.stack([start - (18 * me - 9), end - start, odd]).astype(jnp.int32)
    new_master, new_moment, new_variance, send3, send1, keep1, keep3 = adam(
        info, halo_b, grad_a, grad_b, halo_a, master, moment, variance
    )

    got3 = send(send3, [(i, i ^ 1) for i in ranks])
    got1 = send(
        send1, [(i, i - 1 if i % 2 == 0 else i + 1) for i in ranks if 0 < i < 15]
    )
    got2 = send(
        keep1,
        [
            (i, i - 2 if i % 2 == 0 else i + 2)
            for i in ranks
            if 0 <= (i - 2 if i % 2 == 0 else i + 2) < 16
        ],
    )

    packed = jnp.arange(COLS, dtype=jnp.int32)
    per_group = COLS // GROUPS
    group, within = packed // per_group, packed % per_group
    head_at = group * QPER + jnp.minimum(within, QPER - 1)
    heads = jnp.arange(group_heads.shape[0], dtype=jnp.int32)
    head = jnp.sum(jnp.where(head_at[:, None] == heads, group_heads, 0), axis=1)
    n_heads = group_heads.shape[0]
    column = jnp.where(
        within < QPER, head, jnp.where(within == QPER, n_heads + group, n_heads + GROUPS + group)
    )
    earlier = (block_owner[None, :] == block_owner[:, None]) & (packed[None, :] < packed[:, None])
    spot = block_owner * SCAP + jnp.sum(earlier.astype(jnp.int32), axis=1)
    spots = jnp.arange(8 * SCAP, dtype=jnp.int32)
    table = jnp.sum(jnp.where(spots[:, None] == spot[None, :], column + 1, 0), axis=1) - 1
    out = pack(
        jnp.concatenate([odd[None], table]).astype(jnp.int32), keep3, got3, got1, got2
    )
    got = lax.all_to_all(out, "serve", split_axis=0, concat_axis=0, tiled=True)
    turns = jnp.arange(8, dtype=jnp.int32)
    parts = split((me % 8) ^ turns, got)
    landed = [
        send(parts[j], [(i, 2 * ((i % 8) ^ j) + i // 8) for i in ranks]) for j in range(8)
    ]
    served_blocks, tails = place((me // 2) ^ turns, landed)
    served_scales = tails[0::2, :SCAP, 0].T[None]
    return new_master, new_moment, new_variance, served_blocks, served_scales


def solution(mesh):
    state = P("serve", "dp", None, None)
    return jax.shard_map(
        shards,
        mesh=mesh,
        in_specs=(P("dp", "serve"), P("dp", None), state, state, state, P(), P(), P()),
        out_specs=(state, state, state, P("serve", None, "dp", None), P("serve", None, "dp")),
        check_vma=False,
    )
```

time: 517 us -> 200 us (0.39)
  waiting for transfers between devices: 268 us -> 66.8 us
  local copies, waits for them, and re-layouts: 148 us -> 5.29 us
  Pallas kernels: 0 us -> 47.9 us
  starting transfers between devices: 21 us -> 63.9 us
  other arithmetic: 47.2 us -> 11.4 us
  matrix products: 15.7 us -> 0 us
  between operations: 14.4 us -> 3.14 us
    all_to_all x4 -> x1, waiting for transfers between devices: 149 us -> 17.7 us  [shards(): got = lax.all_to_all(out, 'serve', split_axis=0, concat_axis=0, tiled=True)]
    reduce_scatter x1 -> x0, waiting for transfers between devices: 119 us -> none  [shards(): lax.psum_scatter(jnp.where(live_mask[:, None, None], picked, jnp.float32(...]
    scatter x8 -> x0, local copies, waits for them, and re-layouts: 86.8 us -> none  [the longest x1 28.2 us: shards(): served = jnp.zeros((owner_cap * band_blocks, tile_edge, tile_edge), jnp.b...]
    ppermute x0 -> x27, starting transfers between devices: none -> 58.6 us  [send(): return lax.ppermute(v, 'dp', pairs)]
    ppermute x0 -> x27, waiting for transfers between devices: none -> 49.1 us  [send(): return lax.ppermute(v, 'dp', pairs)]
    pallas_call x0 -> x10, Pallas kernels: none -> 47.9 us  [the longest x6 33.2 us: mm(): pl.pallas_call(mm_body, grid_spec=pltpu.PrefetchScalarGridSpec(num_scalar...]
    gather x1 -> x0, local copies, waits for them, and re-layouts: 19.7 us -> none  [shards(): jnp.take(grad_flat, jnp.minimum(flat_ids, flat_count - 1), axis=0)]
    all_to_all x4 -> x1, starting transfers between devices: 21 us -> 5.26 us  [shards(): got = lax.all_to_all(out, 'serve', split_axis=0, concat_axis=0, tiled=True)]
  transfers between devices with their start and end apart: 5 -> 28, of which waited for: 3 -> 12; matrix products, arithmetic and copies ran while one was open for 17% -> 6% of each run, Pallas kernels for 0% -> 15%
where the time goes in v1:
time: 200 us; the launch traced here: 198 us
  waiting for transfers between devices  66.8 us (33%)
  starting transfers between devices  63.9 us (32%)
  Pallas kernels  47.9 us (24%)
  other arithmetic  11.4 us (6%)
  local copies, waits for them, and re-layouts  5.29 us (3%)
  between operations  3.14 us (2%)
    ppermute x27, starting transfers between devices, send(): return lax.ppermute(v, 'dp', pairs)  58.6 us
    ppermute x27, waiting for transfers between devices, send(): return lax.ppermute(v, 'dp', pairs)  49.1 us
    pallas_call x6, Pallas kernels, mm(): pl.pallas_call(mm_body, grid_spec=pltpu.PrefetchScalarGridSpec(num_scalar...  33.2 us
    all_to_all x1, waiting for transfers between devices, shards(): got = lax.all_to_all(out, 'serve', split_axis=0, concat_axis=0, tiled=True)  17.7 us
    pallas_call x1, Pallas kernels, adam(): pl.pallas_call(adam_body, grid_spec=pltpu.PrefetchScalarGridSpec(num_scal...  10.1 us
    convert_element_type x8, other arithmetic, add(): return total.astype(BF)  9.22 us
    all_to_all x1, starting transfers between devices, shards(): got = lax.all_to_all(out, 'serve', split_axis=0, concat_axis=0, tiled=True)  5.26 us
    unnamed x20, local copies, waits for them, and re-layouts  4.42 us
  transfers between devices with their start and end apart: 28, of which 12 were waited for; matrix products, arithmetic and copies ran while one was open for 6% of the time, Pallas kernels for 15%

profile of v1, /device:TPU:0, one launch (start us, length us, event | category | flops | bytes accessed | tf_op | source)
XLA Modules:
  0.0 198.3 jit_solution(7039201705091959787)
XLA Ops:
  1.2 1.6 copy-done
  2.8 4.2 %gradient_pieces.7 = bf16[4,128,1152]{2,1,0:T(8,128)(2,1)S(1)} custom-call(s32[3,2]{1,0:T(4,128)S(1)} %pad_add_fusion.1.table, bf16[1024,1024]{1,0:T(8,128)(2,1)S(1)} %copy-done, bf16[1024,1024]{1,0:T(8,128)(2,1)S(1)} %copy-done, bf16[1024,4608]{1,0:T(8,128)(2,1)} %right.11), custom_call_target="tpu_custom_call" | custom-call | flops 1207959552 | bytes 6946816 | tf_op jit(solution)/shard_map/gradient_pieces/pallas_call | solution.py:46
  7.0 1.7 collective-permute-start
  8.8 5.0 %gradient_pieces.10 = bf16[4,128,1152]{2,1,0:T(8,128)(2,1)} custom-call(s32[3,2]{1,0:T(4,128)S(1)} %pad_add_fusion.4.table, bf16[1024,1024]{1,0:T(8,128)(2,1)S(1)} %copy-done.1, bf16[1024,1024]{1,0:T(8,128)(2,1)S(1)} %copy-done.1, bf16[1024,4608]{1,0:T(8,128)(2,1)} %right.11), custom_call_target="tpu_custom_call" | custom-call | flops 1207959552 | bytes 6946816 | tf_op jit(solution)/shard_map/gradient_pieces/pallas_call | solution.py:46
  13.8 1.5 collective-permute-start.8
  15.4 5.0 %gradient_pieces.11 = bf16[4,128,1152]{2,1,0:T(8,128)(2,1)} custom-call(s32[3,2]{1,0:T(4,128)S(1)} %pad_add_fusion.5.table, bf16[1024,1024]{1,0:T(8,128)(2,1)S(1)} %copy-done.1, bf16[1024,1024]{1,0:T(8,128)(2,1)S(1)} %copy-done.1, bf16[1024,4608]{1,0:T(8,128)(2,1)} %right.11), custom_call_target="tpu_custom_call" | custom-call | flops 1207959552 | bytes 6946816 | tf_op jit(solution)/shard_map/gradient_pieces/pallas_call | solution.py:46
  20.4 1.7 collective-permute-start.10
  22.3 5.0 %gradient_pieces.8 = bf16[4,128,1152]{2,1,0:T(8,128)(2,1)} custom-call(s32[3,2]{1,0:T(4,128)S(1)} %pad_add_fusion.2.table, bf16[1024,1024]{1,0:T(8,128)(2,1)S(1)} %copy-done.1, bf16[1024,1024]{1,0:T(8,128)(2,1)S(1)} %copy-done.1, bf16[1024,4608]{1,0:T(8,128)(2,1)} %right.11), custom_call_target="tpu_custom_call" | custom-call | flops 1207959552 | bytes 6946816 | tf_op jit(solution)/shard_map/gradient_pieces/pallas_call | solution.py:46
  27.3 1.6 collective-permute-start.2
  29.3 6.9 %gradient_pieces.9 = bf16[8,128,1152]{2,1,0:T(8,128)(2,1)S(1)} custom-call(s32[3,4]{1,0:T(4,128)S(1)} %pad_add_fusion.3.table, bf16[1024,1024]{1,0:T(8,128)(2,1)S(1)} %copy-done.1, bf16[1024,1024]{1,0:T(8,128)(2,1)S(1)} %copy-done.1, bf16[1024,4608]{1,0:T(8,128)(2,1)} %right.11), custom_call_target="tpu_custom_call" | custom-call | flops 2415919104 | bytes 13893632 | tf_op jit(solution)/shard_map/gradient_pieces/pallas_call | solution.py:46
  36.2 1.4 copy-done.4
  37.6 7.1 %gradient_pieces.6 = bf16[8,128,1152]{2,1,0:T(8,128)(2,1)S(1)} custom-call(s32[3,4]{1,0:T(4,128)S(1)} %pad_add_fusion.table, bf16[1024,1024]{1,0:T(8,128)(2,1)S(1)} %copy-done.1, bf16[1024,1024]{1,0:T(8,128)(2,1)S(1)} %copy-done.1, bf16[1024,4608]{1,0:T(8,128)(2,1)} %right.11), custom_call_target="tpu_custom_call" | custom-call | flops 2415919104 | bytes 13893632 | tf_op jit(solution)/shard_map/gradient_pieces/pallas_call | solution.py:46
  44.7 1.4 copy-done.2
  46.1 0.7 fusion.7
  48.7 1.5 add_convert_fusion.3
  50.2 0.5 collective-permute-start.9
  50.8 1.4 add_convert_fusion.7
  52.2 0.4 collective-permute-start.1
  52.6 13.0 %collective-permute-done.9 = bf16[2,128,1152]{2,1,0:T(8,128)(2,1)S(1)} collective-permute-done((bf16[2,128,1152]{2,1,0:T(8,128)(2,1)S(1)}, bf16[2,128,1152]{2,1,0:T(8,128)(2,1)S(1)}, u32[]{:S(2)}, u32[]{:S(2)}) %collective-permute-start.9) | collective-permute-done | bytes 589856 | tf_op jit(solution)/shard_map/ppermute | solution.py:295
  65.6 1.8 add_convert_fusion.2
  67.4 2.0 %collective-permute-start.11 = (bf16[128,1152]{1,0:T(8,128)(2,1)S(1)}, bf16[128,1152]{1,0:T(8,128)(2,1)S(1)}, u32[]{:S(2)}, u32[]{:S(2)}) collective-permute-start(bf16[128,1152]{1,0:T(8,128)(2,1)S(1)} %slice_bitcast_fusion.2), channel_id=1, source_target_pairs={{0,64},{8,72},{16,80},{24,88},{32,96},{40,104},{48,112},{56,120},{... | collective-permute-start | bytes 884744 | tf_op jit(solution)/shard_map/ppermute | solution.py:295
  69.4 0.5 collective-permute-start.12
  69.9 1.6 add_convert_fusion.6
  71.5 0.9 collective-permute-start.3
  72.4 1.0 collective-permute-start.4
  73.5 11.8 %collective-permute-done.12 = bf16[2,128,1152]{2,1,0:T(8,128)(2,1)S(1)} collective-permute-done((bf16[2,128,1152]{2,1,0:T(8,128)(2,1)S(1)}, bf16[2,128,1152]{2,1,0:T(8,128)(2,1)S(1)}, u32[]{:S(2)}, u32[]{:S(2)}) %collective-permute-start.12) | collective-permute-done | bytes 589856 | tf_op jit(solution)/shard_map/ppermute | solution.py:295
  85.3 1.3 add_convert_fusion
  86.6 0.7 collective-permute-start.13
  87.4 2.6 %collective-permute-start.14 = (bf16[128,1152]{1,0:T(8,128)(2,1)S(1)}, bf16[128,1152]{1,0:T(8,128)(2,1)S(1)}, u32[]{:S(2)}, u32[]{:S(2)}) collective-permute-start(bf16[128,1152]{1,0:T(8,128)(2,1)S(1)} %get-tuple-element.44), channel_id=1, source_target_pairs={{0,96},{8,104},{16,112},{24,120},{32,0},{40,8},{48,16},{56,24},{64... | collective-permute-start | bytes 884744 | tf_op jit(solution)/shard_map/ppermute | solution.py:295
  89.9 0.3 collective-permute-done.4
  90.3 1.3 add_convert_fusion.4
  91.6 0.3 collective-permute-start.5
  91.9 3.3 %collective-permute-start.6 = (bf16[128,1152]{1,0:T(8,128)(2,1)S(1)}, bf16[128,1152]{1,0:T(8,128)(2,1)S(1)}, u32[]{:S(2)}, u32[]{:S(2)}) collective-permute-start(bf16[128,1152]{1,0:T(8,128)(2,1)S(1)} %get-tuple-element.46), channel_id=1, source_target_pairs={{0,24},{8,0},{16,8},{24,16},{32,56},{40,32},{48,40},{56,48},{64,88... | collective-permute-start | bytes 884744 | tf_op jit(solution)/shard_map/ppermute | solution.py:295
  95.2 0.2 fusion.2.grad_a
  95.4 1.3 collective-permute-start.15
  96.7 3.1 %collective-permute-done.5 = bf16[128,1152]{1,0:T(8,128)(2,1)S(1)} collective-permute-done((bf16[128,1152]{1,0:T(8,128)(2,1)S(1)}, bf16[128,1152]{1,0:T(8,128)(2,1)S(1)}, u32[]{:S(2)}, u32[]{:S(2)}) %collective-permute-start.5) | collective-permute-done | bytes 294944 | tf_op jit(solution)/shard_map/ppermute | solution.py:295
  99.8 1.5 collective-permute-done.6
  101.4 0.2 fusion.5.grad_b
  101.5 1.5 collective-permute-start.7
  103.1 0.2 convert_reduce_fusion
  103.3 0.1 select_reduce_fusion.1
  103.3 1.2 collective-permute-done.15.halo_a
  104.5 2.7 %collective-permute-done.7.halo_b = bf16[128,1152]{1,0:T(8,128)(2,1)S(1)} collective-permute-done((bf16[128,1152]{1,0:T(8,128)(2,1)S(1)}, bf16[128,1152]{1,0:T(8,128)(2,1)S(1)}, u32[]{:S(2)}, u32[]{:S(2)}) %collective-permute-start.7) | collective-permute-done | bytes 294944 | tf_op jit(solution)/shard_map/ppermute | solution.py:295
  107.2 10.1 %adam_slots.1 = (f32[1,36,128,128]{3,2,1,0:T(8,128)}, f32[1,36,128,128]{3,2,1,0:T(8,128)}, f32[1,36,128,128]{3,2,1,0:T(8,128)}, bf16[208,1152]{1,0:T(8,128)(2,1)...) custom-call(s32[3]{0:T(128)S(1)} %pad_add_fusion.6.info, ...), custom_call_target="tpu_custom_call" | custom-call | flops 11796480 | bytes 16515072 | tf_op jit(solution)/shard_map/adam_slots/pallas_call | solution.py:129
  117.2 2.5 %collective-permute-start.16 = (bf16[208,1152]{1,0:T(8,128)(2,1)S(1)}, bf16[208,1152]{1,0:T(8,128)(2,1)S(1)}, u32[]{:S(2)}, u32[]{:S(2)}) collective-permute-start(bf16[208,1152]{1,0:T(8,128)(2,1)S(1)} %get-tuple-element.26), channel_id=1, source_target_pairs={{0,8},{8,0},{16,24},{24,16},{32,40},{40,32},{48,56},{56,48},{64,72... | collective-permute-start | bytes 1437704 | tf_op jit(solution)/shard_map/ppermute | solution.py:295
  119.7 0.1 select_reduce_fusion
  119.8 0.7 collective-permute-start.17
  120.5 1.3 collective-permute-start.18
  121.9 10.3 %collective-permute-done.18.got2 = bf16[80,1152]{1,0:T(8,128)(2,1)S(1)} collective-permute-done((bf16[80,1152]{1,0:T(8,128)(2,1)S(1)}, bf16[80,1152]{1,0:T(8,128)(2,1)S(1)}, u32[]{:S(2)}, u32[]{:S(2)}) %collective-permute-start.18) | collective-permute-done | bytes 184352 | tf_op jit(solution)/shard_map/ppermute | solution.py:295
  132.2 2.4 %pack_by_owner.1 = bf16[8,592,128]{2,1,0:T(8,128)(2,1)} custom-call(s32[73]{0:T(128)S(1)} %pad_add_fusion.7.info, bf16[208,1152]{1,0:T(8,128)(2,1)S(1)} %get-tuple-element.25.keep3, bf16[208,1152]{1,0:T(8,128)(2,1)S(1)} %collective-permute-done.16.got3, bf16[80,1152]{1,0:T(8,128)(2,1)S(1)} %collective-permute-done.17.got1, ...), custom_call_target="tpu_custom_call" | custom-call | bytes 3637248 | tf_op jit(solution)/shard_map/pack_by_owner/pallas_call | solution.py:203
  134.6 5.3 %all-to-all-start = ((bf16[8,592,128]{2,1,0:T(8,128)(2,1)}), bf16[8,592,128]{2,1,0:T(8,128)(2,1)S(1)}, u32[]{:S(2)}, u32[]{:S(2)}) async-start(bf16[8,592,128]{2,1,0:T(8,128)(2,1)} %pack_by_owner.1), calls=%async_computation | async-start | bytes 2424832 | tf_op jit(solution)/shard_map/all_to_all | solution.py:383
  139.8 17.7 %all-to-all-done.got = bf16[8,592,128]{2,1,0:T(8,128)(2,1)S(1)} async-done(((bf16[8,592,128]{2,1,0:T(8,128)(2,1)}), bf16[8,592,128]{2,1,0:T(8,128)(2,1)S(1)}, u32[]{:S(2)}, u32[]{:S(2)}) %all-to-all-start) | async-done | bytes 1212448 | tf_op jit(solution)/shard_map/all_to_all | solution.py:383
  157.6 0.6 split_by_band.1
  158.2 0.7 collective-permute-start.19
  158.9 6.6 %collective-permute-start.20 = (bf16[592,128]{1,0:T(8,128)(2,1)S(1)}, bf16[592,128]{1,0:T(8,128)(2,1)S(1)}, u32[]{:S(2)}, u32[]{:S(2)}) collective-permute-start(bf16[592,128]{1,0:T(8,128)(2,1)S(1)} %get-tuple-element.30), channel_id=1, source_target_pairs={{0,16},{8,0},{16,48},{24,32},{32,80},{40,64},{48,112},{56,96},{64,... | collective-permute-start | bytes 454664 | tf_op jit(solution)/shard_map/ppermute | solution.py:295
  165.5 2.6 %collective-permute-start.21 = (bf16[592,128]{1,0:T(8,128)(2,1)S(1)}, bf16[592,128]{1,0:T(8,128)(2,1)S(1)}, u32[]{:S(2)}, u32[]{:S(2)}) collective-permute-start(bf16[592,128]{1,0:T(8,128)(2,1)S(1)} %get-tuple-element.31), channel_id=1, source_target_pairs={{0,32},{8,48},{16,0},{24,16},{32,96},{40,112},{48,64},{56,80},{64,... | collective-permute-start | bytes 454664 | tf_op jit(solution)/shard_map/ppermute | solution.py:295
  168.1 5.5 %collective-permute-start.22 = (bf16[592,128]{1,0:T(8,128)(2,1)S(1)}, bf16[592,128]{1,0:T(8,128)(2,1)S(1)}, u32[]{:S(2)}, u32[]{:S(2)}) collective-permute-start(bf16[592,128]{1,0:T(8,128)(2,1)S(1)} %get-tuple-element.32), channel_id=1, source_target_pairs={{0,48},{8,32},{16,16},{24,0},{32,112},{40,96},{48,80},{56,64},{64,... | collective-permute-start | bytes 454664 | tf_op jit(solution)/shard_map/ppermute | solution.py:295
  173.6 10.2 %collective-permute-start.24 = (bf16[592,128]{1,0:T(8,128)(2,1)S(1)}, bf16[592,128]{1,0:T(8,128)(2,1)S(1)}, u32[]{:S(2)}, u32[]{:S(2)}) collective-permute-start(bf16[592,128]{1,0:T(8,128)(2,1)S(1)} %get-tuple-element.34), channel_id=1, source_target_pairs={{0,80},{8,64},{16,112},{24,96},{32,16},{40,0},{48,48},{56,32},{64,... | collective-permute-start | bytes 454664 | tf_op jit(solution)/shard_map/ppermute | solution.py:295
  183.9 3.5 %collective-permute-start.25 = (bf16[592,128]{1,0:T(8,128)(2,1)S(1)}, bf16[592,128]{1,0:T(8,128)(2,1)S(1)}, u32[]{:S(2)}, u32[]{:S(2)}) collective-permute-start(bf16[592,128]{1,0:T(8,128)(2,1)S(1)} %get-tuple-element.35), channel_id=1, source_target_pairs={{0,96},{8,112},{16,64},{24,80},{32,32},{40,48},{48,0},{56,16},{64,... | collective-permute-start | bytes 454664 | tf_op jit(solution)/shard_map/ppermute | solution.py:295
  187.4 3.6 %collective-permute-start.26 = (bf16[592,128]{1,0:T(8,128)(2,1)S(1)}, bf16[592,128]{1,0:T(8,128)(2,1)S(1)}, u32[]{:S(2)}, u32[]{:S(2)}) collective-permute-start(bf16[592,128]{1,0:T(8,128)(2,1)S(1)} %get-tuple-element.36), channel_id=1, source_target_pairs={{0,112},{8,96},{16,80},{24,64},{32,48},{40,32},{48,16},{56,0},{64,... | collective-permute-start | bytes 454664 | tf_op jit(solution)/shard_map/ppermute | solution.py:295
  191.0 2.4 %collective-permute-done.23.refs_4_ = bf16[592,128]{1,0:T(8,128)(2,1)S(1)} collective-permute-done((bf16[592,128]{1,0:T(8,128)(2,1)S(1)}, bf16[592,128]{1,0:T(8,128)(2,1)S(1)}, u32[]{:S(2)}, u32[]{:S(2)}) %collective-permute-start.23) | collective-permute-done | bytes 151584 | tf_op jit(solution)/shard_map/ppermute | solution.py:295
  193.4 2.6 %collective-permute-done.26.refs_7_ = bf16[592,128]{1,0:T(8,128)(2,1)S(1)} collective-permute-done((bf16[592,128]{1,0:T(8,128)(2,1)S(1)}, bf16[592,128]{1,0:T(8,128)(2,1)S(1)}, u32[]{:S(2)}, u32[]{:S(2)}) %collective-permute-start.26) | collective-permute-done | bytes 151584 | tf_op jit(solution)/shard_map/ppermute | solution.py:295
  196.1 1.6 place_served.1
  197.7 0.7 slice_reduce_fusion
  (64 shorter events, 1.5 us)
Async XLA Ops:
  1.2 1.6 copy-start
  2.8 6.0 %copy-start.1 = (bf16[1024,1024]{1,0:T(8,128)(2,1)S(1)}, bf16[1024,1024]{1,0:T(8,128)(2,1)}, u32[]{:S(2)}) copy-start(bf16[1024,1024]{1,0:T(8,128)(2,1)} %left_b.11) | copy-start | bytes 6291460
  7.0 43.8 %collective-permute-start = (bf16[4,128,1152]{2,1,0:T(8,128)(2,1)S(1)}, bf16[4,128,1152]{2,1,0:T(8,128)(2,1)}, u32[]{:S(2)}, u32[]{:S(2)}) collective-permute-start(bf16[4,128,1152]{2,1,0:T(8,128)(2,1)S(1)} %gradient_pieces.7), channel_id=1, source_target_pairs={{0,32},{8,40},{16,48},{24,56},{32,64},{40,72},{48,80},{56,88},{64,... | collective-permute-start | bytes 3538952 | tf_op jit(solution)/shard_map/ppermute | solution.py:295
  13.8 34.9 %collective-permute-start.8 = (bf16[4,128,1152]{2,1,0:T(8,128)(2,1)}, bf16[4,128,1152]{2,1,0:T(8,128)(2,1)}, u32[]{:S(2)}, u32[]{:S(2)}) collective-permute-start(bf16[4,128,1152]{2,1,0:T(8,128)(2,1)} %gradient_pieces.10), channel_id=1, source_target_pairs={{0,8},{8,16},{16,24},{24,0},{32,40},{40,48},{48,56},{56,32},{64,72... | collective-permute-start | bytes 3538952 | tf_op jit(solution)/shard_map/ppermute | solution.py:295
  20.4 32.2 %collective-permute-start.10 = (bf16[4,128,1152]{2,1,0:T(8,128)(2,1)}, bf16[4,128,1152]{2,1,0:T(8,128)(2,1)}, u32[]{:S(2)}, u32[]{:S(2)}) collective-permute-start(bf16[4,128,1152]{2,1,0:T(8,128)(2,1)} %gradient_pieces.11), channel_id=1, source_target_pairs={{0,24},{8,0},{16,8},{24,16},{32,56},{40,32},{48,40},{56,48},{64,88... | collective-permute-start | bytes 3538952 | tf_op jit(solution)/shard_map/ppermute | solution.py:295
  22.3 6.7 %copy-start.8 = (s32[16]{0:T(128)S(1)}, s32[16]{0:T(128)}, u32[]{:S(2)}) copy-start(s32[16]{0:T(128)} %param.13) | copy-start | bytes 196
  27.3 42.6 %collective-permute-start.2 = (bf16[4,128,1152]{2,1,0:T(8,128)(2,1)}, bf16[4,128,1152]{2,1,0:T(8,128)(2,1)}, u32[]{:S(2)}, u32[]{:S(2)}) collective-permute-start(bf16[4,128,1152]{2,1,0:T(8,128)(2,1)} %gradient_pieces.8), channel_id=1, source_target_pairs={{0,96},{8,104},{16,112},{24,120},{32,0},{40,8},{48,16},{56,24},{64... | collective-permute-start | bytes 3538952 | tf_op jit(solution)/shard_map/ppermute | solution.py:295
  36.2 1.4 copy-start.4
  44.7 1.4 copy-start.2
  48.7 16.9 %copy-start.5 = (bf16[8,128,1152]{2,1,0:T(8,128)(2,1)S(1)}, bf16[8,128,1152]{2,1,0:T(8,128)(2,1)}, u32[]{:S(2)}) copy-start(bf16[8,128,1152]{2,1,0:T(8,128)(2,1)} %copy-done.4) | copy-start | bytes 7077892
  50.2 15.4 %collective-permute-start.9 = (bf16[2,128,1152]{2,1,0:T(8,128)(2,1)S(1)}, bf16[2,128,1152]{2,1,0:T(8,128)(2,1)S(1)}, u32[]{:S(2)}, u32[]{:S(2)}) collective-permute-start(bf16[2,128,1152]{2,1,0:T(8,128)(2,1)S(1)} %add_convert_fusion.3), channel_id=1, source_target_pairs={{0,8},{8,16},{16,24},{24,0},{32,40},{40,48},{48,56},{56,32},{64,72... | collective-permute-start | bytes 1769480 | tf_op jit(solution)/shard_map/ppermute | solution.py:295
  52.2 17.7 %collective-permute-start.1 = (bf16[2,128,1152]{2,1,0:T(8,128)(2,1)S(1)}, bf16[2,128,1152]{2,1,0:T(8,128)(2,1)S(1)}, u32[]{:S(2)}, u32[]{:S(2)}) collective-permute-start(bf16[2,128,1152]{2,1,0:T(8,128)(2,1)S(1)} %add_convert_fusion.7), channel_id=1, source_target_pairs={{0,32},{8,40},{16,48},{24,56},{32,64},{40,72},{48,80},{56,88},{64,... | collective-permute-start | bytes 1769480 | tf_op jit(solution)/shard_map/ppermute | solution.py:295
  65.6 4.3 %copy-start.3 = (bf16[8,128,1152]{2,1,0:T(8,128)(2,1)S(1)}, bf16[8,128,1152]{2,1,0:T(8,128)(2,1)}, u32[]{:S(2)}) copy-start(bf16[8,128,1152]{2,1,0:T(8,128)(2,1)} %copy-done.2) | copy-start | bytes 7077892
  67.4 24.5 %collective-permute-start.11 = (bf16[128,1152]{1,0:T(8,128)(2,1)S(1)}, bf16[128,1152]{1,0:T(8,128)(2,1)S(1)}, u32[]{:S(2)}, u32[]{:S(2)}) collective-permute-start(bf16[128,1152]{1,0:T(8,128)(2,1)S(1)} %slice_bitcast_fusion.2), channel_id=1, source_target_pairs={{0,64},{8,72},{16,80},{24,88},{32,96},{40,104},{48,112},{56,120},{... | collective-permute-start | bytes 884744 | tf_op jit(solution)/shard_map/ppermute | solution.py:295
  69.4 15.9 %collective-permute-start.12 = (bf16[2,128,1152]{2,1,0:T(8,128)(2,1)S(1)}, bf16[2,128,1152]{2,1,0:T(8,128)(2,1)S(1)}, u32[]{:S(2)}, u32[]{:S(2)}) collective-permute-start(bf16[2,128,1152]{2,1,0:T(8,128)(2,1)S(1)} %get-tuple-element.40), channel_id=1, source_target_pairs={{0,24},{8,0},{16,8},{24,16},{32,56},{40,32},{48,40},{56,48},{64,88... | collective-permute-start | bytes 1769480 | tf_op jit(solution)/shard_map/ppermute | solution.py:295
  71.5 25.1 %collective-permute-start.3 = (bf16[128,1152]{1,0:T(8,128)(2,1)S(1)}, bf16[128,1152]{1,0:T(8,128)(2,1)S(1)}, u32[]{:S(2)}, u32[]{:S(2)}) collective-permute-start(bf16[128,1152]{1,0:T(8,128)(2,1)S(1)} %slice_bitcast_fusion.6), channel_id=1, source_target_pairs={{0,16},{8,24},{16,0},{24,8},{32,48},{40,56},{48,32},{56,40},{64,80... | collective-permute-start | bytes 884744 | tf_op jit(solution)/shard_map/ppermute | solution.py:295
  72.4 17.9 %collective-permute-start.4 = (bf16[2,128,1152]{2,1,0:T(8,128)(2,1)S(1)}, bf16[2,128,1152]{2,1,0:T(8,128)(2,1)S(1)}, u32[]{:S(2)}, u32[]{:S(2)}) collective-permute-start(bf16[2,128,1152]{2,1,0:T(8,128)(2,1)S(1)} %get-tuple-element.42), channel_id=1, source_target_pairs={{0,96},{8,104},{16,112},{24,120},{32,0},{40,8},{48,16},{56,24},{64... | collective-permute-start | bytes 1769480 | tf_op jit(solution)/shard_map/ppermute | solution.py:295
  86.6 8.6 %collective-permute-start.13 = (bf16[128,1152]{1,0:T(8,128)(2,1)S(1)}, bf16[128,1152]{1,0:T(8,128)(2,1)S(1)}, u32[]{:S(2)}, u32[]{:S(2)}) collective-permute-start(bf16[128,1152]{1,0:T(8,128)(2,1)S(1)} %get-tuple-element.43), channel_id=1, source_target_pairs={{0,32},{8,40},{16,48},{24,56},{32,64},{40,72},{48,80},{56,88},{64,... | collective-permute-start | bytes 884744 | tf_op jit(solution)/shard_map/ppermute | solution.py:295
  87.4 7.8 %collective-permute-start.14 = (bf16[128,1152]{1,0:T(8,128)(2,1)S(1)}, bf16[128,1152]{1,0:T(8,128)(2,1)S(1)}, u32[]{:S(2)}, u32[]{:S(2)}) collective-permute-start(bf16[128,1152]{1,0:T(8,128)(2,1)S(1)} %get-tuple-element.44), channel_id=1, source_target_pairs={{0,96},{8,104},{16,112},{24,120},{32,0},{40,8},{48,16},{56,24},{64... | collective-permute-start | bytes 884744 | tf_op jit(solution)/shard_map/ppermute | solution.py:295
  91.6 8.2 %collective-permute-start.5 = (bf16[128,1152]{1,0:T(8,128)(2,1)S(1)}, bf16[128,1152]{1,0:T(8,128)(2,1)S(1)}, u32[]{:S(2)}, u32[]{:S(2)}) collective-permute-start(bf16[128,1152]{1,0:T(8,128)(2,1)S(1)} %get-tuple-element.45), channel_id=1, source_target_pairs={{0,8},{8,16},{16,24},{24,0},{32,40},{40,48},{48,56},{56,32},{64,72... | collective-permute-start | bytes 884744 | tf_op jit(solution)/shard_map/ppermute | solution.py:295
  91.9 11.2 %copy-start.7 = (s32[36]{0:T(128)S(1)}, s32[36]{0:T(128)}, u32[]{:S(2)}) copy-start(s32[36]{0:T(128)} %param.14) | copy-start | bytes 436
  91.9 11.3 %copy-start.9 = (s32[32]{0:T(128)S(1)}, s32[32]{0:T(128)}, u32[]{:S(2)}) copy-start(s32[32]{0:T(128)} %param.15) | copy-start | bytes 388
  91.9 15.3 %copy-start.6 = (f32[1,36,128,128]{3,2,1,0:T(8,128)S(1)}, f32[1,36,128,128]{3,2,1,0:T(8,128)}, u32[]{:S(2)}) copy-start(f32[1,36,128,128]{3,2,1,0:T(8,128)} %master.1) | copy-start | bytes 7077892
  91.9 9.4 %collective-permute-start.6 = (bf16[128,1152]{1,0:T(8,128)(2,1)S(1)}, bf16[128,1152]{1,0:T(8,128)(2,1)S(1)}, u32[]{:S(2)}, u32[]{:S(2)}) collective-permute-start(bf16[128,1152]{1,0:T(8,128)(2,1)S(1)} %get-tuple-element.46), channel_id=1, source_target_pairs={{0,24},{8,0},{16,8},{24,16},{32,56},{40,32},{48,40},{56,48},{64,88... | collective-permute-start | bytes 884744 | tf_op jit(solution)/shard_map/ppermute | solution.py:295
  95.4 9.2 %collective-permute-start.15 = (bf16[128,1152]{1,0:T(8,128)(2,1)S(1)}, bf16[128,1152]{1,0:T(8,128)(2,1)S(1)}, u32[]{:S(2)}, u32[]{:S(2)}) collective-permute-start(bf16[128,1152]{1,0:T(8,128)(2,1)S(1)} %fusion.2.grad_a), channel_id=1, source_target_pairs={{8,0},{16,8},{24,16},{32,24},{40,32},{48,40},{56,48},{64,56},{72,6... | collective-permute-start | bytes 884744 | tf_op jit(solution)/shard_map/ppermute | solution.py:295
  101.5 5.7 %collective-permute-start.7 = (bf16[128,1152]{1,0:T(8,128)(2,1)S(1)}, bf16[128,1152]{1,0:T(8,128)(2,1)S(1)}, u32[]{:S(2)}, u32[]{:S(2)}) collective-permute-start(bf16[128,1152]{1,0:T(8,128)(2,1)S(1)} %fusion.5.grad_b), channel_id=1, source_target_pairs={{0,8},{8,16},{16,24},{24,32},{32,40},{40,48},{48,56},{56,64},{64,7... | collective-permute-start | bytes 884744 | tf_op jit(solution)/shard_map/ppermute | solution.py:295
  117.2 14.9 %collective-permute-start.16 = (bf16[208,1152]{1,0:T(8,128)(2,1)S(1)}, bf16[208,1152]{1,0:T(8,128)(2,1)S(1)}, u32[]{:S(2)}, u32[]{:S(2)}) collective-permute-start(bf16[208,1152]{1,0:T(8,128)(2,1)S(1)} %get-tuple-element.26), channel_id=1, source_target_pairs={{0,8},{8,0},{16,24},{24,16},{32,40},{40,32},{48,56},{56,48},{64,72... | collective-permute-start | bytes 1437704 | tf_op jit(solution)/shard_map/ppermute | solution.py:295
  119.8 2.1 %collective-permute-start.17 = (bf16[80,1152]{1,0:T(8,128)(2,1)S(1)}, bf16[80,1152]{1,0:T(8,128)(2,1)S(1)}, u32[]{:S(2)}, u32[]{:S(2)}) collective-permute-start(bf16[80,1152]{1,0:T(8,128)(2,1)S(1)} %get-tuple-element.27), channel_id=1, source_target_pairs={{8,16},{16,8},{24,32},{32,24},{40,48},{48,40},{56,64},{64,56},{72,... | collective-permute-start | bytes 552968 | tf_op jit(solution)/shard_map/ppermute | solution.py:295
  120.5 11.7 %collective-permute-start.18 = (bf16[80,1152]{1,0:T(8,128)(2,1)S(1)}, bf16[80,1152]{1,0:T(8,128)(2,1)S(1)}, u32[]{:S(2)}, u32[]{:S(2)}) collective-permute-start(bf16[80,1152]{1,0:T(8,128)(2,1)S(1)} %get-tuple-element.28), channel_id=1, source_target_pairs={{8,24},{16,0},{24,40},{32,16},{40,56},{48,32},{56,72},{64,48},{72,... | collective-permute-start | bytes 552968 | tf_op jit(solution)/shard_map/ppermute | solution.py:295
  134.6 23.0 %all-to-all-start = ((bf16[8,592,128]{2,1,0:T(8,128)(2,1)}), bf16[8,592,128]{2,1,0:T(8,128)(2,1)S(1)}, u32[]{:S(2)}, u32[]{:S(2)}) async-start(bf16[8,592,128]{2,1,0:T(8,128)(2,1)} %pack_by_owner.1), calls=%async_computation | async-start | bytes 2424832 | tf_op jit(solution)/shard_map/all_to_all | solution.py:383
  158.2 15.4 %collective-permute-start.19 = (bf16[592,128]{1,0:T(8,128)(2,1)S(1)}, bf16[592,128]{1,0:T(8,128)(2,1)S(1)}, u32[]{:S(2)}, u32[]{:S(2)}) collective-permute-start(bf16[592,128]{1,0:T(8,128)(2,1)S(1)} %get-tuple-element.29), channel_id=1, source_target_pairs={{0,0},{8,16},{16,32},{24,48},{32,64},{40,80},{48,96},{56,112},{64,... | collective-permute-start | bytes 454664 | tf_op jit(solution)/shard_map/ppermute | solution.py:295
  158.9 25.0 %collective-permute-start.20 = (bf16[592,128]{1,0:T(8,128)(2,1)S(1)}, bf16[592,128]{1,0:T(8,128)(2,1)S(1)}, u32[]{:S(2)}, u32[]{:S(2)}) collective-permute-start(bf16[592,128]{1,0:T(8,128)(2,1)S(1)} %get-tuple-element.30), channel_id=1, source_target_pairs={{0,16},{8,0},{16,48},{24,32},{32,80},{40,64},{48,112},{56,96},{64,... | collective-permute-start | bytes 454664 | tf_op jit(solution)/shard_map/ppermute | solution.py:295
  165.5 21.9 %collective-permute-start.21 = (bf16[592,128]{1,0:T(8,128)(2,1)S(1)}, bf16[592,128]{1,0:T(8,128)(2,1)S(1)}, u32[]{:S(2)}, u32[]{:S(2)}) collective-permute-start(bf16[592,128]{1,0:T(8,128)(2,1)S(1)} %get-tuple-element.31), channel_id=1, source_target_pairs={{0,32},{8,48},{16,0},{24,16},{32,96},{40,112},{48,64},{56,80},{64,... | collective-permute-start | bytes 454664 | tf_op jit(solution)/shard_map/ppermute | solution.py:295
  168.1 22.9 %collective-permute-start.22 = (bf16[592,128]{1,0:T(8,128)(2,1)S(1)}, bf16[592,128]{1,0:T(8,128)(2,1)S(1)}, u32[]{:S(2)}, u32[]{:S(2)}) collective-permute-start(bf16[592,128]{1,0:T(8,128)(2,1)S(1)} %get-tuple-element.32), channel_id=1, source_target_pairs={{0,48},{8,32},{16,16},{24,0},{32,112},{40,96},{48,80},{56,64},{64,... | collective-permute-start | bytes 454664 | tf_op jit(solution)/shard_map/ppermute | solution.py:295
  173.5 19.8 %collective-permute-start.23 = (bf16[592,128]{1,0:T(8,128)(2,1)S(1)}, bf16[592,128]{1,0:T(8,128)(2,1)S(1)}, u32[]{:S(2)}, u32[]{:S(2)}) collective-permute-start(bf16[592,128]{1,0:T(8,128)(2,1)S(1)} %get-tuple-element.33), channel_id=1, source_target_pairs={{0,64},{8,80},{16,96},{24,112},{32,0},{40,16},{48,32},{56,48},{64,... | collective-permute-start | bytes 454664 | tf_op jit(solution)/shard_map/ppermute | solution.py:295
  173.6 19.7 %collective-permute-start.24 = (bf16[592,128]{1,0:T(8,128)(2,1)S(1)}, bf16[592,128]{1,0:T(8,128)(2,1)S(1)}, u32[]{:S(2)}, u32[]{:S(2)}) collective-permute-start(bf16[592,128]{1,0:T(8,128)(2,1)S(1)} %get-tuple-element.34), channel_id=1, source_target_pairs={{0,80},{8,64},{16,112},{24,96},{32,16},{40,0},{48,48},{56,32},{64,... | collective-permute-start | bytes 454664 | tf_op jit(solution)/shard_map/ppermute | solution.py:295
  183.9 9.6 %collective-permute-start.25 = (bf16[592,128]{1,0:T(8,128)(2,1)S(1)}, bf16[592,128]{1,0:T(8,128)(2,1)S(1)}, u32[]{:S(2)}, u32[]{:S(2)}) collective-permute-start(bf16[592,128]{1,0:T(8,128)(2,1)S(1)} %get-tuple-element.35), channel_id=1, source_target_pairs={{0,96},{8,112},{16,64},{24,80},{32,32},{40,48},{48,0},{56,16},{64,... | collective-permute-start | bytes 454664 | tf_op jit(solution)/shard_map/ppermute | solution.py:295
  187.4 8.7 %collective-permute-start.26 = (bf16[592,128]{1,0:T(8,128)(2,1)S(1)}, bf16[592,128]{1,0:T(8,128)(2,1)S(1)}, u32[]{:S(2)}, u32[]{:S(2)}) collective-permute-start(bf16[592,128]{1,0:T(8,128)(2,1)S(1)} %get-tuple-element.36), channel_id=1, source_target_pairs={{0,112},{8,96},{16,80},{24,64},{32,48},{40,32},{48,16},{56,0},{64,... | collective-permute-start | bytes 454664 | tf_op jit(solution)/shard_map/ppermute | solution.py:295

commit v2 on v1

v2 whole, which is shorter than its diff:
```python
import jax
import jax.numpy as jnp
from jax import lax
from jax.experimental import pallas as pl
from jax.experimental.pallas import tpu as pltpu
from jax.sharding import Mesh
from jax.sharding import PartitionSpec as P

QPER = 16
GROUPS = 2
BLK = 128
HALF = 64
UNIT = 9
WIDE = UNIT * BLK
FIRST = 10 * BLK
LAST = 8 * BLK
TILE = 256
CAP = 36
COLS = 36
SCAP = 9
PIECE = 32
MSG = SCAP * PIECE + 16

first_bias = 1.0 - 0.9**10
second_bias = 1.0 - 0.95**10

BF = jnp.bfloat16
F32 = jnp.float32


def cost(flops, nbytes):
    return pl.CostEstimate(flops=flops, bytes_accessed=nbytes, transcendentals=0)


def params(mib=20):
    return pltpu.CompilerParams(vmem_limit_bytes=mib * 1024 * 1024)


def mm_products(refs):
    left = jnp.concatenate([ref[...] for ref in refs[:4]], axis=1)
    for n, right in enumerate(refs[4:]):
        prod = lax.dot_general(
            left, right[...], (((0,), (0,)), ((), ())), preferred_element_type=F32
        ).astype(BF)
        for u in range(4):
            yield u, slice(n * TILE, (n + 1) * TILE), prod[u * BLK : (u + 1) * BLK]


def mm_send_body(table, *refs):
    fwd, bwd = refs[-2:]
    for u, lanes, prod in mm_products(refs[:-2]):
        (fwd if u < 2 else bwd)[u % 2, :, lanes] = prod


def mm_rest_body(table, *refs):
    for u, lanes, prod in mm_products(refs[:-1]):
        refs[-1][u, :, lanes] = prod


def mm(table, inputs, cotangent, part, flip=None):
    tok = inputs.shape[0]
    left = lambda n: pl.BlockSpec((tok, BLK), lambda g, t: (0, t[n, g]))
    right = lambda n: pl.BlockSpec((tok, TILE), lambda g, t: (0, t[4, g] + n))
    tiles = part // TILE
    if flip is None:
        out_specs = pl.BlockSpec((4, BLK, part), lambda g, t: (g, 0, 0))
        out_shape = jax.ShapeDtypeStruct((8, BLK, part), BF)
    else:
        out_specs = [
            pl.BlockSpec((2, BLK, part), lambda g, t: (g, 0, 0)),
            pl.BlockSpec((2, BLK, part), lambda g, t: ((1 - g) if flip else g, 0, 0)),
        ]
        out_shape = [jax.ShapeDtypeStruct((4, BLK, part), BF)] * 2
    return pl.pallas_call(
        mm_rest_body if flip is None else mm_send_body,
        grid_spec=pltpu.PrefetchScalarGridSpec(
            num_scalar_prefetch=1,
            grid=(2,),
            in_specs=[left(n) for n in range(4)] + [right(n) for n in range(tiles)],
            out_specs=out_specs,
        ),
        out_shape=out_shape,
        compiler_params=params(60),
        cost_estimate=cost(2 * 2 * 512 * part * tok, 2 * (tok * (part + 512) + 512 * part) * 2),
        name="gradient_pieces" if flip is None else "gradient_to_send",
    )(table, *([inputs] * 4), *([cotangent] * tiles))


def total(*parts):
    out = parts[0].astype(F32)
    for part in parts[1:]:
        out = out + part.astype(F32)
    return out.astype(BF)


def pair_spec(part, group):
    return pl.BlockSpec((2, BLK, part), lambda s: (group, 0, 0))


def relay_body(to_fwd, to_bwd, fwd, bwd, earlier, out_fwd, out_bwd):
    out_fwd[...] = total(to_fwd[...], fwd[...])
    out_bwd[...] = total(to_bwd[...], bwd[...])


def relay(rest, groups, fwd, bwd, earlier):
    part = rest.shape[2]
    return pl.pallas_call(
        relay_body,
        grid=(1,),
        in_specs=[pair_spec(part, g) for g in (groups[0], groups[1], 0, 0)]
        + [pl.BlockSpec(memory_space=pl.ANY)],
        out_specs=[pair_spec(part, 0)] * 2,
        out_shape=[jax.ShapeDtypeStruct((2, BLK, part), BF)] * 2,
        compiler_params=params(),
        cost_estimate=cost(4 * BLK * part, 12 * BLK * part * 2),
        name="relay_sums",
    )(rest, rest, fwd, bwd, earlier)


def long_sum_body(own_even, own_odd, fwd2, bwd2, fwd, bwd, e0, e1, e2, e3):
    for n, (near, far) in enumerate(((e0, e2), (e1, e3))):
        own, second, first = ((own_even, fwd2, bwd), (own_odd, bwd2, fwd))[n]
        near[...] = total(own[0], second[0], first[0])
        far[...] = total(own[1], second[1], first[1])


def long_sum(rest, groups, fwd2, bwd2, fwd, bwd):
    part = rest.shape[2]
    return pl.pallas_call(
        long_sum_body,
        grid=(1,),
        in_specs=[pair_spec(part, g) for g in (groups[0], groups[1], 0, 0, 1, 1)],
        out_specs=[pl.BlockSpec((BLK, part), lambda s: (0, 0))] * 4,
        out_shape=[jax.ShapeDtypeStruct((BLK, part), BF)] * 4,
        compiler_params=params(),
        cost_estimate=cost(8 * BLK * part, 16 * BLK * part * 2),
        name="long_sums",
    )(rest, rest, fwd2, bwd2, fwd, bwd)


def front_body(own, near, far, other, out, tenth):
    part = total(own[...], near[...], far[...], other[...])
    out[...] = part[:, :WIDE]
    tenth[...] = part[:, WIDE:]


def back_body(own, near, far, other, tenth, out):
    out[:, :BLK] = tenth[...]
    out[:, BLK:] = total(own[...], near[...], far[...], other[...])


def slice_half(body, out_widths, *parts):
    return pl.pallas_call(
        body,
        out_shape=[jax.ShapeDtypeStruct((BLK, w), BF) for w in out_widths],
        compiler_params=params(),
        cost_estimate=cost(4 * BLK * WIDE, 7 * BLK * WIDE * 2),
        name="slice_half",
    )(*parts)


def adam_step(old, moment, variance, grad):
    mom = 0.9 * moment + 0.1 * grad
    var = 0.95 * variance + 0.05 * (grad * grad)
    new = old - 0.02 * (
        (mom * (1.0 / first_bias)) / (jnp.sqrt(var * (1.0 / second_bias)) + 1e-08) + 0.1 * old
    )
    return new, mom, var


def unit_of(place):
    unit = lax.div(place, UNIT)
    return unit, pl.ds(pl.multiple_of((place - unit * UNIT) * BLK, BLK), BLK)


def wrap(slot):
    slot = jnp.where(slot < 0, slot + CAP, slot)
    return jnp.where(slot >= CAP, slot - CAP, slot)


def code_body(units, info, first, second, master, moment, variance, mine, other, scales):
    off, length, odd = info[0], info[1], info[2]
    for n, (unit, grads) in enumerate(zip(units, (first, second))):
        for b in range(UNIT):
            slot = wrap(unit * UNIT + b - off)
            live = slot < length
            lanes = slice(b * BLK, (b + 1) * BLK)
            grad = grads[:, lanes].astype(F32)
            new, _, _ = adam_step(master[0, slot], moment[0, slot], variance[0, slot], grad)
            peak = jnp.max(jnp.abs(new), axis=(0, 1), keepdims=True)
            scale = (peak + 1e-06).astype(BF).astype(F32)
            code = jnp.where(live, new * (1.0 / scale), 0.0).astype(BF)
            top, low = code[:HALF], code[HALF:]
            mine[n, :, lanes] = jnp.where(odd == 1, low, top)
            other[n, :, lanes] = jnp.where(odd == 1, top, low)
            scales[n, :, lanes] = jnp.broadcast_to(jnp.where(live, scale, 0.0), (8, BLK))


def scale_rows(scales, rows):
    return jnp.concatenate(
        [scales[n, 0:1] for n in rows] + [jnp.zeros((16 - len(rows), WIDE), F32)], axis=0
    ).astype(BF)


def own_body(info, a, b, master, moment, variance, keep, send, mine, other, scales):
    code_body((1, 2), info, a, b, master, moment, variance, mine, other, scales)
    tail = scale_rows(scales, (0, 1))
    for ref, held in ((keep, mine), (send, other)):
        ref[:HALF] = held[0]
        ref[HALF : 2 * HALF] = held[1]
        ref[2 * HALF :] = tail


def halo_body(
    info, before, after, master, moment, variance, keep, send, near, far, mine, other, scales
):
    code_body((0, 3), info, before, after, master, moment, variance, mine, other, scales)
    tails = [scale_rows(scales, (n,)) for n in range(2)]

    def write(inside):
        cross = 1 - inside
        keep[:HALF] = mine[inside]
        keep[HALF:] = tails[inside]
        send[:HALF] = other[inside]
        send[HALF:] = tails[inside]
        near[:HALF] = other[cross]
        near[HALF:] = tails[cross]
        far[:HALF] = mine[cross]
        far[HALF:] = tails[cross]

    pl.when(info[2] == 0)(lambda: write(1))
    pl.when(info[2] == 1)(lambda: write(0))


def codes(body, n_out, rows, name, info, a, b, master, moment, variance):
    whole = lambda v: pl.BlockSpec(v.shape, lambda s, t: (0,) * v.ndim)
    return pl.pallas_call(
        body,
        grid_spec=pltpu.PrefetchScalarGridSpec(
            num_scalar_prefetch=1,
            grid=(1,),
            in_specs=[whole(v) for v in (a, b, master, moment, variance)],
            out_specs=[pl.BlockSpec((rows, WIDE), lambda s, t: (0, 0))] * n_out,
            scratch_shapes=[
                pltpu.VMEM((2, HALF, WIDE), BF),
                pltpu.VMEM((2, HALF, WIDE), BF),
                pltpu.VMEM((2, 8, WIDE), F32),
            ],
        ),
        out_shape=[jax.ShapeDtypeStruct((rows, WIDE), BF)] * n_out,
        compiler_params=params(),
        cost_estimate=cost(18 * 16384 * 30, 36 * 16384 * 12),
        name=name,
    )(info, a, b, master, moment, variance)


def state_body(
    info, halo_b, grad_a, grad_b, halo_a, master, moment, variance,
    new_master, new_moment, new_variance, window,
):
    step = pl.program_id(0)
    off, length = info[0], info[1]

    @pl.when(step == 0)
    def _():
        for q, ref in enumerate((halo_b, grad_a, grad_b, halo_a)):
            window[q] = ref[...]

    for n in range(4):
        slot = step * 4 + n
        unit, lanes = unit_of(wrap(off + slot))
        grad = jnp.where(slot < length, window[unit, :, lanes].astype(F32), 0.0)
        new_master[0, n], new_moment[0, n], new_variance[0, n] = adam_step(
            master[0, n], moment[0, n], variance[0, n], grad
        )


def update_state(info, halo_b, grad_a, grad_b, halo_a, master, moment, variance):
    state = pl.BlockSpec((1, 4, BLK, BLK), lambda s, t: (0, s, 0, 0))
    return pl.pallas_call(
        state_body,
        grid_spec=pltpu.PrefetchScalarGridSpec(
            num_scalar_prefetch=1,
            grid=(CAP // 4,),
            in_specs=[pl.BlockSpec((BLK, WIDE), lambda s, t: (0, 0))] * 4 + [state] * 3,
            out_specs=[state] * 3,
            scratch_shapes=[pltpu.VMEM((4, BLK, WIDE), BF)],
        ),
        out_shape=[jax.ShapeDtypeStruct(master.shape, F32)] * 3,
        compiler_params=params(),
        cost_estimate=cost(36 * 16384 * 20, 36 * 16384 * 26),
        name="update_state",
    )(info, halo_b, grad_a, grad_b, halo_a, master, moment, variance)


def pack_body(info, keep2, got2, keep1, got1, near, far, out, row, tails):
    def half(ref, n):
        return ref[n * HALF : (n + 1) * HALF]

    def tail(ref, n):
        at = ref.shape[0] - 16
        return ref[at:].astype(F32)[n : n + 1]

    own, pair = [(keep2, 0), (keep2, 1)], [(got2, 0), (got2, 1)]
    inner_own, inner_pair, by, on = (keep1, 0), (got1, 0), (near, 0), (far, 0)

    def fill(units):
        for q, parts in enumerate(units):
            (a, m), (b, n) = parts
            row[q] = half(a, m) + half(b, n)
            tails[q, 0:1] = tail(a, m) + tail(b, n)

    @pl.when(info[0] == 0)
    def _():
        fill(((own[0], by), (own[1], inner_pair), (pair[0], inner_own), (pair[1], on)))

    @pl.when(info[0] == 1)
    def _():
        fill(((pair[0], on), (pair[1], inner_own), (own[0], inner_pair), (own[1], by)))

    def owner(o, carry):
        rows = []
        for t in range(SCAP):
            col = info[1 + o * SCAP + t]
            unit, lanes = unit_of(jnp.maximum(col, 0))
            piece = row[unit, :, lanes]
            piece = jnp.where(col >= 0, piece, jnp.zeros_like(piece))
            for part in range(2):
                out[2 * o + part, t * PIECE : (t + 1) * PIECE] = piece[
                    part * PIECE : (part + 1) * PIECE
                ]
            rows.append(jnp.where(col >= 0, tails[unit, :, lanes][0:1], 0.0))
        rows.append(jnp.zeros((16 - SCAP, BLK), F32))
        last = jnp.concatenate(rows, axis=0).astype(BF)
        for part in range(2):
            out[2 * o + part, SCAP * PIECE :] = last
        return carry

    lax.fori_loop(0, 8, owner, 0)


def pack(info, *parts):
    return pl.pallas_call(
        pack_body,
        grid_spec=pltpu.PrefetchScalarGridSpec(
            num_scalar_prefetch=1,
            grid=(1,),
            in_specs=[pl.BlockSpec(a.shape, lambda s, t: (0, 0)) for a in parts],
            out_specs=pl.BlockSpec((16, MSG, BLK), lambda s, t: (0, 0, 0)),
            scratch_shapes=[pltpu.VMEM((4, HALF, WIDE), BF), pltpu.VMEM((4, 8, WIDE), F32)],
        ),
        out_shape=jax.ShapeDtypeStruct((16, MSG, BLK), BF),
        compiler_params=params(),
        cost_estimate=cost(0, 3 * 16 * MSG * BLK * 2),
        name="pack_by_owner",
    )(info, *parts)


def place_body(got, out, tails):
    for src in range(16):
        upper, low, x = src // 8, src // 4 % 2, src % 4
        at = (2 * low + x // 2) * BLK + (x % 2) * HALF + upper * PIECE
        for t in range(SCAP):
            out[0, t, at : at + PIECE] = got[src, t * PIECE : (t + 1) * PIECE]
    for q in range(4):
        tails[q] = got[2 * q, SCAP * PIECE :]


def place(got):
    return pl.pallas_call(
        place_body,
        out_shape=[
            jax.ShapeDtypeStruct((1, SCAP, 8 * HALF, BLK), BF),
            jax.ShapeDtypeStruct((4, 16, BLK), BF),
        ],
        compiler_params=params(),
        cost_estimate=cost(0, 2 * 16 * MSG * BLK * 2),
        name="place_served",
    )(got)


def shards(inputs, cotangent, master, moment, variance, slice_start, block_owner, group_heads):
    me = lax.axis_index(("yh", "yl", "x")).astype(jnp.int32)
    y, x = me // 4, me % 4
    ranks = range(16)

    def along_x(k):
        return [(i, i // 4 * 4 + (i + k) % 4) for i in ranks]

    def along_y(k):
        return [(i, (i + 4 * k) % 16) for i in ranks]

    def send(v, pairs):
        return lax.ppermute(v, ("yh", "yl", "x"), pairs)

    def first(k, half):
        to_x = (x + k) % 4
        rows = [2 * ((y + j) % 4) + to_x // 2 for j in (half, half + 2)]
        return rows, (to_x % 2) * 9

    def last(k, half):
        to_y = (y + k) % 4
        tos = [(x + j) % 4 for j in (half, half + 2)]
        return [2 * to_y + t // 2 for t in tos], (tos[0] % 2) * 9 + 5

    def pieces(part, steps, flip=None):
        columns = [g0[0] + g1[0] + [g0[1]] for g0, g1 in steps]
        table = jnp.stack([jnp.stack(c) for c in columns], axis=1)
        return mm(table.astype(jnp.int32), inputs, cotangent, part, flip)

    def long_start(part, groups, flip, along):
        fwd, bwd = pieces(part, groups, flip)
        return send(fwd, along(1)), send(bwd, along(-1))

    a_fwd, a_bwd = long_start(
        FIRST, ((first(2, 0), first(2, 1)), (first(1, 1), first(3, 0))), False, along_x
    )
    b_fwd, b_bwd = long_start(
        LAST, ((last(2, 0), last(3, 0)), (last(1, 1), last(2, 1))), True, along_y
    )
    rest_a = pieces(FIRST, ((first(0, 0), first(0, 1)), (first(1, 0), first(3, 1))))
    rest_b = pieces(LAST, ((last(0, 0), last(1, 0)), (last(0, 1), last(3, 1))))

    def long_end(rest, out_groups, own_groups, fwd, bwd, along, earlier):
        fwd2, bwd2 = relay(rest, out_groups, fwd, bwd, earlier)
        return long_sum(
            rest, own_groups, send(fwd2, along(1)), send(bwd2, along(-1)), fwd, bwd
        )

    part_a = long_end(rest_a, (2, 3), (0, 1), a_fwd, a_bwd, along_x, rest_b)
    part_b = long_end(rest_b, (1, 3), (0, 2), b_fwd, b_bwd, along_y, rest_a)

    def short(parts, along):
        return [parts[0]] + [send(parts[k], along(k)) for k in (2, 1, 3)]

    grad_a, tenth = slice_half(front_body, (WIDE, BLK), *short(part_a, along_y))
    (grad_b,) = slice_half(back_body, (WIDE,), *short(part_b, along_x), tenth)
    halo_a = send(grad_a, [(i + 1, i) for i in range(15)])
    halo_b = send(grad_b, [(i, i + 1) for i in range(15)])

    flat = 16 * 18
    ends = jnp.concatenate([slice_start[1:], jnp.full((1,), flat, jnp.int32)])
    is_me = jnp.arange(16, dtype=jnp.int32) == me
    start = jnp.sum(jnp.where(is_me, slice_start, 0))
    end = jnp.sum(jnp.where(is_me, ends, 0))
    odd = x % 2
    info = jnp.stack([start - (18 * me - 9), end - start, odd]).astype(jnp.int32)
    state = (master, moment, variance)
    keep2, send2 = codes(
        own_body, 2, 2 * HALF + 16, "codes_of_own", info, grad_a, grad_b, *state
    )
    got2 = send(send2, [(i, i ^ 1) for i in ranks])
    keep1, send1, near, far = codes(
        halo_body, 4, HALF + 16, "codes_of_halo", info, halo_b, halo_a, *state
    )
    got1 = send(send1, [(i, i ^ 1) for i in ranks])
    steps = [(i, -1 if i % 2 == 0 else 1) for i in ranks]
    near = send(near, [(i, i + d) for i, d in steps if 0 <= i + d < 16])
    far = send(far, [(i, i + 2 * d) for i, d in steps if 0 <= i + 2 * d < 16])

    packed = jnp.arange(COLS, dtype=jnp.int32)
    per_group = COLS // GROUPS
    group, within = packed // per_group, packed % per_group
    head_at = group * QPER + jnp.minimum(within, QPER - 1)
    heads = jnp.arange(group_heads.shape[0], dtype=jnp.int32)
    head = jnp.sum(jnp.where(head_at[:, None] == heads, group_heads, 0), axis=1)
    n_heads = group_heads.shape[0]
    column = jnp.where(
        within < QPER, head, jnp.where(within == QPER, n_heads + group, n_heads + GROUPS + group)
    )
    earlier = (block_owner[None, :] == block_owner[:, None]) & (packed[None, :] < packed[:, None])
    spot = block_owner * SCAP + jnp.sum(earlier.astype(jnp.int32), axis=1)
    spots = jnp.arange(8 * SCAP, dtype=jnp.int32)
    table = jnp.sum(jnp.where(spots[:, None] == spot[None, :], column + 1, 0), axis=1) - 1
    pack_info = jnp.concatenate([odd[None], table]).astype(jnp.int32)
    out = pack(pack_info, keep2, got2, keep1, got1, near, far)
    out, info = lax.optimization_barrier((out, info))
    new_master, new_moment, new_variance = update_state(
        info, halo_b, grad_a, grad_b, halo_a, *state
    )
    got = lax.all_to_all(out, ("z", "core", "yh"), split_axis=0, concat_axis=0, tiled=True)
    got = lax.all_to_all(got, ("yh", "yl", "x"), split_axis=0, concat_axis=0, tiled=True)
    served_blocks, tails = place(got)
    served_scales = tails[:, :SCAP, 0].T[None]
    return new_master, new_moment, new_variance, served_blocks, served_scales


def solution(mesh):
    dp, serve = ("yh", "yl", "x"), ("z", "core")
    mesh = Mesh(mesh.devices.reshape(2, 2, 4, 4, 2), dp + serve)
    state = P(serve, dp, None, None)
    return jax.shard_map(
        shards,
        mesh=mesh,
        in_specs=(P(dp, serve), P(dp, None), state, state, state, P(), P(), P()),
        out_specs=(state, state, state, P(serve, None, dp, None), P(serve, None, dp)),
        check_vma=False,
    )
```

time: 200 us -> 175 us (0.88)
  blocking collectives: 0 us -> 29.8 us
  starting transfers between devices: 63.9 us -> 38.2 us
  waiting for transfers between devices: 66.8 us -> 42.2 us
  other arithmetic: 11.4 us -> 1.28 us
  local copies, waits for them, and re-layouts: 5.29 us -> 11.4 us
    all_to_all x0 -> x1, blocking collectives: none -> 29.8 us  [shards(): lax.all_to_all(out, ('z', 'core', 'yh'), split_axis=0, concat_axis=0, til...]
    ppermute x27 -> x20, starting transfers between devices: 58.6 us -> 33.6 us  [send(): return lax.ppermute(v, ('yh', 'yl', 'x'), pairs)]
    ppermute x27 -> x20, waiting for transfers between devices: 49.1 us -> 30.6 us  [send(): return lax.ppermute(v, ('yh', 'yl', 'x'), pairs)]
    convert_element_type x8 -> x0, other arithmetic: 9.22 us -> none  [add(): return total.astype(BF)]
    all_to_all x1, waiting for transfers between devices: 17.7 us -> 11.6 us  [shards(): lax.all_to_all(got, ('yh', 'yl', 'x'), split_axis=0, concat_axis=0, tiled...]
    another operation x0 -> x12, local copies, waits for them, and re-layouts: none -> 3.38 us  [pieces(): table = jnp.stack([jnp.stack(c) for c in columns], axis=1)]
    unnamed x20 -> x34, local copies, waits for them, and re-layouts: 4.42 us -> 7.29 us
    pallas_call x9 -> x14, Pallas kernels: 45.5 us -> 47.1 us  [the longest x4 27.2 us: mm(): pl.pallas_call(mm_rest_body if flip is None else mm_send_body, grid_spec=...]
  transfers between devices with their start and end apart: 28 -> 21, of which waited for: 12 -> 9; matrix products, arithmetic and copies ran while one was open for 6% -> 2% of each run, Pallas kernels for 15% -> 21%
where the time goes in v2:
time: 175 us; the launch traced here: 174 us
  Pallas kernels  48.5 us (28%)
  waiting for transfers between devices  42.2 us (24%)
  starting transfers between devices  38.2 us (22%)
  blocking collectives  29.8 us (17%)
  local copies, waits for them, and re-layouts  11.4 us (7%)
  between operations  3.01 us (2%)
    ppermute x20, starting transfers between devices, send(): return lax.ppermute(v, ('yh', 'yl', 'x'), pairs)  33.6 us
    ppermute x20, waiting for transfers between devices, send(): return lax.ppermute(v, ('yh', 'yl', 'x'), pairs)  30.6 us
    all_to_all x1, blocking collectives, shards(): lax.all_to_all(out, ('z', 'core', 'yh'), split_axis=0, concat_axis=0, til...  29.8 us
    pallas_call x4, Pallas kernels, mm(): pl.pallas_call(mm_rest_body if flip is None else mm_send_body, grid_spec=...  27.2 us
    all_to_all x1, waiting for transfers between devices, shards(): lax.all_to_all(got, ('yh', 'yl', 'x'), split_axis=0, concat_axis=0, tiled...  11.6 us
    unnamed x34, local copies, waits for them, and re-layouts  7.29 us
    pallas_call x1, Pallas kernels, update_state(): pl.pallas_call(state_body, grid_spec=pltpu.PrefetchScalarGridSpec(num_sca...  5.63 us
    all_to_all x1, starting transfers between devices, shards(): lax.all_to_all(got, ('yh', 'yl', 'x'), split_axis=0, concat_axis=0, tiled...  4.65 us
  transfers between devices with their start and end apart: 21, of which 9 were waited for; matrix products, arithmetic and copies ran while one was open for 2% of the time, Pallas kernels for 21%

profile of v2, /device:TPU:0, one launch (start us, length us, event | category | flops | bytes accessed | tf_op | source)
XLA Modules:
  0.0 174.4 jit_solution(4724002002360502736)
XLA Ops:
  0.9 0.1 stack.175
  0.9 0.1 stack.181
  1.0 0.7 copy.34.table
  1.7 7.1 %gradient_to_send.2 = (bf16[4,128,1280]{2,1,0:T(8,128)(2,1)}, bf16[4,128,1280]{2,1,0:T(8,128)(2,1)}) custom-call(s32[5,2]{1,0:T(8,128)} %copy.34.table, bf16[1024,1024]{1,0:T(8,128)(2,1)} %refs_3_.7, bf16[1024,1024]{1,0:T(8,128)(2,1)} %refs_3_.7, bf16[1024,1024]{1,0:T(8,128)(2,1)} %refs_3_.7, bf16[1024,1024]{1,0:T(8,128)(2,1)} %refs_3_.7, ...), custom_call_target="tpu_custom_call" | custom-call | flops 2684354560 | bytes 9961472 | tf_op jit(solution)/shard_map/gradient_to_send/pallas_call | solution.py:74
  8.8 1.6 collective-permute-start
  10.4 1.7 collective-permute-start.1
  12.1 0.1 stack.191
  12.3 0.7 copy.36.table
  12.9 6.3 %gradient_to_send.3 = (bf16[4,128,1024]{2,1,0:T(8,128)(2,1)}, bf16[4,128,1024]{2,1,0:T(8,128)(2,1)}) custom-call(s32[5,2]{1,0:T(8,128)} %copy.36.table, bf16[1024,1024]{1,0:T(8,128)(2,1)} %refs_3_.7, bf16[1024,1024]{1,0:T(8,128)(2,1)} %refs_3_.7, bf16[1024,1024]{1,0:T(8,128)(2,1)} %refs_3_.7, bf16[1024,1024]{1,0:T(8,128)(2,1)} %refs_3_.7, ...), custom_call_target="tpu_custom_call" | custom-call | flops 2147483648 | bytes 8388608 | tf_op jit(solution)/shard_map/gradient_to_send/pallas_call | solution.py:74
  19.3 1.7 collective-permute-start.7
  20.9 1.6 collective-permute-start.8
  22.8 0.7 copy.35.table
  23.5 0.7 copy.33.table
  24.2 6.4 %gradient_pieces.3.earlier.to_fwd.to_bwd.own_even.own_odd = bf16[8,128,1024]{2,1,0:T(8,128)(2,1)} custom-call(s32[5,2]{1,0:T(8,128)} %copy.35.table, bf16[1024,1024]{1,0:T(8,128)(2,1)} %refs_3_.7, bf16[1024,1024]{1,0:T(8,128)(2,1)} %refs_3_.7, bf16[1024,1024]{1,0:T(8,128)(2,1)} %refs_3_.7, bf16[1024,1024]{1,0:T(8,128)(2,1)} %refs_3_.7, ...), custom_call_target="tpu_custom_call" | custom-call | flops 2147483648 | bytes 8388608 | tf_op jit(solution)/shard_map/gradient_pieces/pallas_call | solution.py:74
  30.6 7.4 %gradient_pieces.2.to_fwd.to_bwd.own_even.own_odd.earlier = bf16[8,128,1280]{2,1,0:T(8,128)(2,1)} custom-call(s32[5,2]{1,0:T(8,128)} %copy.33.table, bf16[1024,1024]{1,0:T(8,128)(2,1)} %refs_3_.7, bf16[1024,1024]{1,0:T(8,128)(2,1)} %refs_3_.7, bf16[1024,1024]{1,0:T(8,128)(2,1)} %refs_3_.7, bf16[1024,1024]{1,0:T(8,128)(2,1)} %refs_3_.7, ...), custom_call_target="tpu_custom_call" | custom-call | flops 2684354560 | bytes 9961472 | tf_op jit(solution)/shard_map/gradient_pieces/pallas_call | solution.py:74
  37.9 2.7 %collective-permute-done.fwd = bf16[4,128,1280]{2,1,0:T(8,128)(2,1)S(1)} collective-permute-done((bf16[4,128,1280]{2,1,0:T(8,128)(2,1)}, bf16[4,128,1280]{2,1,0:T(8,128)(2,1)S(1)}, u32[]{:S(2)}, u32[]{:S(2)}) %collective-permute-start) | collective-permute-done | bytes 1310752 | tf_op jit(solution)/shard_map/ppermute | solution.py:394
  40.7 0.3 collective-permute-done.1.bwd
  41.0 1.7 copy-done
  42.7 1.4 relay_sums.2
  44.1 1.6 collective-permute-start.2
  45.7 1.7 collective-permute-start.3
  47.4 2.3 %relay_sums.3 = (bf16[2,128,1024]{2,1,0:T(8,128)(2,1)}, bf16[2,128,1024]{2,1,0:T(8,128)(2,1)}) custom-call(bf16[8,128,1024]{2,1,0:T(8,128)(2,1)S(1)} %copy-done.2, bf16[8,128,1024]{2,1,0:T(8,128)(2,1)S(1)} %copy-done.2, bf16[4,128,1024]{2,1,0:T(8,128)(2,1)} %collective-permute-done.7.fwd, bf16[4,128,1024]{2,1,0:T(8,128)(2,1)} %collective-permute-done.8.bwd, ...), custom_call_target="tpu_custom_call" | custom-call | flops 524288 | bytes 3145728 | tf_op jit(solution)/shard_map/relay_sums/pallas_call | solution.py:107
  49.7 1.6 collective-permute-start.9
  51.3 1.7 collective-permute-start.10
  53.0 7.7 %collective-permute-done.2.fwd2 = bf16[2,128,1280]{2,1,0:T(8,128)(2,1)S(1)} collective-permute-done((bf16[2,128,1280]{2,1,0:T(8,128)(2,1)S(1)}, bf16[2,128,1280]{2,1,0:T(8,128)(2,1)S(1)}, u32[]{:S(2)}, u32[]{:S(2)}) %collective-permute-start.2) | collective-permute-done | bytes 655392 | tf_op jit(solution)/shard_map/ppermute | solution.py:394
  60.7 2.2 %long_sums.2 = (bf16[128,1280]{1,0:T(8,128)(2,1)S(1)}, bf16[128,1280]{1,0:T(8,128)(2,1)S(1)}, bf16[128,1280]{1,0:T(8,128)(2,1)}, bf16[128,1280]{1,0:T(8,128)(2,1)S(1)}) custom-call(bf16[8,128,1280]{2,1,0:T(8,128)(2,1)S(1)} %copy-done.1, bf16[8,128,1280]{2,1,0:T(8,128)(2,1)S(1)} %copy-done.1, bf16[2,128,1280]{2,1,0:T(8,128)(2,1)S(1)} %collective-permute-done.2.fwd2, ...), custom_call_target="tpu_custom_call" | custom-call | flops 1310720 | bytes 5242880 | tf_op jit(solution)/shard_map/long_sums/pallas_call | solution.py:129
  62.9 0.7 copy-done.8
  63.6 0.7 copy-done.10
  64.3 0.7 copy-done.12
  65.1 3.4 %collective-permute-start.4 = (bf16[128,1280]{1,0:T(8,128)(2,1)}, bf16[128,1280]{1,0:T(8,128)(2,1)S(1)}, u32[]{:S(2)}, u32[]{:S(2)}) collective-permute-start(bf16[128,1280]{1,0:T(8,128)(2,1)} %get-tuple-element.41), channel_id=1, source_target_pairs={{0,64},{8,72},{16,80},{24,88},{32,96},{40,104},{48,112},{56,120},{... | collective-permute-start | bytes 983048 | tf_op jit(solution)/shard_map/ppermute | solution.py:394
  68.5 0.7 fusion.1
  71.2 2.0 %long_sums.3 = (bf16[128,1024]{1,0:T(8,128)(2,1)S(1)}, bf16[128,1024]{1,0:T(8,128)(2,1)S(1)}, bf16[128,1024]{1,0:T(8,128)(2,1)S(1)}, bf16[128,1024]{1,0:T(8,128)(2,1)S(1)}) custom-call(bf16[8,128,1024]{2,1,0:T(8,128)(2,1)S(1)} %copy-done.2, bf16[8,128,1024]{2,1,0:T(8,128)(2,1)S(1)} %copy-done.2, bf16[2,128,1024]{2,1,0:T(8,128)(2,1)} %collective-permute-done.9.fwd2, ...), custom_call_target="tpu_custom_call" | custom-call | flops 1048576 | bytes 4194304 | tf_op jit(solution)/shard_map/long_sums/pallas_call | solution.py:129
  73.3 2.8 %collective-permute-start.11 = (bf16[128,1024]{1,0:T(8,128)(2,1)S(1)}, bf16[128,1024]{1,0:T(8,128)(2,1)S(1)}, u32[]{:S(2)}, u32[]{:S(2)}) collective-permute-start(bf16[128,1024]{1,0:T(8,128)(2,1)S(1)} %get-tuple-element.50), channel_id=1, source_target_pairs={{0,16},{8,24},{16,0},{24,8},{32,48},{40,56},{48,32},{56,40},{64,80... | collective-permute-start | bytes 786440 | tf_op jit(solution)/shard_map/ppermute | solution.py:394
  76.1 1.1 collective-permute-start.12
  77.2 2.1 %collective-permute-start.13 = (bf16[128,1024]{1,0:T(8,128)(2,1)S(1)}, bf16[128,1024]{1,0:T(8,128)(2,1)S(1)}, u32[]{:S(2)}, u32[]{:S(2)}) collective-permute-start(bf16[128,1024]{1,0:T(8,128)(2,1)S(1)} %get-tuple-element.52), channel_id=1, source_target_pairs={{0,24},{8,0},{16,8},{24,16},{32,56},{40,32},{48,40},{56,48},{64,88... | collective-permute-start | bytes 786440 | tf_op jit(solution)/shard_map/ppermute | solution.py:394
  79.3 0.7 collective-permute-start.5
  80.0 2.6 %collective-permute-start.6 = (bf16[128,1280]{1,0:T(8,128)(2,1)S(1)}, bf16[128,1280]{1,0:T(8,128)(2,1)S(1)}, u32[]{:S(2)}, u32[]{:S(2)}) collective-permute-start(bf16[128,1280]{1,0:T(8,128)(2,1)S(1)} %copy-done.11), channel_id=1, source_target_pairs={{0,96},{8,104},{16,112},{24,120},{32,0},{40,8},{48,16},{56,24},{64... | collective-permute-start | bytes 983048 | tf_op jit(solution)/shard_map/ppermute | solution.py:394
  82.6 0.2 convert_reduce_fusion
  82.8 0.1 select_reduce_fusion.1
  82.9 4.7 %collective-permute-done.5.far = bf16[128,1280]{1,0:T(8,128)(2,1)S(1)} collective-permute-done((bf16[128,1280]{1,0:T(8,128)(2,1)S(1)}, bf16[128,1280]{1,0:T(8,128)(2,1)S(1)}, u32[]{:S(2)}, u32[]{:S(2)}) %collective-permute-start.5) | collective-permute-done | bytes 327712 | tf_op jit(solution)/shard_map/ppermute | solution.py:394
  87.6 0.2 slice_half.2
  87.8 0.1 slice_half.3.b.grad_b
  88.0 1.8 %collective-permute-start.15 = (bf16[128,1152]{1,0:T(8,128)(2,1)S(1)}, bf16[128,1152]{1,0:T(8,128)(2,1)S(1)}, u32[]{:S(2)}, u32[]{:S(2)}) collective-permute-start(bf16[128,1152]{1,0:T(8,128)(2,1)S(1)} %slice_half.3.b.grad_b), channel_id=1, source_target_pairs={{0,8},{8,16},{16,24},{24,32},{32,40},{40,48},{48,56},{56,64},{64,7... | collective-permute-start | bytes 884744 | tf_op jit(solution)/shard_map/ppermute | solution.py:394
  89.8 1.3 collective-permute-start.16
  91.1 0.1 select_reduce_fusion
  91.2 1.9 %codes_of_own.1 = (bf16[144,1152]{1,0:T(8,128)(2,1)S(1)}, bf16[144,1152]{1,0:T(8,128)(2,1)S(1)}) custom-call(s32[3]{0:T(128)S(1)} %pad_add_fusion.5.info, bf16[128,1152]{1,0:T(8,128)(2,1)S(1)} %get-tuple-element.44.a.grad_a, bf16[128,1152]{1,0:T(8,128)(2,1)S(1)} %slice_half.3.b.grad_b, f32[1,36,128,128]{3,2,1,0:T(8,128)S(1)} %copy-done.3, ...), custom_call_target="tpu_custom_call" | custom-call | flops 8847360 | bytes 7077888 | tf_op jit(solution)/shard_map/codes_of_own/pallas_call | solution.py:237
  93.1 2.7 %collective-permute-start.14 = (bf16[144,1152]{1,0:T(8,128)(2,1)S(1)}, bf16[144,1152]{1,0:T(8,128)(2,1)S(1)}, u32[]{:S(2)}, u32[]{:S(2)}) collective-permute-start(bf16[144,1152]{1,0:T(8,128)(2,1)S(1)} %get-tuple-element.55), channel_id=1, source_target_pairs={{0,8},{8,0},{16,24},{24,16},{32,40},{40,32},{48,56},{56,48},{64,72... | collective-permute-start | bytes 995336 | tf_op jit(solution)/shard_map/ppermute | solution.py:394
  95.8 5.8 %collective-permute-done.16.after.halo_a = bf16[128,1152]{1,0:T(8,128)(2,1)S(1)} collective-permute-done((bf16[128,1152]{1,0:T(8,128)(2,1)S(1)}, bf16[128,1152]{1,0:T(8,128)(2,1)S(1)}, u32[]{:S(2)}, u32[]{:S(2)}) %collective-permute-start.16) | collective-permute-done | bytes 294944 | tf_op jit(solution)/shard_map/ppermute | solution.py:394
  101.6 1.9 %codes_of_halo.1 = (bf16[80,1152]{1,0:T(8,128)(2,1)S(1)}, bf16[80,1152]{1,0:T(8,128)(2,1)S(1)}, bf16[80,1152]{1,0:T(8,128)(2,1)S(1)}, bf16[80,1152]{1,0:T(8,128)(2,1)S(1)}) custom-call(s32[3]{0:T(128)S(1)} %pad_add_fusion.5.info, bf16[128,1152]{1,0:T(8,128)(2,1)S(1)} %collective-permute-done.15.before.halo_b, ...), custom_call_target="tpu_custom_call" | custom-call | flops 8847360 | bytes 7077888 | tf_op jit(solution)/shard_map/codes_of_halo/pallas_call | solution.py:237
  103.5 0.1 collective-permute-start.17
  103.6 0.7 collective-permute-start.18
  104.3 1.3 collective-permute-start.19
  105.7 1.9 %collective-permute-done.14.got2 = bf16[144,1152]{1,0:T(8,128)(2,1)S(1)} collective-permute-done((bf16[144,1152]{1,0:T(8,128)(2,1)S(1)}, bf16[144,1152]{1,0:T(8,128)(2,1)S(1)}, u32[]{:S(2)}, u32[]{:S(2)}) %collective-permute-start.14) | collective-permute-done | bytes 331808 | tf_op jit(solution)/shard_map/ppermute | solution.py:394
  107.6 2.8 %collective-permute-done.17.got1 = bf16[80,1152]{1,0:T(8,128)(2,1)S(1)} collective-permute-done((bf16[80,1152]{1,0:T(8,128)(2,1)S(1)}, bf16[80,1152]{1,0:T(8,128)(2,1)S(1)}, u32[]{:S(2)}, u32[]{:S(2)}) %collective-permute-start.17) | collective-permute-done | bytes 184352 | tf_op jit(solution)/shard_map/ppermute | solution.py:394
  110.4 4.6 %collective-permute-done.19.far = bf16[80,1152]{1,0:T(8,128)(2,1)S(1)} collective-permute-done((bf16[80,1152]{1,0:T(8,128)(2,1)S(1)}, bf16[80,1152]{1,0:T(8,128)(2,1)S(1)}, u32[]{:S(2)}, u32[]{:S(2)}) %collective-permute-start.19) | collective-permute-done | bytes 184352 | tf_op jit(solution)/shard_map/ppermute | solution.py:394
  115.0 1.3 pack_by_owner.1
  116.3 29.8 %all_to_all.10 = bf16[16,304,128]{2,1,0:T(8,128)(2,1)} all-to-all(bf16[16,304,128]{2,1,0:T(8,128)(2,1)S(1)} %pack_by_owner.1), channel_id=1, replica_groups=mesh['yh'=2,'yl'=2,'x'=4,'z'=4,'core'=2] {'z','core','yh'}, dimensions={0} | all-to-all | bytes 2490368 | tf_op jit(solution)/shard_map/all_to_all | solution.py:481
  146.1 4.7 %all-to-all-start.1 = ((bf16[16,304,128]{2,1,0:T(8,128)(2,1)}), bf16[16,304,128]{2,1,0:T(8,128)(2,1)}, u32[]{:S(2)}, u32[]{:S(2)}) async-start(bf16[16,304,128]{2,1,0:T(8,128)(2,1)} %all_to_all.10), calls=%async_computation.1 | async-start | bytes 2490368 | tf_op jit(solution)/shard_map/all_to_all | solution.py:482
  150.8 1.7 copy-done.5
  152.5 1.7 copy-done.7
  154.1 5.6 %update_state.1 = (f32[1,36,128,128]{3,2,1,0:T(8,128)}, f32[1,36,128,128]{3,2,1,0:T(8,128)}, f32[1,36,128,128]{3,2,1,0:T(8,128)}) custom-call(s32[3]{0:T(128)S(1)} %pad_add_fusion.5.info, bf16[128,1152]{1,0:T(8,128)(2,1)S(1)} %collective-permute-done.15.before.halo_b, bf16[128,1152]{1,0:T(8,128)(2,1)S(1)} %get-tuple-element.44.a.grad_a, ...), custom_call_target="tpu_custom_call" | custom-call | flops 11796480 | bytes 15335424 | tf_op jit(solution)/shard_map/update_state/pallas_call | solution.py:280
  159.8 11.6 %all-to-all-done.1.got = bf16[16,304,128]{2,1,0:T(8,128)(2,1)} async-done(((bf16[16,304,128]{2,1,0:T(8,128)(2,1)}), bf16[16,304,128]{2,1,0:T(8,128)(2,1)}, u32[]{:S(2)}, u32[]{:S(2)}) %all-to-all-start.1) | async-done | bytes 1245216 | tf_op jit(solution)/shard_map/all_to_all | solution.py:482
  171.4 2.4 %place_served.1 = (bf16[1,9,512,128]{3,2,1,0:T(8,128)(2,1)}, bf16[4,16,128]{2,1,0:T(8,128)(2,1)S(1)}) custom-call(bf16[16,304,128]{2,1,0:T(8,128)(2,1)} %all-to-all-done.1.got), custom_call_target="tpu_custom_call" | custom-call | bytes 2490368 | tf_op jit(solution)/shard_map/place_served/pallas_call | solution.py:370
  173.8 0.7 slice_reduce_fusion
  (55 shorter events, 0.8 us)
Async XLA Ops:
  8.8 31.8 %collective-permute-start = (bf16[4,128,1280]{2,1,0:T(8,128)(2,1)}, bf16[4,128,1280]{2,1,0:T(8,128)(2,1)S(1)}, u32[]{:S(2)}, u32[]{:S(2)}) collective-permute-start(bf16[4,128,1280]{2,1,0:T(8,128)(2,1)} %get-tuple-element.36), channel_id=1, source_target_pairs={{0,8},{8,16},{16,24},{24,0},{32,40},{40,48},{48,56},{56,32},{64,72... | collective-permute-start | bytes 3932168 | tf_op jit(solution)/shard_map/ppermute | solution.py:394
  10.4 30.6 %collective-permute-start.1 = (bf16[4,128,1280]{2,1,0:T(8,128)(2,1)}, bf16[4,128,1280]{2,1,0:T(8,128)(2,1)}, u32[]{:S(2)}, u32[]{:S(2)}) collective-permute-start(bf16[4,128,1280]{2,1,0:T(8,128)(2,1)} %get-tuple-element.37), channel_id=1, source_target_pairs={{0,24},{8,0},{16,8},{24,16},{32,56},{40,32},{48,40},{56,48},{64,88... | collective-permute-start | bytes 3932168 | tf_op jit(solution)/shard_map/ppermute | solution.py:394
  19.3 28.2 %collective-permute-start.7 = (bf16[4,128,1024]{2,1,0:T(8,128)(2,1)}, bf16[4,128,1024]{2,1,0:T(8,128)(2,1)}, u32[]{:S(2)}, u32[]{:S(2)}) collective-permute-start(bf16[4,128,1024]{2,1,0:T(8,128)(2,1)} %get-tuple-element.45), channel_id=1, source_target_pairs={{0,32},{8,40},{16,48},{24,56},{32,64},{40,72},{48,80},{56,88},{64,... | collective-permute-start | bytes 3145736 | tf_op jit(solution)/shard_map/ppermute | solution.py:394
  20.9 26.5 %collective-permute-start.8 = (bf16[4,128,1024]{2,1,0:T(8,128)(2,1)}, bf16[4,128,1024]{2,1,0:T(8,128)(2,1)}, u32[]{:S(2)}, u32[]{:S(2)}) collective-permute-start(bf16[4,128,1024]{2,1,0:T(8,128)(2,1)} %get-tuple-element.46), channel_id=1, source_target_pairs={{0,96},{8,104},{16,112},{24,120},{32,0},{40,8},{48,16},{56,24},{64... | collective-permute-start | bytes 3145736 | tf_op jit(solution)/shard_map/ppermute | solution.py:394
  30.6 10.4 %copy-start.2 = (bf16[8,128,1024]{2,1,0:T(8,128)(2,1)S(1)}, bf16[8,128,1024]{2,1,0:T(8,128)(2,1)}, u32[]{:S(2)}) copy-start(bf16[8,128,1024]{2,1,0:T(8,128)(2,1)} %gradient_pieces.3.earlier.to_fwd.to_bwd.own_even.own_odd) | copy-start | bytes 6291460
  41.0 1.7 copy-start
  44.1 16.6 %collective-permute-start.2 = (bf16[2,128,1280]{2,1,0:T(8,128)(2,1)S(1)}, bf16[2,128,1280]{2,1,0:T(8,128)(2,1)S(1)}, u32[]{:S(2)}, u32[]{:S(2)}) collective-permute-start(bf16[2,128,1280]{2,1,0:T(8,128)(2,1)S(1)} %get-tuple-element.38), channel_id=1, source_target_pairs={{0,8},{8,16},{16,24},{24,0},{32,40},{40,48},{48,56},{56,32},{64,72... | collective-permute-start | bytes 1966088 | tf_op jit(solution)/shard_map/ppermute | solution.py:394
  45.7 15.0 %copy-start.1 = (bf16[8,128,1280]{2,1,0:T(8,128)(2,1)S(1)}, bf16[8,128,1280]{2,1,0:T(8,128)(2,1)}, u32[]{:S(2)}) copy-start(bf16[8,128,1280]{2,1,0:T(8,128)(2,1)} %gradient_pieces.2.to_fwd.to_bwd.own_even.own_odd.earlier) | copy-start | bytes 7864324
  45.7 15.0 %collective-permute-start.3 = (bf16[2,128,1280]{2,1,0:T(8,128)(2,1)S(1)}, bf16[2,128,1280]{2,1,0:T(8,128)(2,1)S(1)}, u32[]{:S(2)}, u32[]{:S(2)}) collective-permute-start(bf16[2,128,1280]{2,1,0:T(8,128)(2,1)S(1)} %get-tuple-element.39), channel_id=1, source_target_pairs={{0,24},{8,0},{16,8},{24,16},{32,56},{40,32},{48,40},{56,48},{64,88... | collective-permute-start | bytes 1966088 | tf_op jit(solution)/shard_map/ppermute | solution.py:394
  49.7 21.5 %collective-permute-start.9 = (bf16[2,128,1024]{2,1,0:T(8,128)(2,1)}, bf16[2,128,1024]{2,1,0:T(8,128)(2,1)}, u32[]{:S(2)}, u32[]{:S(2)}) collective-permute-start(bf16[2,128,1024]{2,1,0:T(8,128)(2,1)} %get-tuple-element.47), channel_id=1, source_target_pairs={{0,32},{8,40},{16,48},{24,56},{32,64},{40,72},{48,80},{56,88},{64,... | collective-permute-start | bytes 1572872 | tf_op jit(solution)/shard_map/ppermute | solution.py:394
  51.3 17.2 %copy-start.15 = (s32[16]{0:T(128)S(1)}, s32[16]{0:T(128)}, u32[]{:S(2)}) copy-start(s32[16]{0:T(128)} %param.13) | copy-start | bytes 196
  51.3 19.9 %collective-permute-start.10 = (bf16[2,128,1024]{2,1,0:T(8,128)(2,1)}, bf16[2,128,1024]{2,1,0:T(8,128)(2,1)}, u32[]{:S(2)}, u32[]{:S(2)}) collective-permute-start(bf16[2,128,1024]{2,1,0:T(8,128)(2,1)} %get-tuple-element.48), channel_id=1, source_target_pairs={{0,96},{8,104},{16,112},{24,120},{32,0},{40,8},{48,16},{56,24},{64... | collective-permute-start | bytes 1572872 | tf_op jit(solution)/shard_map/ppermute | solution.py:394
  62.9 0.7 copy-start.8
  63.6 0.7 copy-start.10
  64.3 0.7 copy-start.12
  65.1 14.9 %collective-permute-start.4 = (bf16[128,1280]{1,0:T(8,128)(2,1)}, bf16[128,1280]{1,0:T(8,128)(2,1)S(1)}, u32[]{:S(2)}, u32[]{:S(2)}) collective-permute-start(bf16[128,1280]{1,0:T(8,128)(2,1)} %get-tuple-element.41), channel_id=1, source_target_pairs={{0,64},{8,72},{16,80},{24,88},{32,96},{40,104},{48,112},{56,120},{... | collective-permute-start | bytes 983048 | tf_op jit(solution)/shard_map/ppermute | solution.py:394
  71.1 8.2 %copy-start.13 = (bf16[128,1280]{1,0:T(8,128)(2,1)S(1)}, bf16[128,1280]{1,0:T(8,128)(2,1)}, u32[]{:S(2)}) copy-start(bf16[128,1280]{1,0:T(8,128)(2,1)} %copy-done.12) | copy-start | bytes 983044
  71.1 8.9 %copy-start.11 = (bf16[128,1280]{1,0:T(8,128)(2,1)S(1)}, bf16[128,1280]{1,0:T(8,128)(2,1)}, u32[]{:S(2)}) copy-start(bf16[128,1280]{1,0:T(8,128)(2,1)} %copy-done.10) | copy-start | bytes 983044
  71.2 11.5 %copy-start.14 = (s32[36]{0:T(128)S(1)}, s32[36]{0:T(128)}, u32[]{:S(2)}) copy-start(s32[36]{0:T(128)} %param.14) | copy-start | bytes 436
  71.2 11.7 %copy-start.16 = (s32[32]{0:T(128)S(1)}, s32[32]{0:T(128)}, u32[]{:S(2)}) copy-start(s32[32]{0:T(128)} %param.15) | copy-start | bytes 388
  71.2 16.4 %copy-start.9 = (bf16[128,1280]{1,0:T(8,128)(2,1)S(1)}, bf16[128,1280]{1,0:T(8,128)(2,1)}, u32[]{:S(2)}) copy-start(bf16[128,1280]{1,0:T(8,128)(2,1)} %copy-done.8) | copy-start | bytes 983044
  71.2 20.0 %copy-start.4 = (f32[1,36,128,128]{3,2,1,0:T(8,128)S(1)}, f32[1,36,128,128]{3,2,1,0:T(8,128)}, u32[]{:S(2)}) copy-start(f32[1,36,128,128]{3,2,1,0:T(8,128)} %moment.5) | copy-start | bytes 7077892
  71.2 20.0 %copy-start.6 = (f32[1,36,128,128]{3,2,1,0:T(8,128)S(1)}, f32[1,36,128,128]{3,2,1,0:T(8,128)}, u32[]{:S(2)}) copy-start(f32[1,36,128,128]{3,2,1,0:T(8,128)} %variance.5) | copy-start | bytes 7077892
  73.3 17.9 %copy-start.3 = (f32[1,36,128,128]{3,2,1,0:T(8,128)S(1)}, f32[1,36,128,128]{3,2,1,0:T(8,128)}, u32[]{:S(2)}) copy-start(f32[1,36,128,128]{3,2,1,0:T(8,128)} %master.5) | copy-start | bytes 7077892
  73.3 14.5 %collective-permute-start.11 = (bf16[128,1024]{1,0:T(8,128)(2,1)S(1)}, bf16[128,1024]{1,0:T(8,128)(2,1)S(1)}, u32[]{:S(2)}, u32[]{:S(2)}) collective-permute-start(bf16[128,1024]{1,0:T(8,128)(2,1)S(1)} %get-tuple-element.50), channel_id=1, source_target_pairs={{0,16},{8,24},{16,0},{24,8},{32,48},{40,56},{48,32},{56,40},{64,80... | collective-permute-start | bytes 786440 | tf_op jit(solution)/shard_map/ppermute | solution.py:394
  76.1 11.7 %collective-permute-start.12 = (bf16[128,1024]{1,0:T(8,128)(2,1)S(1)}, bf16[128,1024]{1,0:T(8,128)(2,1)S(1)}, u32[]{:S(2)}, u32[]{:S(2)}) collective-permute-start(bf16[128,1024]{1,0:T(8,128)(2,1)S(1)} %get-tuple-element.51), channel_id=1, source_target_pairs={{0,8},{8,16},{16,24},{24,0},{32,40},{40,48},{48,56},{56,32},{64,72... | collective-permute-start | bytes 786440 | tf_op jit(solution)/shard_map/ppermute | solution.py:394
  77.2 10.6 %collective-permute-start.13 = (bf16[128,1024]{1,0:T(8,128)(2,1)S(1)}, bf16[128,1024]{1,0:T(8,128)(2,1)S(1)}, u32[]{:S(2)}, u32[]{:S(2)}) collective-permute-start(bf16[128,1024]{1,0:T(8,128)(2,1)S(1)} %get-tuple-element.52), channel_id=1, source_target_pairs={{0,24},{8,0},{16,8},{24,16},{32,56},{40,32},{48,40},{56,48},{64,88... | collective-permute-start | bytes 786440 | tf_op jit(solution)/shard_map/ppermute | solution.py:394
  79.3 8.3 %collective-permute-start.5 = (bf16[128,1280]{1,0:T(8,128)(2,1)S(1)}, bf16[128,1280]{1,0:T(8,128)(2,1)S(1)}, u32[]{:S(2)}, u32[]{:S(2)}) collective-permute-start(bf16[128,1280]{1,0:T(8,128)(2,1)S(1)} %copy-done.13), channel_id=1, source_target_pairs={{0,32},{8,40},{16,48},{24,56},{32,64},{40,72},{48,80},{56,88},{64,... | collective-permute-start | bytes 983048 | tf_op jit(solution)/shard_map/ppermute | solution.py:394
  80.0 7.6 %collective-permute-start.6 = (bf16[128,1280]{1,0:T(8,128)(2,1)S(1)}, bf16[128,1280]{1,0:T(8,128)(2,1)S(1)}, u32[]{:S(2)}, u32[]{:S(2)}) collective-permute-start(bf16[128,1280]{1,0:T(8,128)(2,1)S(1)} %copy-done.11), channel_id=1, source_target_pairs={{0,96},{8,104},{16,112},{24,120},{32,0},{40,8},{48,16},{56,24},{64... | collective-permute-start | bytes 983048 | tf_op jit(solution)/shard_map/ppermute | solution.py:394
  88.0 7.8 %collective-permute-start.15 = (bf16[128,1152]{1,0:T(8,128)(2,1)S(1)}, bf16[128,1152]{1,0:T(8,128)(2,1)S(1)}, u32[]{:S(2)}, u32[]{:S(2)}) collective-permute-start(bf16[128,1152]{1,0:T(8,128)(2,1)S(1)} %slice_half.3.b.grad_b), channel_id=1, source_target_pairs={{0,8},{8,16},{16,24},{24,32},{32,40},{40,48},{48,56},{56,64},{64,7... | collective-permute-start | bytes 884744 | tf_op jit(solution)/shard_map/ppermute | solution.py:394
  89.8 11.8 %collective-permute-start.16 = (bf16[128,1152]{1,0:T(8,128)(2,1)S(1)}, bf16[128,1152]{1,0:T(8,128)(2,1)S(1)}, u32[]{:S(2)}, u32[]{:S(2)}) collective-permute-start(bf16[128,1152]{1,0:T(8,128)(2,1)S(1)} %get-tuple-element.44.a.grad_a), channel_id=1, source_target_pairs={{8,0},{16,8},{24,16},{32,24},{40,32},{48,40},{56,48},{64,56},{72,6... | collective-permute-start | bytes 884744 | tf_op jit(solution)/shard_map/ppermute | solution.py:394
  93.1 14.5 %collective-permute-start.14 = (bf16[144,1152]{1,0:T(8,128)(2,1)S(1)}, bf16[144,1152]{1,0:T(8,128)(2,1)S(1)}, u32[]{:S(2)}, u32[]{:S(2)}) collective-permute-start(bf16[144,1152]{1,0:T(8,128)(2,1)S(1)} %get-tuple-element.55), channel_id=1, source_target_pairs={{0,8},{8,0},{16,24},{24,16},{32,40},{40,32},{48,56},{56,48},{64,72... | collective-permute-start | bytes 995336 | tf_op jit(solution)/shard_map/ppermute | solution.py:394
  103.5 6.9 %collective-permute-start.17 = (bf16[80,1152]{1,0:T(8,128)(2,1)S(1)}, bf16[80,1152]{1,0:T(8,128)(2,1)S(1)}, u32[]{:S(2)}, u32[]{:S(2)}) collective-permute-start(bf16[80,1152]{1,0:T(8,128)(2,1)S(1)} %get-tuple-element.57), channel_id=1, source_target_pairs={{0,8},{8,0},{16,24},{24,16},{32,40},{40,32},{48,56},{56,48},{64,72... | collective-permute-start | bytes 552968 | tf_op jit(solution)/shard_map/ppermute | solution.py:394
  103.6 6.8 %collective-permute-start.18 = (bf16[80,1152]{1,0:T(8,128)(2,1)S(1)}, bf16[80,1152]{1,0:T(8,128)(2,1)S(1)}, u32[]{:S(2)}, u32[]{:S(2)}) collective-permute-start(bf16[80,1152]{1,0:T(8,128)(2,1)S(1)} %get-tuple-element.58), channel_id=1, source_target_pairs={{8,16},{16,8},{24,32},{32,24},{40,48},{48,40},{56,64},{64,56},{72,... | collective-permute-start | bytes 552968 | tf_op jit(solution)/shard_map/ppermute | solution.py:394
  104.3 10.7 %collective-permute-start.19 = (bf16[80,1152]{1,0:T(8,128)(2,1)S(1)}, bf16[80,1152]{1,0:T(8,128)(2,1)S(1)}, u32[]{:S(2)}, u32[]{:S(2)}) collective-permute-start(bf16[80,1152]{1,0:T(8,128)(2,1)S(1)} %get-tuple-element.59), channel_id=1, source_target_pairs={{8,24},{16,0},{24,40},{32,16},{40,56},{48,32},{56,72},{64,48},{72,... | collective-permute-start | bytes 552968 | tf_op jit(solution)/shard_map/ppermute | solution.py:394
  146.1 25.2 %all-to-all-start.1 = ((bf16[16,304,128]{2,1,0:T(8,128)(2,1)}), bf16[16,304,128]{2,1,0:T(8,128)(2,1)}, u32[]{:S(2)}, u32[]{:S(2)}) async-start(bf16[16,304,128]{2,1,0:T(8,128)(2,1)} %all_to_all.10), calls=%async_computation.1 | async-start | bytes 2490368 | tf_op jit(solution)/shard_map/all_to_all | solution.py:482
  150.8 1.7 copy-start.5
  152.5 1.7 copy-start.7

commit v3 on v2

--- a/solution.py
+++ b/solution.py
@@ -1,3 +1,5 @@
+import functools
+
 import jax
 import jax.numpy as jnp
 from jax import lax
@@ -46,22 +48,42 @@
             yield u, slice(n * TILE, (n + 1) * TILE), prod[u * BLK : (u + 1) * BLK]
 
 
-def mm_send_body(table, *refs):
+def mm_send_body(tiles, spot, *refs):
     fwd, bwd = refs[-2:]
-    for u, lanes, prod in mm_products(refs[:-2]):
+    for u, lanes, prod in mm_products(refs[: 4 + tiles]):
         (fwd if u < 2 else bwd)[u % 2, :, lanes] = prod
 
 
-def mm_rest_body(table, *refs):
+def mm_rest_body(spot, *refs):
     for u, lanes, prod in mm_products(refs[:-1]):
         refs[-1][u, :, lanes] = prod
 
 
-def mm(table, inputs, cotangent, part, flip=None):
+def mm(spot, which, steps, inputs, cotangent, flip=None):
     tok = inputs.shape[0]
-    left = lambda n: pl.BlockSpec((tok, BLK), lambda g, t: (0, t[n, g]))
-    right = lambda n: pl.BlockSpec((tok, TILE), lambda g, t: (0, t[4, g] + n))
+    part = FIRST if which == 0 else LAST
     tiles = part // TILE
+
+    def spread(n, g, t):
+        (k0, j0), (k1, j1) = steps[0][n], steps[1][n]
+        k, j = jnp.where(g == 0, k0, k1), jnp.where(g == 0, j0, j1)
+        dx, dy = (k, j) if which == 0 else (j, k)
+        return (t[0] + dx) & 3, (t[1] + dy) & 3
+
+    def left(n):
+        def at(g, t):
+            to_x, to_y = spread(n, g, t)
+            return 0, 2 * to_y + (to_x >> 1)
+
+        return pl.BlockSpec((tok, BLK), at)
+
+    def right(n):
+        def at(g, t):
+            to_x, _ = spread(0, g, t)
+            return 0, (to_x & 1) * 9 + (0 if which == 0 else FIRST // TILE) + n
+
+        return pl.BlockSpec((tok, TILE), at)
+
     if flip is None:
         out_specs = pl.BlockSpec((4, BLK, part), lambda g, t: (g, 0, 0))
         out_shape = jax.ShapeDtypeStruct((8, BLK, part), BF)
@@ -72,7 +94,7 @@
         ]
         out_shape = [jax.ShapeDtypeStruct((4, BLK, part), BF)] * 2
     return pl.pallas_call(
-        mm_rest_body if flip is None else mm_send_body,
+        mm_rest_body if flip is None else functools.partial(mm_send_body, tiles),
         grid_spec=pltpu.PrefetchScalarGridSpec(
             num_scalar_prefetch=1,
             grid=(2,),
@@ -83,7 +105,7 @@
         compiler_params=params(60),
         cost_estimate=cost(2 * 2 * 512 * part * tok, 2 * (tok * (part + 512) + 512 * part) * 2),
         name="gradient_pieces" if flip is None else "gradient_to_send",
-    )(table, *([inputs] * 4), *([cotangent] * tiles))
+    )(spot, *([inputs] * 4), *([cotangent] * tiles))
 
 
 def total(*parts):
@@ -97,7 +119,8 @@
     return pl.BlockSpec((2, BLK, part), lambda s: (group, 0, 0))
 
 
-def relay_body(to_fwd, to_bwd, fwd, bwd, earlier, out_fwd, out_bwd):
+def relay_body(to_fwd, to_bwd, fwd, bwd, *refs):
+    out_fwd, out_bwd = refs[-2:]
     out_fwd[...] = total(to_fwd[...], fwd[...])
     out_bwd[...] = total(to_bwd[...], bwd[...])
 
@@ -108,13 +131,13 @@
         relay_body,
         grid=(1,),
         in_specs=[pair_spec(part, g) for g in (groups[0], groups[1], 0, 0)]
-        + [pl.BlockSpec(memory_space=pl.ANY)],
+        + [pl.BlockSpec(memory_space=pl.ANY)] * len(earlier),
         out_specs=[pair_spec(part, 0)] * 2,
         out_shape=[jax.ShapeDtypeStruct((2, BLK, part), BF)] * 2,
         compiler_params=params(),
         cost_estimate=cost(4 * BLK * part, 12 * BLK * part * 2),
         name="relay_sums",
-    )(rest, rest, fwd, bwd, earlier)
+    )(rest, rest, fwd, bwd, *earlier)
 
 
 def long_sum_body(own_even, own_odd, fwd2, bwd2, fwd, bwd, e0, e1, e2, e3):
@@ -138,25 +161,39 @@
     )(rest, rest, fwd2, bwd2, fwd, bwd)
 
 
-def front_body(own, near, far, other, out, tenth):
-    part = total(own[...], near[...], far[...], other[...])
-    out[...] = part[:, :WIDE]
-    tenth[...] = part[:, WIDE:]
-
-
-def back_body(own, near, far, other, tenth, out):
-    out[:, :BLK] = tenth[...]
-    out[:, BLK:] = total(own[...], near[...], far[...], other[...])
-
-
-def slice_half(body, out_widths, *parts):
-    return pl.pallas_call(
-        body,
-        out_shape=[jax.ShapeDtypeStruct((BLK, w), BF) for w in out_widths],
-        compiler_params=params(),
-        cost_estimate=cost(4 * BLK * WIDE, 7 * BLK * WIDE * 2),
-        name="slice_half",
-    )(*parts)
+def slice_body(info, *refs):
+    front, back, to_pair, to_cross = refs[8:]
+    first = total(*(ref[...] for ref in refs[:4]))
+    last = total(*(ref[...] for ref in refs[4:8]))
+    front[...] = first[:, :WIDE]
+    back[:, :BLK] = first[:, WIDE:]
+    back[:, BLK:] = last
+
+    @pl.when(info[2] == 0)
+    def _():
+        to_pair[...] = back[...]
+        to_cross[...] = front[...]
+
+    @pl.when(info[2] == 1)
+    def _():
+        to_pair[...] = front[...]
+        to_cross[...] = back[...]
+
+
+def slices(info, *parts):
+    return pl.pallas_call(
+        slice_body,
+        grid_spec=pltpu.PrefetchScalarGridSpec(
+            num_scalar_prefetch=1,
+            grid=(1,),
+            in_specs=[pl.BlockSpec(v.shape, lambda s, t: (0, 0)) for v in parts],
+            out_specs=[pl.BlockSpec((BLK, WIDE), lambda s, t: (0, 0))] * 4,
+        ),
+        out_shape=[jax.ShapeDtypeStruct((BLK, WIDE), BF)] * 4,
+        compiler_params=params(),
+        cost_estimate=cost(8 * BLK * WIDE, 12 * BLK * WIDE * 2),
+        name="slices",
+    )(info, *parts)
 
 
 def adam_step(old, moment, variance, grad):
@@ -212,24 +249,16 @@
 
 
 def halo_body(
-    info, before, after, master, moment, variance, keep, send, near, far, mine, other, scales
+    info, inside, cross, master, moment, variance, keep, send, near, far, mine, other, scales
 ):
-    code_body((0, 3), info, before, after, master, moment, variance, mine, other, scales)
-    tails = [scale_rows(scales, (n,)) for n in range(2)]
-
-    def write(inside):
-        cross = 1 - inside
-        keep[:HALF] = mine[inside]
-        keep[HALF:] = tails[inside]
-        send[:HALF] = other[inside]
-        send[HALF:] = tails[inside]
-        near[:HALF] = other[cross]
-        near[HALF:] = tails[cross]
-        far[:HALF] = mine[cross]
-        far[HALF:] = tails[cross]
-
-    pl.when(info[2] == 0)(lambda: write(1))
-    pl.when(info[2] == 1)(lambda: write(0))
+    odd = info[2]
+    units = (3 - 3 * odd, 3 * odd)
+    code_body(units, info, inside, cross, master, moment, variance, mine, other, scales)
+    for n, outs in enumerate(((keep, send), (far, near))):
+        tail = scale_rows(scales, (n,))
+        for ref, held in zip(outs, (mine, other)):
+            ref[:HALF] = held[n]
+            ref[HALF:] = tail
 
 
 def codes(body, n_out, rows, name, info, a, b, master, moment, variance):
@@ -255,7 +284,7 @@
 
 
 def state_body(
-    info, halo_b, grad_a, grad_b, halo_a, master, moment, variance,
+    info, inside, front, back, cross, master, moment, variance,
     new_master, new_moment, new_variance, window,
 ):
     step = pl.program_id(0)
@@ -263,8 +292,10 @@
 
     @pl.when(step == 0)
     def _():
-        for q, ref in enumerate((halo_b, grad_a, grad_b, halo_a)):
-            window[q] = ref[...]
+        window[1] = front[...]
+        window[2] = back[...]
+        window[3 - 3 * info[2]] = inside[...]
+        window[3 * info[2]] = cross[...]
 
     for n in range(4):
         slot = step * 4 + n
@@ -275,7 +306,7 @@
         )
 
 
-def update_state(info, halo_b, grad_a, grad_b, halo_a, master, moment, variance):
+def update_state(info, inside, front, back, cross, master, moment, variance):
     state = pl.BlockSpec((1, 4, BLK, BLK), lambda s, t: (0, s, 0, 0))
     return pl.pallas_call(
         state_body,
@@ -290,7 +321,7 @@
         compiler_params=params(),
         cost_estimate=cost(36 * 16384 * 20, 36 * 16384 * 26),
         name="update_state",
-    )(info, halo_b, grad_a, grad_b, halo_a, master, moment, variance)
+    )(info, inside, front, back, cross, master, moment, variance)
 
 
 def pack_body(info, keep2, got2, keep1, got1, near, far, out, row, tails):
@@ -356,14 +387,17 @@
     )(info, *parts)
 
 
-def place_body(got, out, tails):
+def place_body(got, out, scales):
     for src in range(16):
         upper, low, x = src // 8, src // 4 % 2, src % 4
         at = (2 * low + x // 2) * BLK + (x % 2) * HALF + upper * PIECE
         for t in range(SCAP):
             out[0, t, at : at + PIECE] = got[src, t * PIECE : (t + 1) * PIECE]
+    lane = lax.broadcasted_iota(jnp.int32, (16, BLK), 1)
+    rows = jnp.zeros((16, BLK), F32)
     for q in range(4):
-        tails[q] = got[2 * q, SCAP * PIECE :]
+        rows = jnp.where(lane == q, got[2 * q, SCAP * PIECE :].astype(F32), rows)
+    scales[0] = rows[:SCAP, :4].astype(BF)
 
 
 def place(got):
@@ -371,7 +405,7 @@
         place_body,
         out_shape=[
             jax.ShapeDtypeStruct((1, SCAP, 8 * HALF, BLK), BF),
-            jax.ShapeDtypeStruct((4, 16, BLK), BF),
+            jax.ShapeDtypeStruct((1, SCAP, 4), BF),
         ],
         compiler_params=params(),
         cost_estimate=cost(0, 2 * 16 * MSG * BLK * 2),
@@ -393,50 +427,32 @@
     def send(v, pairs):
         return lax.ppermute(v, ("yh", "yl", "x"), pairs)
 
-    def first(k, half):
-        to_x = (x + k) % 4
-        rows = [2 * ((y + j) % 4) + to_x // 2 for j in (half, half + 2)]
-        return rows, (to_x % 2) * 9
-
-    def last(k, half):
-        to_y = (y + k) % 4
-        tos = [(x + j) % 4 for j in (half, half + 2)]
-        return [2 * to_y + t // 2 for t in tos], (tos[0] % 2) * 9 + 5
-
-    def pieces(part, steps, flip=None):
-        columns = [g0[0] + g1[0] + [g0[1]] for g0, g1 in steps]
-        table = jnp.stack([jnp.stack(c) for c in columns], axis=1)
-        return mm(table.astype(jnp.int32), inputs, cotangent, part, flip)
-
-    def long_start(part, groups, flip, along):
-        fwd, bwd = pieces(part, groups, flip)
+    here = jnp.stack([x, y]).astype(jnp.int32)
+
+    def two(k, half):
+        return [(k, half), (k, half + 2)]
+
+    def pieces(which, steps, flip=None):
+        return mm(here, which, [g0 + g1 for g0, g1 in steps], inputs, cotangent, flip)
+
+    def long_start(which, groups, flip, along):
+        fwd, bwd = pieces(which, groups, flip)
         return send(fwd, along(1)), send(bwd, along(-1))
 
     a_fwd, a_bwd = long_start(
-        FIRST, ((first(2, 0), first(2, 1)), (first(1, 1), first(3, 0))), False, along_x
+        0, ((two(2, 0), two(2, 1)), (two(1, 1), two(3, 0))), False, along_x
     )
     b_fwd, b_bwd = long_start(
-        LAST, ((last(2, 0), last(3, 0)), (last(1, 1), last(2, 1))), True, along_y
-    )
-    rest_a = pieces(FIRST, ((first(0, 0), first(0, 1)), (first(1, 0), first(3, 1))))
-    rest_b = pieces(LAST, ((last(0, 0), last(1, 0)), (last(0, 1), last(3, 1))))
+        1, ((two(2, 0), two(3, 0)), (two(1, 1), two(2, 1))), True, along_y
+    )
+    rest_a = pieces(0, ((two(0, 0), two(0, 1)), (two(1, 0), two(3, 1))))
+    rest_b = pieces(1, ((two(0, 0), two(1, 0)), (two(0, 1), two(3, 1))))
 
     def long_end(rest, out_groups, own_groups, fwd, bwd, along, earlier):
         fwd2, bwd2 = relay(rest, out_groups, fwd, bwd, earlier)
         return long_sum(
             rest, own_groups, send(fwd2, along(1)), send(bwd2, along(-1)), fwd, bwd
         )
-
-    part_a = long_end(rest_a, (2, 3), (0, 1), a_fwd, a_bwd, along_x, rest_b)
-    part_b = long_end(rest_b, (1, 3), (0, 2), b_fwd, b_bwd, along_y, rest_a)
-
-    def short(parts, along):
-        return [parts[0]] + [send(parts[k], along(k)) for k in (2, 1, 3)]
-
-    grad_a, tenth = slice_half(front_body, (WIDE, BLK), *short(part_a, along_y))
-    (grad_b,) = slice_half(back_body, (WIDE,), *short(part_b, along_x), tenth)
-    halo_a = send(grad_a, [(i + 1, i) for i in range(15)])
-    halo_b = send(grad_b, [(i, i + 1) for i in range(15)])
 
     flat = 16 * 18
     ends = jnp.concatenate([slice_start[1:], jnp.full((1,), flat, jnp.int32)])
@@ -445,18 +461,6 @@
     end = jnp.sum(jnp.where(is_me, ends, 0))
     odd = x % 2
     info = jnp.stack([start - (18 * me - 9), end - start, odd]).astype(jnp.int32)
-    state = (master, moment, variance)
-    keep2, send2 = codes(
-        own_body, 2, 2 * HALF + 16, "codes_of_own", info, grad_a, grad_b, *state
-    )
-    got2 = send(send2, [(i, i ^ 1) for i in ranks])
-    keep1, send1, near, far = codes(
-        halo_body, 4, HALF + 16, "codes_of_halo", info, halo_b, halo_a, *state
-    )
-    got1 = send(send1, [(i, i ^ 1) for i in ranks])
-    steps = [(i, -1 if i % 2 == 0 else 1) for i in ranks]
-    near = send(near, [(i, i + d) for i, d in steps if 0 <= i + d < 16])
-    far = send(far, [(i, i + 2 * d) for i, d in steps if 0 <= i + 2 * d < 16])
 
     packed = jnp.arange(COLS, dtype=jnp.int32)
     per_group = COLS // GROUPS
@@ -473,16 +477,46 @@
     spots = jnp.arange(8 * SCAP, dtype=jnp.int32)
     table = jnp.sum(jnp.where(spots[:, None] == spot[None, :], column + 1, 0), axis=1) - 1
     pack_info = jnp.concatenate([odd[None], table]).astype(jnp.int32)
+
+    part_a = long_end(rest_a, (2, 3), (0, 1), a_fwd, a_bwd, along_x,
+        (rest_b,),
+    )
+    part_b = long_end(rest_b, (1, 3), (0, 2), b_fwd, b_bwd, along_y, (rest_a,)
+    )
+
+    def short(parts, along):
+        return [parts[0]] + [send(parts[k], along(k)) for k in (2, 1, 3)]
+
+    front, back, to_pair, to_cross = slices(
+        info, *short(part_a, along_y), *short(part_b, along_x)
+    )
+    pairs = [(i, i ^ 1) for i in ranks]
+    near_by = [(i, i - 1 if i % 2 == 0 else i + 1) for i in ranks if 0 < i < 15]
+    far_off = [
+        (i, i - 2 if i % 2 == 0 else i + 2)
+        for i in ranks
+        if 0 <= (i - 2 if i % 2 == 0 else i + 2) < 16
+    ]
+    inside = send(to_pair, pairs)
+    cross = send(to_cross, near_by)
+
+    state = (master, moment, variance)
+    keep2, send2 = codes(own_body, 2, 2 * HALF + 16, "codes_of_own", info, front, back, *state)
+    got2 = send(send2, pairs)
+    keep1, send1, near, far = codes(
+        halo_body, 4, HALF + 16, "codes_of_halo", info, inside, cross, *state
+    )
+    got1 = send(send1, pairs)
+    near = send(near, near_by)
+    far = send(far, far_off)
+
+    updated = update_state(info, inside, front, back, cross, *state)
+    got1, near, far, *updated = lax.optimization_barrier((got1, near, far, *updated))
     out = pack(pack_info, keep2, got2, keep1, got1, near, far)
-    out, info = lax.optimization_barrier((out, info))
-    new_master, new_moment, new_variance = update_state(
-        info, halo_b, grad_a, grad_b, halo_a, *state
-    )
     got = lax.all_to_all(out, ("z", "core", "yh"), split_axis=0, concat_axis=0, tiled=True)
     got = lax.all_to_all(got, ("yh", "yl", "x"), split_axis=0, concat_axis=0, tiled=True)
-    served_blocks, tails = place(got)
-    served_scales = tails[:, :SCAP, 0].T[None]
-    return new_master, new_moment, new_variance, served_blocks, served_scales
+    served_blocks, served_scales = place(got)
+    return (*updated, served_blocks, served_scales)
 
 
 def solution(mesh):

time: 175 us -> 173 us (0.989)
  blocking collectives: 29.8 us -> 50.9 us
  waiting for transfers between devices: 42.2 us -> 28.1 us
  local copies, waits for them, and re-layouts: 11.4 us -> 5.23 us
  starting transfers between devices: 38.2 us -> 34.7 us
    all_to_all x0 -> x1, blocking collectives: none -> 23 us  [shards(): lax.all_to_all(got, ('yh', 'yl', 'x'), split_axis=0, concat_axis=0, tiled...]
    all_to_all x1 -> x0, waiting for transfers between devices: 11.6 us -> none  [shards(): lax.all_to_all(got, ('yh', 'yl', 'x'), split_axis=0, concat_axis=0, tiled...]
    all_to_all x1 -> x0, starting transfers between devices: 4.65 us -> none  [shards(): lax.all_to_all(got, ('yh', 'yl', 'x'), split_axis=0, concat_axis=0, tiled...]
    another operation x12 -> x0, local copies, waits for them, and re-layouts: 3.38 us -> none  [pieces(): table = jnp.stack([jnp.stack(c) for c in columns], axis=1)]
    ppermute x20, waiting for transfers between devices: 30.6 us -> 28.1 us  [send(): return lax.ppermute(v, ('yh', 'yl', 'x'), pairs)]
    unnamed x34 -> x29, local copies, waits for them, and re-layouts: 7.29 us -> 5.16 us
    all_to_all x1, blocking collectives: 29.8 us -> 28 us  [shards(): lax.all_to_all(out, ('z', 'core', 'yh'), split_axis=0, concat_axis=0, til...]
    pallas_call x6 -> x5, Pallas kernels: 27.5 us -> 28.8 us  [the longest x4 27 us: mm(): pl.pallas_call(mm_rest_body if flip is None else functools.partial(mm_sen...]
  transfers between devices with their start and end apart: 21 -> 20, of which waited for: 9 -> 8; matrix products, arithmetic and copies ran while one was open for 2% -> 1% of each run, Pallas kernels for 21% -> 22%
where the time goes in v3:
time: 173 us
  blocking collectives  50.9 us (29%)
  Pallas kernels  48.8 us (28%)
  starting transfers between devices  34.7 us (20%)
  waiting for transfers between devices  28.1 us (16%)
  local copies, waits for them, and re-layouts  5.23 us (3%)
  between operations  2.82 us (2%)
  other arithmetic  1.97 us (1%)
    ppermute x20, starting transfers between devices, send(): return lax.ppermute(v, ('yh', 'yl', 'x'), pairs)  34.7 us
    ppermute x20, waiting for transfers between devices, send(): return lax.ppermute(v, ('yh', 'yl', 'x'), pairs)  28.1 us
    all_to_all x1, blocking collectives, shards(): lax.all_to_all(out, ('z', 'core', 'yh'), split_axis=0, concat_axis=0, til...  28 us
    pallas_call x4, Pallas kernels, mm(): pl.pallas_call(mm_rest_body if flip is None else functools.partial(mm_sen...  27 us
    all_to_all x1, blocking collectives, shards(): lax.all_to_all(got, ('yh', 'yl', 'x'), split_axis=0, concat_axis=0, tiled...  23 us
    pallas_call x1, Pallas kernels, update_state(): pl.pallas_call(state_body, grid_spec=pltpu.PrefetchScalarGridSpec(num_sca...  5.63 us
    unnamed x29, local copies, waits for them, and re-layouts  5.16 us
    pallas_call x2, Pallas kernels, relay(): pl.pallas_call(relay_body, grid=(1,), in_specs=[pair_spec(part, g) for g...  4.2 us
  transfers between devices with their start and end apart: 20, of which 8 were waited for; matrix products, arithmetic and copies ran while one was open for 1% of the time, Pallas kernels for 22%

profile of v3, /device:TPU:0, one launch (start us, length us, event | category | flops | bytes accessed | tf_op | source)
XLA Modules:
  0.0 172.5 jit_solution(8980442041945643340)
XLA Ops:
  0.7 0.6 pad_add_fusion.1.spot
  1.3 7.1 %gradient_to_send.2 = (bf16[4,128,1280]{2,1,0:T(8,128)(2,1)}, bf16[4,128,1280]{2,1,0:T(8,128)(2,1)}) custom-call(s32[2]{0:T(128)} %pad_add_fusion.1.spot, bf16[1024,1024]{1,0:T(8,128)(2,1)} %refs_3_.7, bf16[1024,1024]{1,0:T(8,128)(2,1)} %refs_3_.7, bf16[1024,1024]{1,0:T(8,128)(2,1)} %refs_3_.7, bf16[1024,1024]{1,0:T(8,128)(2,1)} %refs_3_.7, ...), custom_call_target="tpu_custom_call" | custom-call | flops 2684354560 | bytes 9961472 | tf_op jit(solution)/shard_map/gradient_to_send/pallas_call | solution.py:96
  8.4 1.6 collective-permute-start
  10.0 1.7 collective-permute-start.1
  11.6 6.3 %gradient_to_send.3 = (bf16[4,128,1024]{2,1,0:T(8,128)(2,1)}, bf16[4,128,1024]{2,1,0:T(8,128)(2,1)}) custom-call(s32[2]{0:T(128)} %pad_add_fusion.1.spot, bf16[1024,1024]{1,0:T(8,128)(2,1)} %refs_3_.7, bf16[1024,1024]{1,0:T(8,128)(2,1)} %refs_3_.7, bf16[1024,1024]{1,0:T(8,128)(2,1)} %refs_3_.7, bf16[1024,1024]{1,0:T(8,128)(2,1)} %refs_3_.7, ...), custom_call_target="tpu_custom_call" | custom-call | flops 2147483648 | bytes 8388608 | tf_op jit(solution)/shard_map/gradient_to_send/pallas_call | solution.py:96
  17.9 1.7 collective-permute-start.7
  19.6 1.6 collective-permute-start.8
  21.1 6.3 %gradient_pieces.3.refs_0_.to_fwd.to_bwd.own_even.own_odd = bf16[8,128,1024]{2,1,0:T(8,128)(2,1)} custom-call(s32[2]{0:T(128)} %pad_add_fusion.1.spot, bf16[1024,1024]{1,0:T(8,128)(2,1)} %refs_3_.7, bf16[1024,1024]{1,0:T(8,128)(2,1)} %refs_3_.7, bf16[1024,1024]{1,0:T(8,128)(2,1)} %refs_3_.7, bf16[1024,1024]{1,0:T(8,128)(2,1)} %refs_3_.7, ...), custom_call_target="tpu_custom_call" | custom-call | flops 2147483648 | bytes 8388608 | tf_op jit(solution)/shard_map/gradient_pieces/pallas_call | solution.py:96
  27.4 7.3 %gradient_pieces.2.to_fwd.to_bwd.own_even.own_odd.refs_0_ = bf16[8,128,1280]{2,1,0:T(8,128)(2,1)} custom-call(s32[2]{0:T(128)} %pad_add_fusion.1.spot, bf16[1024,1024]{1,0:T(8,128)(2,1)} %refs_3_.7, bf16[1024,1024]{1,0:T(8,128)(2,1)} %refs_3_.7, bf16[1024,1024]{1,0:T(8,128)(2,1)} %refs_3_.7, bf16[1024,1024]{1,0:T(8,128)(2,1)} %refs_3_.7, ...), custom_call_target="tpu_custom_call" | custom-call | flops 2684354560 | bytes 9961472 | tf_op jit(solution)/shard_map/gradient_pieces/pallas_call | solution.py:96
  34.8 9.1 %collective-permute-done.7.fwd = bf16[4,128,1024]{2,1,0:T(8,128)(2,1)} collective-permute-done((bf16[4,128,1024]{2,1,0:T(8,128)(2,1)}, bf16[4,128,1024]{2,1,0:T(8,128)(2,1)}, u32[]{:S(2)}, u32[]{:S(2)}) %collective-permute-start.7) | collective-permute-done | bytes 1048608 | tf_op jit(solution)/shard_map/ppermute | solution.py:428
  43.9 0.0 collective-permute-done.8.bwd
  43.9 1.7 %copy-done = bf16[8,128,1280]{2,1,0:T(8,128)(2,1)S(1)} copy-done((bf16[8,128,1280]{2,1,0:T(8,128)(2,1)S(1)}, bf16[8,128,1280]{2,1,0:T(8,128)(2,1)}, u32[]{:S(2)}) %copy-start) | copy-done | bytes 2621464
  45.7 1.4 relay_sums.3
  47.1 1.7 collective-permute-start.9
  48.8 1.6 collective-permute-start.10
  50.4 2.8 %relay_sums.2 = (bf16[2,128,1280]{2,1,0:T(8,128)(2,1)}, bf16[2,128,1280]{2,1,0:T(8,128)(2,1)}) custom-call(bf16[8,128,1280]{2,1,0:T(8,128)(2,1)S(1)} %copy-done, bf16[8,128,1280]{2,1,0:T(8,128)(2,1)S(1)} %copy-done, bf16[4,128,1280]{2,1,0:T(8,128)(2,1)S(1)} %collective-permute-done.fwd, bf16[4,128,1280]{2,1,0:T(8,128)(2,1)} %collective-permute-done.1.bwd, ...), custom_call_target="tpu_custom_call" | custom-call | flops 655360 | bytes 3932160 | tf_op jit(solution)/shard_map/relay_sums/pallas_call | solution.py:130
  53.2 0.3 collective-permute-start.2
  53.5 2.9 %collective-permute-start.3 = (bf16[2,128,1280]{2,1,0:T(8,128)(2,1)}, bf16[2,128,1280]{2,1,0:T(8,128)(2,1)}, u32[]{:S(2)}, u32[]{:S(2)}) collective-permute-start(bf16[2,128,1280]{2,1,0:T(8,128)(2,1)} %get-tuple-element.45), channel_id=1, source_target_pairs={{0,24},{8,0},{16,8},{24,16},{32,56},{40,32},{48,40},{56,48},{64,88... | collective-permute-start | bytes 1966088 | tf_op jit(solution)/shard_map/ppermute | solution.py:428
  56.4 4.2 %collective-permute-done.9.fwd2 = bf16[2,128,1024]{2,1,0:T(8,128)(2,1)S(1)} collective-permute-done((bf16[2,128,1024]{2,1,0:T(8,128)(2,1)S(1)}, bf16[2,128,1024]{2,1,0:T(8,128)(2,1)S(1)}, u32[]{:S(2)}, u32[]{:S(2)}) %collective-permute-start.9) | collective-permute-done | bytes 524320 | tf_op jit(solution)/shard_map/ppermute | solution.py:428
  60.7 0.0 collective-permute-done.10.bwd2
  60.7 2.1 %long_sums.3 = (bf16[128,1024]{1,0:T(8,128)(2,1)S(1)}, bf16[128,1024]{1,0:T(8,128)(2,1)S(1)}, bf16[128,1024]{1,0:T(8,128)(2,1)}, bf16[128,1024]{1,0:T(8,128)(2,1)S(1)}) custom-call(bf16[8,128,1024]{2,1,0:T(8,128)(2,1)S(1)} %copy-done.3, bf16[8,128,1024]{2,1,0:T(8,128)(2,1)S(1)} %copy-done.3, bf16[2,128,1024]{2,1,0:T(8,128)(2,1)S(1)} %collective-permute-done.9.fwd2, ...), custom_call_target="tpu_custom_call" | custom-call | flops 1048576 | bytes 4194304 | tf_op jit(solution)/shard_map/long_sums/pallas_call | solution.py:152
  62.8 0.7 copy-done.9
  63.5 0.7 copy-done.10
  64.2 1.7 %collective-permute-start.11 = (bf16[128,1024]{1,0:T(8,128)(2,1)}, bf16[128,1024]{1,0:T(8,128)(2,1)}, u32[]{:S(2)}, u32[]{:S(2)}) collective-permute-start(bf16[128,1024]{1,0:T(8,128)(2,1)} %get-tuple-element.55), channel_id=1, source_target_pairs={{0,16},{8,24},{16,0},{24,8},{32,48},{40,56},{48,32},{56,40},{64,80... | collective-permute-start | bytes 786440 | tf_op jit(solution)/shard_map/ppermute | solution.py:428
  65.9 0.1 slice.3
  66.0 0.8 fusion.1
  68.8 0.6 collective-permute-start.12
  69.5 2.7 %collective-permute-start.13 = (bf16[128,1024]{1,0:T(8,128)(2,1)}, bf16[128,1024]{1,0:T(8,128)(2,1)S(1)}, u32[]{:S(2)}, u32[]{:S(2)}) collective-permute-start(bf16[128,1024]{1,0:T(8,128)(2,1)} %copy-done.9), channel_id=1, source_target_pairs={{0,24},{8,0},{16,8},{24,16},{32,56},{40,32},{48,40},{56,48},{64,88... | collective-permute-start | bytes 786440 | tf_op jit(solution)/shard_map/ppermute | solution.py:428
  72.1 2.3 %collective-permute-done.2.fwd2 = bf16[2,128,1280]{2,1,0:T(8,128)(2,1)S(1)} collective-permute-done((bf16[2,128,1280]{2,1,0:T(8,128)(2,1)}, bf16[2,128,1280]{2,1,0:T(8,128)(2,1)S(1)}, u32[]{:S(2)}, u32[]{:S(2)}) %collective-permute-start.2) | collective-permute-done | bytes 655392 | tf_op jit(solution)/shard_map/ppermute | solution.py:428
  74.4 1.0 collective-permute-done.3.bwd2
  75.4 1.3 copy-done.8
  76.7 1.9 %long_sums.2 = (bf16[128,1280]{1,0:T(8,128)(2,1)S(1)}, bf16[128,1280]{1,0:T(8,128)(2,1)S(1)}, bf16[128,1280]{1,0:T(8,128)(2,1)S(1)}, bf16[128,1280]{1,0:T(8,128)(2,1)S(1)}) custom-call(bf16[8,128,1280]{2,1,0:T(8,128)(2,1)S(1)} %copy-done.1, bf16[8,128,1280]{2,1,0:T(8,128)(2,1)S(1)} %copy-done.1, bf16[2,128,1280]{2,1,0:T(8,128)(2,1)S(1)} %collective-permute-done.2.fwd2, ...), custom_call_target="tpu_custom_call" | custom-call | flops 1310720 | bytes 5242880 | tf_op jit(solution)/shard_map/long_sums/pallas_call | solution.py:152
  78.6 0.0 copy-start.4
  78.7 1.3 collective-permute-start.4
  79.9 1.1 collective-permute-start.5
  81.1 0.0 collective-permute-done.11.refs_5_
  81.1 2.1 %collective-permute-start.6 = (bf16[128,1280]{1,0:T(8,128)(2,1)S(1)}, bf16[128,1280]{1,0:T(8,128)(2,1)S(1)}, u32[]{:S(2)}, u32[]{:S(2)}) collective-permute-start(bf16[128,1280]{1,0:T(8,128)(2,1)S(1)} %get-tuple-element.49), channel_id=1, source_target_pairs={{0,96},{8,104},{16,112},{24,120},{32,0},{40,8},{48,16},{56,24},{64... | collective-permute-start | bytes 983048 | tf_op jit(solution)/shard_map/ppermute | solution.py:428
  83.2 0.1 pad_add_fusion.info
  83.3 0.2 convert_reduce_fusion
  83.5 0.1 select_reduce_fusion.1
  83.5 0.0 collective-permute-done.12.refs_6_
  83.6 3.9 %collective-permute-done.4.refs_1_ = bf16[128,1280]{1,0:T(8,128)(2,1)S(1)} collective-permute-done((bf16[128,1280]{1,0:T(8,128)(2,1)S(1)}, bf16[128,1280]{1,0:T(8,128)(2,1)S(1)}, u32[]{:S(2)}, u32[]{:S(2)}) %collective-permute-start.4) | collective-permute-done | bytes 327712 | tf_op jit(solution)/shard_map/ppermute | solution.py:428
  87.4 3.4 %collective-permute-done.5.refs_2_ = bf16[128,1280]{1,0:T(8,128)(2,1)S(1)} collective-permute-done((bf16[128,1280]{1,0:T(8,128)(2,1)S(1)}, bf16[128,1280]{1,0:T(8,128)(2,1)S(1)}, u32[]{:S(2)}, u32[]{:S(2)}) %collective-permute-start.5) | collective-permute-done | bytes 327712 | tf_op jit(solution)/shard_map/ppermute | solution.py:428
  90.8 1.8 %slices.1 = (bf16[128,1152]{1,0:T(8,128)(2,1)S(1)}, bf16[128,1152]{1,0:T(8,128)(2,1)S(1)}, bf16[128,1152]{1,0:T(8,128)(2,1)S(1)}, bf16[128,1152]{1,0:T(8,128)(2,1)S(1)}) custom-call(s32[3]{0:T(128)S(1)} %pad_add_fusion.info, bf16[128,1280]{1,0:T(8,128)(2,1)S(1)} %get-tuple-element.46.refs_0_, bf16[128,1280]{1,0:T(8,128)(2,1)S(1)} %collective-permute-done.4.refs_1_, ...), custom_call_target="tpu_custom_call" | custom-call | flops 1179648 | bytes 3538944 | tf_op jit(solution)/shard_map/slices/pallas_call | solution.py:184
  92.7 0.1 collective-permute-start.14
  92.8 0.7 collective-permute-start.15
  93.5 0.1 select_reduce_fusion
  93.6 1.9 %codes_of_own.1 = (bf16[144,1152]{1,0:T(8,128)(2,1)S(1)}, bf16[144,1152]{1,0:T(8,128)(2,1)S(1)}) custom-call(s32[3]{0:T(128)S(1)} %pad_add_fusion.info, bf16[128,1152]{1,0:T(8,128)(2,1)S(1)} %get-tuple-element.63.front.a, bf16[128,1152]{1,0:T(8,128)(2,1)S(1)} %get-tuple-element.64.back.b, f32[1,36,128,128]{3,2,1,0:T(8,128)S(1)} %copy-done.4, ...), custom_call_target="tpu_custom_call" | custom-call | flops 8847360 | bytes 7077888 | tf_op jit(solution)/shard_map/codes_of_own/pallas_call | solution.py:266
  95.4 7.0 %collective-permute-start.19 = (bf16[144,1152]{1,0:T(8,128)(2,1)S(1)}, bf16[144,1152]{1,0:T(8,128)(2,1)S(1)}, u32[]{:S(2)}, u32[]{:S(2)}) collective-permute-start(bf16[144,1152]{1,0:T(8,128)(2,1)S(1)} %get-tuple-element.72), channel_id=1, source_target_pairs={{0,8},{8,0},{16,24},{24,16},{32,40},{40,32},{48,56},{56,48},{64,72... | collective-permute-start | bytes 995336 | tf_op jit(solution)/shard_map/ppermute | solution.py:428
  102.4 0.3 collective-permute-done.14.inside
  102.7 0.0 collective-permute-done.15.cross
  102.7 1.9 %codes_of_halo.1 = (bf16[80,1152]{1,0:T(8,128)(2,1)S(1)}, bf16[80,1152]{1,0:T(8,128)(2,1)S(1)}, bf16[80,1152]{1,0:T(8,128)(2,1)S(1)}, bf16[80,1152]{1,0:T(8,128)(2,1)S(1)}) custom-call(s32[3]{0:T(128)S(1)} %pad_add_fusion.info, bf16[128,1152]{1,0:T(8,128)(2,1)S(1)} %collective-permute-done.14.inside, bf16[128,1152]{1,0:T(8,128)(2,1)S(1)} %collective-permute-done.15.cross, ...), custom_call_target="tpu_custom_call" | custom-call | flops 8847360 | bytes 7077888 | tf_op jit(solution)/shard_map/codes_of_halo/pallas_call | solution.py:266
  104.6 2.4 %collective-permute-start.16 = (bf16[80,1152]{1,0:T(8,128)(2,1)S(1)}, bf16[80,1152]{1,0:T(8,128)(2,1)S(1)}, u32[]{:S(2)}, u32[]{:S(2)}) collective-permute-start(bf16[80,1152]{1,0:T(8,128)(2,1)S(1)} %get-tuple-element.60), channel_id=1, source_target_pairs={{0,8},{8,0},{16,24},{24,16},{32,40},{40,32},{48,56},{56,48},{64,72... | collective-permute-start | bytes 552968 | tf_op jit(solution)/shard_map/ppermute | solution.py:428
  107.0 0.7 collective-permute-start.17
  107.7 1.3 collective-permute-start.18
  109.0 0.1 pad_add_fusion.2.info
  109.0 5.6 %update_state.1 = (f32[1,36,128,128]{3,2,1,0:T(8,128)}, f32[1,36,128,128]{3,2,1,0:T(8,128)}, f32[1,36,128,128]{3,2,1,0:T(8,128)}) custom-call(s32[3]{0:T(128)S(1)} %pad_add_fusion.info, bf16[128,1152]{1,0:T(8,128)(2,1)S(1)} %collective-permute-done.14.inside, bf16[128,1152]{1,0:T(8,128)(2,1)S(1)} %get-tuple-element.63.front.a, ...), custom_call_target="tpu_custom_call" | custom-call | flops 11796480 | bytes 15335424 | tf_op jit(solution)/shard_map/update_state/pallas_call | solution.py:311
  114.7 0.0 collective-permute-done.16.got1
  114.7 3.8 %collective-permute-done.18.far = bf16[80,1152]{1,0:T(8,128)(2,1)S(1)} collective-permute-done((bf16[80,1152]{1,0:T(8,128)(2,1)S(1)}, bf16[80,1152]{1,0:T(8,128)(2,1)S(1)}, u32[]{:S(2)}, u32[]{:S(2)}) %collective-permute-start.18) | collective-permute-done | bytes 184352 | tf_op jit(solution)/shard_map/ppermute | solution.py:428
  118.5 1.3 pack_by_owner.1
  119.8 28.0 %all_to_all.10 = bf16[16,304,128]{2,1,0:T(8,128)(2,1)S(1)} all-to-all(bf16[16,304,128]{2,1,0:T(8,128)(2,1)S(1)} %pack_by_owner.1), channel_id=1, replica_groups=mesh['yh'=2,'yl'=2,'x'=4,'z'=4,'core'=2] {'z','core','yh'}, dimensions={0} | all-to-all | bytes 2490368 | tf_op jit(solution)/shard_map/all_to_all | solution.py:516
  147.8 23.0 %all_to_all.11.got = bf16[16,304,128]{2,1,0:T(8,128)(2,1)S(1)} all-to-all(bf16[16,304,128]{2,1,0:T(8,128)(2,1)S(1)} %all_to_all.10), channel_id=1, replica_groups=mesh['yh'=2,'yl'=2,'x'=4,'z'=4,'core'=2] {'yh','yl','x'}, dimensions={0} | all-to-all | bytes 2490368 | tf_op jit(solution)/shard_map/all_to_all | solution.py:517
  170.8 1.1 place_served.1
  171.9 0.7 copy.14
  (32 shorter events, 0.1 us)
Async XLA Ops:
  8.4 42.0 %collective-permute-start = (bf16[4,128,1280]{2,1,0:T(8,128)(2,1)}, bf16[4,128,1280]{2,1,0:T(8,128)(2,1)S(1)}, u32[]{:S(2)}, u32[]{:S(2)}) collective-permute-start(bf16[4,128,1280]{2,1,0:T(8,128)(2,1)} %get-tuple-element.42), channel_id=1, source_target_pairs={{0,8},{8,16},{16,24},{24,0},{32,40},{40,48},{48,56},{56,32},{64,72... | collective-permute-start | bytes 3932168 | tf_op jit(solution)/shard_map/ppermute | solution.py:428
  10.0 40.5 %collective-permute-start.1 = (bf16[4,128,1280]{2,1,0:T(8,128)(2,1)}, bf16[4,128,1280]{2,1,0:T(8,128)(2,1)}, u32[]{:S(2)}, u32[]{:S(2)}) collective-permute-start(bf16[4,128,1280]{2,1,0:T(8,128)(2,1)} %get-tuple-element.43), channel_id=1, source_target_pairs={{0,24},{8,0},{16,8},{24,16},{32,56},{40,32},{48,40},{56,48},{64,88... | collective-permute-start | bytes 3932168 | tf_op jit(solution)/shard_map/ppermute | solution.py:428
  17.9 26.0 %collective-permute-start.7 = (bf16[4,128,1024]{2,1,0:T(8,128)(2,1)}, bf16[4,128,1024]{2,1,0:T(8,128)(2,1)}, u32[]{:S(2)}, u32[]{:S(2)}) collective-permute-start(bf16[4,128,1024]{2,1,0:T(8,128)(2,1)} %get-tuple-element.50), channel_id=1, source_target_pairs={{0,32},{8,40},{16,48},{24,56},{32,64},{40,72},{48,80},{56,88},{64,... | collective-permute-start | bytes 3145736 | tf_op jit(solution)/shard_map/ppermute | solution.py:428
  19.6 24.4 %collective-permute-start.8 = (bf16[4,128,1024]{2,1,0:T(8,128)(2,1)}, bf16[4,128,1024]{2,1,0:T(8,128)(2,1)}, u32[]{:S(2)}, u32[]{:S(2)}) collective-permute-start(bf16[4,128,1024]{2,1,0:T(8,128)(2,1)} %get-tuple-element.51), channel_id=1, source_target_pairs={{0,96},{8,104},{16,112},{24,120},{32,0},{40,8},{48,16},{56,24},{64... | collective-permute-start | bytes 3145736 | tf_op jit(solution)/shard_map/ppermute | solution.py:428
  27.4 16.5 %copy-start.2 = (bf16[8,128,1024]{2,1,0:T(8,128)(2,1)S(1)}, bf16[8,128,1024]{2,1,0:T(8,128)(2,1)}, u32[]{:S(2)}) copy-start(bf16[8,128,1024]{2,1,0:T(8,128)(2,1)} %gradient_pieces.3.refs_0_.to_fwd.to_bwd.own_even.own_odd) | copy-start | bytes 6291460
  43.9 1.7 %copy-start = (bf16[8,128,1280]{2,1,0:T(8,128)(2,1)S(1)}, bf16[8,128,1280]{2,1,0:T(8,128)(2,1)}, u32[]{:S(2)}) copy-start(bf16[8,128,1280]{2,1,0:T(8,128)(2,1)} %gradient_pieces.2.to_fwd.to_bwd.own_even.own_odd.refs_0_) | copy-start | bytes 7864324
  47.1 13.6 %collective-permute-start.9 = (bf16[2,128,1024]{2,1,0:T(8,128)(2,1)S(1)}, bf16[2,128,1024]{2,1,0:T(8,128)(2,1)S(1)}, u32[]{:S(2)}, u32[]{:S(2)}) collective-permute-start(bf16[2,128,1024]{2,1,0:T(8,128)(2,1)S(1)} %get-tuple-element.52), channel_id=1, source_target_pairs={{0,32},{8,40},{16,48},{24,56},{32,64},{40,72},{48,80},{56,88},{64,... | collective-permute-start | bytes 1572872 | tf_op jit(solution)/shard_map/ppermute | solution.py:428
  48.8 11.9 %copy-start.3 = (bf16[8,128,1024]{2,1,0:T(8,128)(2,1)S(1)}, bf16[8,128,1024]{2,1,0:T(8,128)(2,1)}, u32[]{:S(2)}) copy-start(bf16[8,128,1024]{2,1,0:T(8,128)(2,1)} %gradient_pieces.3.refs_0_.to_fwd.to_bwd.own_even.own_odd) | copy-start | bytes 6291460
  48.8 11.9 %collective-permute-start.10 = (bf16[2,128,1024]{2,1,0:T(8,128)(2,1)S(1)}, bf16[2,128,1024]{2,1,0:T(8,128)(2,1)S(1)}, u32[]{:S(2)}, u32[]{:S(2)}) collective-permute-start(bf16[2,128,1024]{2,1,0:T(8,128)(2,1)S(1)} %get-tuple-element.53), channel_id=1, source_target_pairs={{0,96},{8,104},{16,112},{24,120},{32,0},{40,8},{48,16},{56,24},{64... | collective-permute-start | bytes 1572872 | tf_op jit(solution)/shard_map/ppermute | solution.py:428
  50.4 2.8 %copy-start.7 = (bf16[4,128,1280]{2,1,0:T(8,128)(2,1)}, bf16[4,128,1280]{2,1,0:T(8,128)(2,1)S(1)}, u32[]{:S(2)}) copy-start(bf16[4,128,1280]{2,1,0:T(8,128)(2,1)S(1)} %collective-permute-done.fwd) | copy-start | bytes 3932164
  53.2 21.2 %collective-permute-start.2 = (bf16[2,128,1280]{2,1,0:T(8,128)(2,1)}, bf16[2,128,1280]{2,1,0:T(8,128)(2,1)S(1)}, u32[]{:S(2)}, u32[]{:S(2)}) collective-permute-start(bf16[2,128,1280]{2,1,0:T(8,128)(2,1)} %get-tuple-element.44), channel_id=1, source_target_pairs={{0,8},{8,16},{16,24},{24,0},{32,40},{40,48},{48,56},{56,32},{64,72... | collective-permute-start | bytes 1966088 | tf_op jit(solution)/shard_map/ppermute | solution.py:428
  53.5 12.4 %copy-start.12 = (s32[16]{0:T(128)S(1)}, s32[16]{0:T(128)}, u32[]{:S(2)}) copy-start(s32[16]{0:T(128)} %param.13) | copy-start | bytes 196
  53.5 21.9 %copy-start.1 = (bf16[8,128,1280]{2,1,0:T(8,128)(2,1)S(1)}, bf16[8,128,1280]{2,1,0:T(8,128)(2,1)}, u32[]{:S(2)}) copy-start(bf16[8,128,1280]{2,1,0:T(8,128)(2,1)} %gradient_pieces.2.to_fwd.to_bwd.own_even.own_odd.refs_0_) | copy-start | bytes 7864324
  53.5 21.9 %collective-permute-start.3 = (bf16[2,128,1280]{2,1,0:T(8,128)(2,1)}, bf16[2,128,1280]{2,1,0:T(8,128)(2,1)}, u32[]{:S(2)}, u32[]{:S(2)}) collective-permute-start(bf16[2,128,1280]{2,1,0:T(8,128)(2,1)} %get-tuple-element.45), channel_id=1, source_target_pairs={{0,24},{8,0},{16,8},{24,16},{32,56},{40,32},{48,40},{56,48},{64,88... | collective-permute-start | bytes 1966088 | tf_op jit(solution)/shard_map/ppermute | solution.py:428
  62.8 0.7 copy-start.9
  63.5 0.7 copy-start.10
  64.2 16.9 %collective-permute-start.11 = (bf16[128,1024]{1,0:T(8,128)(2,1)}, bf16[128,1024]{1,0:T(8,128)(2,1)}, u32[]{:S(2)}, u32[]{:S(2)}) collective-permute-start(bf16[128,1024]{1,0:T(8,128)(2,1)} %get-tuple-element.55), channel_id=1, source_target_pairs={{0,16},{8,24},{16,0},{24,8},{32,48},{40,56},{48,32},{56,40},{64,80... | collective-permute-start | bytes 786440 | tf_op jit(solution)/shard_map/ppermute | solution.py:428
  68.8 14.7 %collective-permute-start.12 = (bf16[128,1024]{1,0:T(8,128)(2,1)}, bf16[128,1024]{1,0:T(8,128)(2,1)S(1)}, u32[]{:S(2)}, u32[]{:S(2)}) collective-permute-start(bf16[128,1024]{1,0:T(8,128)(2,1)} %copy-done.10), channel_id=1, source_target_pairs={{0,8},{8,16},{16,24},{24,0},{32,40},{40,48},{48,56},{56,32},{64,72... | collective-permute-start | bytes 786440 | tf_op jit(solution)/shard_map/ppermute | solution.py:428
  69.4 13.8 %copy-start.11 = (s32[36]{0:T(128)S(1)}, s32[36]{0:T(128)}, u32[]{:S(2)}) copy-start(s32[36]{0:T(128)} %param.14) | copy-start | bytes 436
  69.5 14.0 %copy-start.13 = (s32[32]{0:T(128)S(1)}, s32[32]{0:T(128)}, u32[]{:S(2)}) copy-start(s32[32]{0:T(128)} %param.15) | copy-start | bytes 388
  69.5 14.1 %collective-permute-start.13 = (bf16[128,1024]{1,0:T(8,128)(2,1)}, bf16[128,1024]{1,0:T(8,128)(2,1)S(1)}, u32[]{:S(2)}, u32[]{:S(2)}) collective-permute-start(bf16[128,1024]{1,0:T(8,128)(2,1)} %copy-done.9), channel_id=1, source_target_pairs={{0,24},{8,0},{16,8},{24,16},{32,56},{40,32},{48,40},{56,48},{64,88... | collective-permute-start | bytes 786440 | tf_op jit(solution)/shard_map/ppermute | solution.py:428
  75.4 1.3 copy-start.8
  76.7 16.9 %copy-start.5 = (f32[1,36,128,128]{3,2,1,0:T(8,128)S(1)}, f32[1,36,128,128]{3,2,1,0:T(8,128)}, u32[]{:S(2)}) copy-start(f32[1,36,128,128]{3,2,1,0:T(8,128)} %moment.5) | copy-start | bytes 7077892
  76.7 16.9 %copy-start.6 = (f32[1,36,128,128]{3,2,1,0:T(8,128)S(1)}, f32[1,36,128,128]{3,2,1,0:T(8,128)}, u32[]{:S(2)}) copy-start(f32[1,36,128,128]{3,2,1,0:T(8,128)} %variance.5) | copy-start | bytes 7077892
  78.6 14.9 %copy-start.4 = (f32[1,36,128,128]{3,2,1,0:T(8,128)S(1)}, f32[1,36,128,128]{3,2,1,0:T(8,128)}, u32[]{:S(2)}) copy-start(f32[1,36,128,128]{3,2,1,0:T(8,128)} %master.5) | copy-start | bytes 7077892
  78.7 8.8 %collective-permute-start.4 = (bf16[128,1280]{1,0:T(8,128)(2,1)S(1)}, bf16[128,1280]{1,0:T(8,128)(2,1)S(1)}, u32[]{:S(2)}, u32[]{:S(2)}) collective-permute-start(bf16[128,1280]{1,0:T(8,128)(2,1)S(1)} %get-tuple-element.47), channel_id=1, source_target_pairs={{0,64},{8,72},{16,80},{24,88},{32,96},{40,104},{48,112},{56,120},{... | collective-permute-start | bytes 983048 | tf_op jit(solution)/shard_map/ppermute | solution.py:428
  79.9 10.9 %collective-permute-start.5 = (bf16[128,1280]{1,0:T(8,128)(2,1)S(1)}, bf16[128,1280]{1,0:T(8,128)(2,1)S(1)}, u32[]{:S(2)}, u32[]{:S(2)}) collective-permute-start(bf16[128,1280]{1,0:T(8,128)(2,1)S(1)} %get-tuple-element.48), channel_id=1, source_target_pairs={{0,32},{8,40},{16,48},{24,56},{32,64},{40,72},{48,80},{56,88},{64,... | collective-permute-start | bytes 983048 | tf_op jit(solution)/shard_map/ppermute | solution.py:428
  81.1 9.7 %collective-permute-start.6 = (bf16[128,1280]{1,0:T(8,128)(2,1)S(1)}, bf16[128,1280]{1,0:T(8,128)(2,1)S(1)}, u32[]{:S(2)}, u32[]{:S(2)}) collective-permute-start(bf16[128,1280]{1,0:T(8,128)(2,1)S(1)} %get-tuple-element.49), channel_id=1, source_target_pairs={{0,96},{8,104},{16,112},{24,120},{32,0},{40,8},{48,16},{56,24},{64... | collective-permute-start | bytes 983048 | tf_op jit(solution)/shard_map/ppermute | solution.py:428
  92.7 10.0 %collective-permute-start.14 = (bf16[128,1152]{1,0:T(8,128)(2,1)S(1)}, bf16[128,1152]{1,0:T(8,128)(2,1)S(1)}, u32[]{:S(2)}, u32[]{:S(2)}) collective-permute-start(bf16[128,1152]{1,0:T(8,128)(2,1)S(1)} %get-tuple-element.58), channel_id=1, source_target_pairs={{0,8},{8,0},{16,24},{24,16},{32,40},{40,32},{48,56},{56,48},{64,72... | collective-permute-start | bytes 884744 | tf_op jit(solution)/shard_map/ppermute | solution.py:428
  92.8 9.9 %collective-permute-start.15 = (bf16[128,1152]{1,0:T(8,128)(2,1)S(1)}, bf16[128,1152]{1,0:T(8,128)(2,1)S(1)}, u32[]{:S(2)}, u32[]{:S(2)}) collective-permute-start(bf16[128,1152]{1,0:T(8,128)(2,1)S(1)} %get-tuple-element.59), channel_id=1, source_target_pairs={{8,16},{16,8},{24,32},{32,24},{40,48},{48,40},{56,64},{64,56},{72,... | collective-permute-start | bytes 884744 | tf_op jit(solution)/shard_map/ppermute | solution.py:428
  95.4 23.1 %collective-permute-start.19 = (bf16[144,1152]{1,0:T(8,128)(2,1)S(1)}, bf16[144,1152]{1,0:T(8,128)(2,1)S(1)}, u32[]{:S(2)}, u32[]{:S(2)}) collective-permute-start(bf16[144,1152]{1,0:T(8,128)(2,1)S(1)} %get-tuple-element.72), channel_id=1, source_target_pairs={{0,8},{8,0},{16,24},{24,16},{32,40},{40,32},{48,56},{56,48},{64,72... | collective-permute-start | bytes 995336 | tf_op jit(solution)/shard_map/ppermute | solution.py:428
  104.6 10.1 %collective-permute-start.16 = (bf16[80,1152]{1,0:T(8,128)(2,1)S(1)}, bf16[80,1152]{1,0:T(8,128)(2,1)S(1)}, u32[]{:S(2)}, u32[]{:S(2)}) collective-permute-start(bf16[80,1152]{1,0:T(8,128)(2,1)S(1)} %get-tuple-element.60), channel_id=1, source_target_pairs={{0,8},{8,0},{16,24},{24,16},{32,40},{40,32},{48,56},{56,48},{64,72... | collective-permute-start | bytes 552968 | tf_op jit(solution)/shard_map/ppermute | solution.py:428
  107.0 7.7 %collective-permute-start.17 = (bf16[80,1152]{1,0:T(8,128)(2,1)S(1)}, bf16[80,1152]{1,0:T(8,128)(2,1)S(1)}, u32[]{:S(2)}, u32[]{:S(2)}) collective-permute-start(bf16[80,1152]{1,0:T(8,128)(2,1)S(1)} %get-tuple-element.61), channel_id=1, source_target_pairs={{8,16},{16,8},{24,32},{32,24},{40,48},{48,40},{56,64},{64,56},{72,... | collective-permute-start | bytes 552968 | tf_op jit(solution)/shard_map/ppermute | solution.py:428
  107.7 10.9 %collective-permute-start.18 = (bf16[80,1152]{1,0:T(8,128)(2,1)S(1)}, bf16[80,1152]{1,0:T(8,128)(2,1)S(1)}, u32[]{:S(2)}, u32[]{:S(2)}) collective-permute-start(bf16[80,1152]{1,0:T(8,128)(2,1)S(1)} %get-tuple-element.62), channel_id=1, source_target_pairs={{8,24},{16,0},{24,40},{32,16},{40,56},{48,32},{56,72},{64,48},{72,... | collective-permute-start | bytes 552968 | tf_op jit(solution)/shard_map/ppermute | solution.py:428

commit v4 on v3

--- a/solution.py
+++ b/solution.py
@@ -20,6 +20,7 @@
 CAP = 36
 COLS = 36
 SCAP = 9
+STEP = 9
 PIECE = 32
 MSG = SCAP * PIECE + 16
 
@@ -155,7 +156,7 @@
         in_specs=[pair_spec(part, g) for g in (groups[0], groups[1], 0, 0, 1, 1)],
         out_specs=[pl.BlockSpec((BLK, part), lambda s: (0, 0))] * 4,
         out_shape=[jax.ShapeDtypeStruct((BLK, part), BF)] * 4,
-        compiler_params=params(),
+        compiler_params=params(48),
         cost_estimate=cost(8 * BLK * part, 16 * BLK * part * 2),
         name="long_sums",
     )(rest, rest, fwd2, bwd2, fwd, bwd)
@@ -297,8 +298,8 @@
         window[3 - 3 * info[2]] = inside[...]
         window[3 * info[2]] = cross[...]
 
-    for n in range(4):
-        slot = step * 4 + n
+    for n in range(STEP):
+        slot = step * STEP + n
         unit, lanes = unit_of(wrap(off + slot))
         grad = jnp.where(slot < length, window[unit, :, lanes].astype(F32), 0.0)
         new_master[0, n], new_moment[0, n], new_variance[0, n] = adam_step(
@@ -307,18 +308,18 @@
 
 
 def update_state(info, inside, front, back, cross, master, moment, variance):
-    state = pl.BlockSpec((1, 4, BLK, BLK), lambda s, t: (0, s, 0, 0))
+    state = pl.BlockSpec((1, STEP, BLK, BLK), lambda s, t: (0, s, 0, 0))
     return pl.pallas_call(
         state_body,
         grid_spec=pltpu.PrefetchScalarGridSpec(
             num_scalar_prefetch=1,
-            grid=(CAP // 4,),
+            grid=(CAP // STEP,),
             in_specs=[pl.BlockSpec((BLK, WIDE), lambda s, t: (0, 0))] * 4 + [state] * 3,
             out_specs=[state] * 3,
             scratch_shapes=[pltpu.VMEM((4, BLK, WIDE), BF)],
         ),
         out_shape=[jax.ShapeDtypeStruct(master.shape, F32)] * 3,
-        compiler_params=params(),
+        compiler_params=params(32),
         cost_estimate=cost(36 * 16384 * 20, 36 * 16384 * 26),
         name="update_state",
     )(info, inside, front, back, cross, master, moment, variance)
@@ -478,11 +479,8 @@
     table = jnp.sum(jnp.where(spots[:, None] == spot[None, :], column + 1, 0), axis=1) - 1
     pack_info = jnp.concatenate([odd[None], table]).astype(jnp.int32)
 
-    part_a = long_end(rest_a, (2, 3), (0, 1), a_fwd, a_bwd, along_x,
-        (rest_b,),
-    )
-    part_b = long_end(rest_b, (1, 3), (0, 2), b_fwd, b_bwd, along_y, (rest_a,)
-    )
+    part_a = long_end(rest_a, (2, 3), (0, 1), a_fwd, a_bwd, along_x, (rest_b,))
+    part_b = long_end(rest_b, (1, 3), (0, 2), b_fwd, b_bwd, along_y, (rest_a,))
 
     def short(parts, along):
         return [parts[0]] + [send(parts[k], along(k)) for k in (2, 1, 3)]

time: 173 us -> 170 us (0.983)
  waiting for transfers between devices: 28.1 us -> 30.7 us
  Pallas kernels: 48.8 us -> 46.4 us
  starting transfers between devices: 34.7 us -> 32.6 us
    ppermute x20, waiting for transfers between devices: 28.1 us -> 30.7 us  [send(): return lax.ppermute(v, ('yh', 'yl', 'x'), pairs)]
    ppermute x20, starting transfers between devices: 34.7 us -> 32.6 us  [send(): return lax.ppermute(v, ('yh', 'yl', 'x'), pairs)]
    unnamed x29 -> x21, local copies, waits for them, and re-layouts: 5.16 us -> 3.83 us
  transfers between devices with their start and end apart: 20 -> 20, of which waited for: 8 -> 8; matrix products, arithmetic and copies ran while one was open for 1% -> 1% of each run, Pallas kernels for 22% -> 21%
where the time goes in v4:
time: 170 us; the launch traced here: 169 us
  blocking collectives  51 us (30%)
  Pallas kernels  46.4 us (27%)
  starting transfers between devices  32.6 us (19%)
  waiting for transfers between devices  30.7 us (18%)
  local copies, waits for them, and re-layouts  3.9 us (2%)
  between operations  2.8 us (2%)
  other arithmetic  1.97 us (1%)
    ppermute x20, starting transfers between devices, send(): return lax.ppermute(v, ('yh', 'yl', 'x'), pairs)  32.6 us
    ppermute x20, waiting for transfers between devices, send(): return lax.ppermute(v, ('yh', 'yl', 'x'), pairs)  30.7 us
    all_to_all x1, blocking collectives, shards(): lax.all_to_all(out, ('z', 'core', 'yh'), split_axis=0, concat_axis=0, til...  28 us
    pallas_call x4, Pallas kernels, mm(): pl.pallas_call(mm_rest_body if flip is None else functools.partial(mm_sen...  27 us
    all_to_all x1, blocking collectives, shards(): lax.all_to_all(got, ('yh', 'yl', 'x'), split_axis=0, concat_axis=0, tiled...  23 us
    pallas_call x2, Pallas kernels, long_sum(): pl.pallas_call(long_sum_body, grid=(1,), in_specs=[pair_spec(part, g) for...  4.41 us
    pallas_call x1, Pallas kernels, update_state(): pl.pallas_call(state_body, grid_spec=pltpu.PrefetchScalarGridSpec(num_sca...  4.27 us
    unnamed x21, local copies, waits for them, and re-layouts  3.83 us
  transfers between devices with their start and end apart: 20, of which 8 were waited for; matrix products, arithmetic and copies ran while one was open for 1% of the time, Pallas kernels for 21%

profile of v4, /device:TPU:0, one launch (start us, length us, event | category | flops | bytes accessed | tf_op | source)
XLA Modules:
  0.0 169.4 jit_solution(16729147715153250071)
XLA Ops:
  0.7 0.6 pad_add_fusion.1.spot
  1.3 7.1 %gradient_to_send.2 = (bf16[4,128,1280]{2,1,0:T(8,128)(2,1)}, bf16[4,128,1280]{2,1,0:T(8,128)(2,1)}) custom-call(s32[2]{0:T(128)} %pad_add_fusion.1.spot, bf16[1024,1024]{1,0:T(8,128)(2,1)} %refs_3_.7, bf16[1024,1024]{1,0:T(8,128)(2,1)} %refs_3_.7, bf16[1024,1024]{1,0:T(8,128)(2,1)} %refs_3_.7, bf16[1024,1024]{1,0:T(8,128)(2,1)} %refs_3_.7, ...), custom_call_target="tpu_custom_call" | custom-call | flops 2684354560 | bytes 9961472 | tf_op jit(solution)/shard_map/gradient_to_send/pallas_call | solution.py:97
  8.4 1.6 collective-permute-start
  10.0 1.7 collective-permute-start.1
  11.6 6.2 %gradient_to_send.3 = (bf16[4,128,1024]{2,1,0:T(8,128)(2,1)}, bf16[4,128,1024]{2,1,0:T(8,128)(2,1)}) custom-call(s32[2]{0:T(128)} %pad_add_fusion.1.spot, bf16[1024,1024]{1,0:T(8,128)(2,1)} %refs_3_.7, bf16[1024,1024]{1,0:T(8,128)(2,1)} %refs_3_.7, bf16[1024,1024]{1,0:T(8,128)(2,1)} %refs_3_.7, bf16[1024,1024]{1,0:T(8,128)(2,1)} %refs_3_.7, ...), custom_call_target="tpu_custom_call" | custom-call | flops 2147483648 | bytes 8388608 | tf_op jit(solution)/shard_map/gradient_to_send/pallas_call | solution.py:97
  17.9 1.7 collective-permute-start.7
  19.6 1.6 collective-permute-start.8
  21.1 6.3 %gradient_pieces.3.refs_0_.to_fwd.to_bwd.own_even.own_odd = bf16[8,128,1024]{2,1,0:T(8,128)(2,1)} custom-call(s32[2]{0:T(128)} %pad_add_fusion.1.spot, bf16[1024,1024]{1,0:T(8,128)(2,1)} %refs_3_.7, bf16[1024,1024]{1,0:T(8,128)(2,1)} %refs_3_.7, bf16[1024,1024]{1,0:T(8,128)(2,1)} %refs_3_.7, bf16[1024,1024]{1,0:T(8,128)(2,1)} %refs_3_.7, ...), custom_call_target="tpu_custom_call" | custom-call | flops 2147483648 | bytes 8388608 | tf_op jit(solution)/shard_map/gradient_pieces/pallas_call | solution.py:97
  27.4 7.3 %gradient_pieces.2.to_fwd.to_bwd.own_even.own_odd.refs_0_ = bf16[8,128,1280]{2,1,0:T(8,128)(2,1)} custom-call(s32[2]{0:T(128)} %pad_add_fusion.1.spot, bf16[1024,1024]{1,0:T(8,128)(2,1)} %refs_3_.7, bf16[1024,1024]{1,0:T(8,128)(2,1)} %refs_3_.7, bf16[1024,1024]{1,0:T(8,128)(2,1)} %refs_3_.7, bf16[1024,1024]{1,0:T(8,128)(2,1)} %refs_3_.7, ...), custom_call_target="tpu_custom_call" | custom-call | flops 2684354560 | bytes 9961472 | tf_op jit(solution)/shard_map/gradient_pieces/pallas_call | solution.py:97
  34.7 9.2 %collective-permute-done.7.fwd = bf16[4,128,1024]{2,1,0:T(8,128)(2,1)} collective-permute-done((bf16[4,128,1024]{2,1,0:T(8,128)(2,1)}, bf16[4,128,1024]{2,1,0:T(8,128)(2,1)}, u32[]{:S(2)}, u32[]{:S(2)}) %collective-permute-start.7) | collective-permute-done | bytes 1048608 | tf_op jit(solution)/shard_map/ppermute | solution.py:429
  43.9 0.0 collective-permute-done.8.bwd
  43.9 1.7 %copy-done = bf16[8,128,1280]{2,1,0:T(8,128)(2,1)S(1)} copy-done((bf16[8,128,1280]{2,1,0:T(8,128)(2,1)S(1)}, bf16[8,128,1280]{2,1,0:T(8,128)(2,1)}, u32[]{:S(2)}) %copy-start) | copy-done | bytes 2621464
  45.7 1.4 relay_sums.3
  47.1 1.7 collective-permute-start.9
  48.8 1.6 collective-permute-start.10
  50.4 0.0 collective-permute-done.fwd
  50.4 2.3 %relay_sums.2 = (bf16[2,128,1280]{2,1,0:T(8,128)(2,1)}, bf16[2,128,1280]{2,1,0:T(8,128)(2,1)}) custom-call(bf16[8,128,1280]{2,1,0:T(8,128)(2,1)S(1)} %copy-done, bf16[8,128,1280]{2,1,0:T(8,128)(2,1)S(1)} %copy-done, bf16[4,128,1280]{2,1,0:T(8,128)(2,1)S(1)} %collective-permute-done.fwd, bf16[4,128,1280]{2,1,0:T(8,128)(2,1)} %collective-permute-done.1.bwd, ...), custom_call_target="tpu_custom_call" | custom-call | flops 655360 | bytes 3932160 | tf_op jit(solution)/shard_map/relay_sums/pallas_call | solution.py:131
  52.7 0.3 collective-permute-start.2
  53.0 2.9 %collective-permute-start.3 = (bf16[2,128,1280]{2,1,0:T(8,128)(2,1)}, bf16[2,128,1280]{2,1,0:T(8,128)(2,1)S(1)}, u32[]{:S(2)}, u32[]{:S(2)}) collective-permute-start(bf16[2,128,1280]{2,1,0:T(8,128)(2,1)} %get-tuple-element.45), channel_id=1, source_target_pairs={{0,24},{8,0},{16,8},{24,16},{32,56},{40,32},{48,40},{56,48},{64,88... | collective-permute-start | bytes 1966088 | tf_op jit(solution)/shard_map/ppermute | solution.py:429
  56.0 4.8 %collective-permute-done.9.fwd2 = bf16[2,128,1024]{2,1,0:T(8,128)(2,1)S(1)} collective-permute-done((bf16[2,128,1024]{2,1,0:T(8,128)(2,1)S(1)}, bf16[2,128,1024]{2,1,0:T(8,128)(2,1)S(1)}, u32[]{:S(2)}, u32[]{:S(2)}) %collective-permute-start.9) | collective-permute-done | bytes 524320 | tf_op jit(solution)/shard_map/ppermute | solution.py:429
  60.7 0.0 collective-permute-done.10.bwd2
  60.7 2.3 %long_sums.3 = (bf16[128,1024]{1,0:T(8,128)(2,1)S(1)}, bf16[128,1024]{1,0:T(8,128)(2,1)S(1)}, bf16[128,1024]{1,0:T(8,128)(2,1)}, bf16[128,1024]{1,0:T(8,128)(2,1)S(1)}) custom-call(bf16[8,128,1024]{2,1,0:T(8,128)(2,1)} %gradient_pieces.3.refs_0_.to_fwd.to_bwd.own_even.own_odd, bf16[8,128,1024]{2,1,0:T(8,128)(2,1)} %gradient_pieces.3.refs_0_.to_fwd.to_bwd.own_even.own_odd, ...), custom_call_target="tpu_custom_call" | custom-call | flops 1048576 | bytes 4194304 | tf_op jit(solution)/shard_map/long_sums/pallas_call | solution.py:153
  63.0 0.7 copy-done.5
  63.7 0.7 copy-done.6
  64.4 1.7 %collective-permute-start.11 = (bf16[128,1024]{1,0:T(8,128)(2,1)}, bf16[128,1024]{1,0:T(8,128)(2,1)S(1)}, u32[]{:S(2)}, u32[]{:S(2)}) collective-permute-start(bf16[128,1024]{1,0:T(8,128)(2,1)} %get-tuple-element.55), channel_id=1, source_target_pairs={{0,16},{8,24},{16,0},{24,8},{32,48},{40,56},{48,32},{56,40},{64,80... | collective-permute-start | bytes 786440 | tf_op jit(solution)/shard_map/ppermute | solution.py:429
  66.2 0.1 slice.3
  66.2 0.8 fusion.1
  69.0 0.6 collective-permute-start.12
  69.7 2.7 %collective-permute-start.13 = (bf16[128,1024]{1,0:T(8,128)(2,1)}, bf16[128,1024]{1,0:T(8,128)(2,1)S(1)}, u32[]{:S(2)}, u32[]{:S(2)}) collective-permute-start(bf16[128,1024]{1,0:T(8,128)(2,1)} %copy-done.5), channel_id=1, source_target_pairs={{0,24},{8,0},{16,8},{24,16},{32,56},{40,32},{48,40},{56,48},{64,88... | collective-permute-start | bytes 786440 | tf_op jit(solution)/shard_map/ppermute | solution.py:429
  72.3 0.9 collective-permute-done.2.fwd2
  73.2 1.6 collective-permute-done.3.bwd2
  74.8 2.1 %long_sums.2 = (bf16[128,1280]{1,0:T(8,128)(2,1)S(1)}, bf16[128,1280]{1,0:T(8,128)(2,1)S(1)}, bf16[128,1280]{1,0:T(8,128)(2,1)S(1)}, bf16[128,1280]{1,0:T(8,128)(2,1)S(1)}) custom-call(bf16[8,128,1280]{2,1,0:T(8,128)(2,1)} %gradient_pieces.2.to_fwd.to_bwd.own_even.own_odd.refs_0_, ...), custom_call_target="tpu_custom_call" | custom-call | flops 1310720 | bytes 5242880 | tf_op jit(solution)/shard_map/long_sums/pallas_call | solution.py:153
  76.9 0.0 copy-start.2
  76.9 0.6 collective-permute-start.4
  77.5 1.3 collective-permute-start.5
  78.8 1.9 %collective-permute-start.6 = (bf16[128,1280]{1,0:T(8,128)(2,1)S(1)}, bf16[128,1280]{1,0:T(8,128)(2,1)S(1)}, u32[]{:S(2)}, u32[]{:S(2)}) collective-permute-start(bf16[128,1280]{1,0:T(8,128)(2,1)S(1)} %get-tuple-element.49), channel_id=1, source_target_pairs={{0,96},{8,104},{16,112},{24,120},{32,0},{40,8},{48,16},{56,24},{64... | collective-permute-start | bytes 983048 | tf_op jit(solution)/shard_map/ppermute | solution.py:429
  80.8 0.1 pad_add_fusion.info
  80.8 0.2 convert_reduce_fusion
  81.0 0.1 select_reduce_fusion.1
  81.1 0.0 collective-permute-done.12.refs_6_
  81.1 4.8 %collective-permute-done.4.refs_1_ = bf16[128,1280]{1,0:T(8,128)(2,1)S(1)} collective-permute-done((bf16[128,1280]{1,0:T(8,128)(2,1)S(1)}, bf16[128,1280]{1,0:T(8,128)(2,1)S(1)}, u32[]{:S(2)}, u32[]{:S(2)}) %collective-permute-start.4) | collective-permute-done | bytes 327712 | tf_op jit(solution)/shard_map/ppermute | solution.py:429
  85.9 3.4 %collective-permute-done.5.refs_2_ = bf16[128,1280]{1,0:T(8,128)(2,1)S(1)} collective-permute-done((bf16[128,1280]{1,0:T(8,128)(2,1)S(1)}, bf16[128,1280]{1,0:T(8,128)(2,1)S(1)}, u32[]{:S(2)}, u32[]{:S(2)}) %collective-permute-start.5) | collective-permute-done | bytes 327712 | tf_op jit(solution)/shard_map/ppermute | solution.py:429
  89.3 0.0 collective-permute-done.6.refs_3_
  89.3 0.9 slices.1
  90.3 0.1 collective-permute-start.14
  90.3 0.7 collective-permute-start.15
  91.1 0.1 select_reduce_fusion
  91.2 1.9 %codes_of_own.1 = (bf16[144,1152]{1,0:T(8,128)(2,1)S(1)}, bf16[144,1152]{1,0:T(8,128)(2,1)S(1)}) custom-call(s32[3]{0:T(128)S(1)} %pad_add_fusion.info, bf16[128,1152]{1,0:T(8,128)(2,1)S(1)} %get-tuple-element.63.front.a, bf16[128,1152]{1,0:T(8,128)(2,1)S(1)} %get-tuple-element.64.back.b, f32[1,36,128,128]{3,2,1,0:T(8,128)S(1)} %copy-done.2, ...), custom_call_target="tpu_custom_call" | custom-call | flops 8847360 | bytes 7077888 | tf_op jit(solution)/shard_map/codes_of_own/pallas_call | solution.py:267
  93.0 6.2 %collective-permute-start.19 = (bf16[144,1152]{1,0:T(8,128)(2,1)S(1)}, bf16[144,1152]{1,0:T(8,128)(2,1)S(1)}, u32[]{:S(2)}, u32[]{:S(2)}) collective-permute-start(bf16[144,1152]{1,0:T(8,128)(2,1)S(1)} %get-tuple-element.72), channel_id=1, source_target_pairs={{0,8},{8,0},{16,24},{24,16},{32,40},{40,32},{48,56},{56,48},{64,72... | collective-permute-start | bytes 995336 | tf_op jit(solution)/shard_map/ppermute | solution.py:429
  99.3 0.9 collective-permute-done.14.inside
  100.2 1.9 %codes_of_halo.1 = (bf16[80,1152]{1,0:T(8,128)(2,1)S(1)}, bf16[80,1152]{1,0:T(8,128)(2,1)S(1)}, bf16[80,1152]{1,0:T(8,128)(2,1)S(1)}, bf16[80,1152]{1,0:T(8,128)(2,1)S(1)}) custom-call(s32[3]{0:T(128)S(1)} %pad_add_fusion.info, bf16[128,1152]{1,0:T(8,128)(2,1)S(1)} %collective-permute-done.14.inside, bf16[128,1152]{1,0:T(8,128)(2,1)S(1)} %collective-permute-done.15.cross, ...), custom_call_target="tpu_custom_call" | custom-call | flops 8847360 | bytes 7077888 | tf_op jit(solution)/shard_map/codes_of_halo/pallas_call | solution.py:267
  102.0 1.8 %collective-permute-start.16 = (bf16[80,1152]{1,0:T(8,128)(2,1)S(1)}, bf16[80,1152]{1,0:T(8,128)(2,1)S(1)}, u32[]{:S(2)}, u32[]{:S(2)}) collective-permute-start(bf16[80,1152]{1,0:T(8,128)(2,1)S(1)} %get-tuple-element.60), channel_id=1, source_target_pairs={{0,8},{8,0},{16,24},{24,16},{32,40},{40,32},{48,56},{56,48},{64,72... | collective-permute-start | bytes 552968 | tf_op jit(solution)/shard_map/ppermute | solution.py:429
  103.8 0.7 collective-permute-start.17
  104.5 1.3 collective-permute-start.18
  105.8 0.1 pad_add_fusion.2.info
  105.9 4.3 %update_state.1 = (f32[1,36,128,128]{3,2,1,0:T(8,128)}, f32[1,36,128,128]{3,2,1,0:T(8,128)}, f32[1,36,128,128]{3,2,1,0:T(8,128)}) custom-call(s32[3]{0:T(128)S(1)} %pad_add_fusion.info, bf16[128,1152]{1,0:T(8,128)(2,1)S(1)} %collective-permute-done.14.inside, bf16[128,1152]{1,0:T(8,128)(2,1)S(1)} %get-tuple-element.63.front.a, ...), custom_call_target="tpu_custom_call" | custom-call | flops 11796480 | bytes 15335424 | tf_op jit(solution)/shard_map/update_state/pallas_call | solution.py:312
  110.2 0.0 collective-permute-done.16.got1
  110.2 0.0 collective-permute-done.17.near
  110.2 5.2 %collective-permute-done.18.far = bf16[80,1152]{1,0:T(8,128)(2,1)S(1)} collective-permute-done((bf16[80,1152]{1,0:T(8,128)(2,1)S(1)}, bf16[80,1152]{1,0:T(8,128)(2,1)S(1)}, u32[]{:S(2)}, u32[]{:S(2)}) %collective-permute-start.18) | collective-permute-done | bytes 184352 | tf_op jit(solution)/shard_map/ppermute | solution.py:429
  115.4 1.3 pack_by_owner.1
  116.7 28.0 %all_to_all.10 = bf16[16,304,128]{2,1,0:T(8,128)(2,1)S(1)} all-to-all(bf16[16,304,128]{2,1,0:T(8,128)(2,1)S(1)} %pack_by_owner.1), channel_id=1, replica_groups=mesh['yh'=2,'yl'=2,'x'=4,'z'=4,'core'=2] {'z','core','yh'}, dimensions={0} | all-to-all | bytes 2490368 | tf_op jit(solution)/shard_map/all_to_all | solution.py:514
  144.7 23.0 %all_to_all.11.got = bf16[16,304,128]{2,1,0:T(8,128)(2,1)S(1)} all-to-all(bf16[16,304,128]{2,1,0:T(8,128)(2,1)S(1)} %all_to_all.10), channel_id=1, replica_groups=mesh['yh'=2,'yl'=2,'x'=4,'z'=4,'core'=2] {'yh','yl','x'}, dimensions={0} | all-to-all | bytes 2490368 | tf_op jit(solution)/shard_map/all_to_all | solution.py:515
  167.7 1.1 place_served.1
  168.8 0.7 copy.14
  (24 shorter events, 0.1 us)
Async XLA Ops:
  8.4 42.0 %collective-permute-start = (bf16[4,128,1280]{2,1,0:T(8,128)(2,1)}, bf16[4,128,1280]{2,1,0:T(8,128)(2,1)S(1)}, u32[]{:S(2)}, u32[]{:S(2)}) collective-permute-start(bf16[4,128,1280]{2,1,0:T(8,128)(2,1)} %get-tuple-element.42), channel_id=1, source_target_pairs={{0,8},{8,16},{16,24},{24,0},{32,40},{40,48},{48,56},{56,32},{64,72... | collective-permute-start | bytes 3932168 | tf_op jit(solution)/shard_map/ppermute | solution.py:429
  10.0 40.4 %collective-permute-start.1 = (bf16[4,128,1280]{2,1,0:T(8,128)(2,1)}, bf16[4,128,1280]{2,1,0:T(8,128)(2,1)}, u32[]{:S(2)}, u32[]{:S(2)}) collective-permute-start(bf16[4,128,1280]{2,1,0:T(8,128)(2,1)} %get-tuple-element.43), channel_id=1, source_target_pairs={{0,24},{8,0},{16,8},{24,16},{32,56},{40,32},{48,40},{56,48},{64,88... | collective-permute-start | bytes 3932168 | tf_op jit(solution)/shard_map/ppermute | solution.py:429
  17.9 26.0 %collective-permute-start.7 = (bf16[4,128,1024]{2,1,0:T(8,128)(2,1)}, bf16[4,128,1024]{2,1,0:T(8,128)(2,1)}, u32[]{:S(2)}, u32[]{:S(2)}) collective-permute-start(bf16[4,128,1024]{2,1,0:T(8,128)(2,1)} %get-tuple-element.50), channel_id=1, source_target_pairs={{0,32},{8,40},{16,48},{24,56},{32,64},{40,72},{48,80},{56,88},{64,... | collective-permute-start | bytes 3145736 | tf_op jit(solution)/shard_map/ppermute | solution.py:429
  19.6 24.4 %collective-permute-start.8 = (bf16[4,128,1024]{2,1,0:T(8,128)(2,1)}, bf16[4,128,1024]{2,1,0:T(8,128)(2,1)}, u32[]{:S(2)}, u32[]{:S(2)}) collective-permute-start(bf16[4,128,1024]{2,1,0:T(8,128)(2,1)} %get-tuple-element.51), channel_id=1, source_target_pairs={{0,96},{8,104},{16,112},{24,120},{32,0},{40,8},{48,16},{56,24},{64... | collective-permute-start | bytes 3145736 | tf_op jit(solution)/shard_map/ppermute | solution.py:429
  27.4 16.5 %copy-start.1 = (bf16[8,128,1024]{2,1,0:T(8,128)(2,1)S(1)}, bf16[8,128,1024]{2,1,0:T(8,128)(2,1)}, u32[]{:S(2)}) copy-start(bf16[8,128,1024]{2,1,0:T(8,128)(2,1)} %gradient_pieces.3.refs_0_.to_fwd.to_bwd.own_even.own_odd) | copy-start | bytes 6291460
  43.9 1.7 %copy-start = (bf16[8,128,1280]{2,1,0:T(8,128)(2,1)S(1)}, bf16[8,128,1280]{2,1,0:T(8,128)(2,1)}, u32[]{:S(2)}) copy-start(bf16[8,128,1280]{2,1,0:T(8,128)(2,1)} %gradient_pieces.2.to_fwd.to_bwd.own_even.own_odd.refs_0_) | copy-start | bytes 7864324
  47.1 13.6 %collective-permute-start.9 = (bf16[2,128,1024]{2,1,0:T(8,128)(2,1)S(1)}, bf16[2,128,1024]{2,1,0:T(8,128)(2,1)S(1)}, u32[]{:S(2)}, u32[]{:S(2)}) collective-permute-start(bf16[2,128,1024]{2,1,0:T(8,128)(2,1)S(1)} %get-tuple-element.52), channel_id=1, source_target_pairs={{0,32},{8,40},{16,48},{24,56},{32,64},{40,72},{48,80},{56,88},{64,... | collective-permute-start | bytes 1572872 | tf_op jit(solution)/shard_map/ppermute | solution.py:429
  48.8 11.9 %collective-permute-start.10 = (bf16[2,128,1024]{2,1,0:T(8,128)(2,1)S(1)}, bf16[2,128,1024]{2,1,0:T(8,128)(2,1)S(1)}, u32[]{:S(2)}, u32[]{:S(2)}) collective-permute-start(bf16[2,128,1024]{2,1,0:T(8,128)(2,1)S(1)} %get-tuple-element.53), channel_id=1, source_target_pairs={{0,96},{8,104},{16,112},{24,120},{32,0},{40,8},{48,16},{56,24},{64... | collective-permute-start | bytes 1572872 | tf_op jit(solution)/shard_map/ppermute | solution.py:429
  52.7 20.5 %collective-permute-start.2 = (bf16[2,128,1280]{2,1,0:T(8,128)(2,1)}, bf16[2,128,1280]{2,1,0:T(8,128)(2,1)S(1)}, u32[]{:S(2)}, u32[]{:S(2)}) collective-permute-start(bf16[2,128,1280]{2,1,0:T(8,128)(2,1)} %get-tuple-element.44), channel_id=1, source_target_pairs={{0,8},{8,16},{16,24},{24,0},{32,40},{40,48},{48,56},{56,32},{64,72... | collective-permute-start | bytes 1966088 | tf_op jit(solution)/shard_map/ppermute | solution.py:429
  53.0 13.1 %copy-start.8 = (s32[16]{0:T(128)S(1)}, s32[16]{0:T(128)}, u32[]{:S(2)}) copy-start(s32[16]{0:T(128)} %param.13) | copy-start | bytes 196
  53.0 21.8 %collective-permute-start.3 = (bf16[2,128,1280]{2,1,0:T(8,128)(2,1)}, bf16[2,128,1280]{2,1,0:T(8,128)(2,1)S(1)}, u32[]{:S(2)}, u32[]{:S(2)}) collective-permute-start(bf16[2,128,1280]{2,1,0:T(8,128)(2,1)} %get-tuple-element.45), channel_id=1, source_target_pairs={{0,24},{8,0},{16,8},{24,16},{32,56},{40,32},{48,40},{56,48},{64,88... | collective-permute-start | bytes 1966088 | tf_op jit(solution)/shard_map/ppermute | solution.py:429
  63.0 0.7 copy-start.5
  63.7 0.7 copy-start.6
  64.4 14.4 %collective-permute-start.11 = (bf16[128,1024]{1,0:T(8,128)(2,1)}, bf16[128,1024]{1,0:T(8,128)(2,1)S(1)}, u32[]{:S(2)}, u32[]{:S(2)}) collective-permute-start(bf16[128,1024]{1,0:T(8,128)(2,1)} %get-tuple-element.55), channel_id=1, source_target_pairs={{0,16},{8,24},{16,0},{24,8},{32,48},{40,56},{48,32},{56,40},{64,80... | collective-permute-start | bytes 786440 | tf_op jit(solution)/shard_map/ppermute | solution.py:429
  69.0 12.1 %collective-permute-start.12 = (bf16[128,1024]{1,0:T(8,128)(2,1)}, bf16[128,1024]{1,0:T(8,128)(2,1)S(1)}, u32[]{:S(2)}, u32[]{:S(2)}) collective-permute-start(bf16[128,1024]{1,0:T(8,128)(2,1)} %copy-done.6), channel_id=1, source_target_pairs={{0,8},{8,16},{16,24},{24,0},{32,40},{40,48},{48,56},{56,32},{64,72... | collective-permute-start | bytes 786440 | tf_op jit(solution)/shard_map/ppermute | solution.py:429
  69.6 11.2 %copy-start.7 = (s32[36]{0:T(128)S(1)}, s32[36]{0:T(128)}, u32[]{:S(2)}) copy-start(s32[36]{0:T(128)} %param.14) | copy-start | bytes 436
  69.7 11.4 %copy-start.9 = (s32[32]{0:T(128)S(1)}, s32[32]{0:T(128)}, u32[]{:S(2)}) copy-start(s32[32]{0:T(128)} %param.15) | copy-start | bytes 388
  69.7 11.5 %collective-permute-start.13 = (bf16[128,1024]{1,0:T(8,128)(2,1)}, bf16[128,1024]{1,0:T(8,128)(2,1)S(1)}, u32[]{:S(2)}, u32[]{:S(2)}) collective-permute-start(bf16[128,1024]{1,0:T(8,128)(2,1)} %copy-done.5), channel_id=1, source_target_pairs={{0,24},{8,0},{16,8},{24,16},{32,56},{40,32},{48,40},{56,48},{64,88... | collective-permute-start | bytes 786440 | tf_op jit(solution)/shard_map/ppermute | solution.py:429
  74.8 16.3 %copy-start.3 = (f32[1,36,128,128]{3,2,1,0:T(8,128)S(1)}, f32[1,36,128,128]{3,2,1,0:T(8,128)}, u32[]{:S(2)}) copy-start(f32[1,36,128,128]{3,2,1,0:T(8,128)} %moment.5) | copy-start | bytes 7077892
  74.8 16.3 %copy-start.4 = (f32[1,36,128,128]{3,2,1,0:T(8,128)S(1)}, f32[1,36,128,128]{3,2,1,0:T(8,128)}, u32[]{:S(2)}) copy-start(f32[1,36,128,128]{3,2,1,0:T(8,128)} %variance.5) | copy-start | bytes 7077892
  76.9 14.2 %copy-start.2 = (f32[1,36,128,128]{3,2,1,0:T(8,128)S(1)}, f32[1,36,128,128]{3,2,1,0:T(8,128)}, u32[]{:S(2)}) copy-start(f32[1,36,128,128]{3,2,1,0:T(8,128)} %master.5) | copy-start | bytes 7077892
  76.9 9.0 %collective-permute-start.4 = (bf16[128,1280]{1,0:T(8,128)(2,1)S(1)}, bf16[128,1280]{1,0:T(8,128)(2,1)S(1)}, u32[]{:S(2)}, u32[]{:S(2)}) collective-permute-start(bf16[128,1280]{1,0:T(8,128)(2,1)S(1)} %get-tuple-element.47), channel_id=1, source_target_pairs={{0,64},{8,72},{16,80},{24,88},{32,96},{40,104},{48,112},{56,120},{... | collective-permute-start | bytes 983048 | tf_op jit(solution)/shard_map/ppermute | solution.py:429
  77.5 11.8 %collective-permute-start.5 = (bf16[128,1280]{1,0:T(8,128)(2,1)S(1)}, bf16[128,1280]{1,0:T(8,128)(2,1)S(1)}, u32[]{:S(2)}, u32[]{:S(2)}) collective-permute-start(bf16[128,1280]{1,0:T(8,128)(2,1)S(1)} %get-tuple-element.48), channel_id=1, source_target_pairs={{0,32},{8,40},{16,48},{24,56},{32,64},{40,72},{48,80},{56,88},{64,... | collective-permute-start | bytes 983048 | tf_op jit(solution)/shard_map/ppermute | solution.py:429
  78.8 10.5 %collective-permute-start.6 = (bf16[128,1280]{1,0:T(8,128)(2,1)S(1)}, bf16[128,1280]{1,0:T(8,128)(2,1)S(1)}, u32[]{:S(2)}, u32[]{:S(2)}) collective-permute-start(bf16[128,1280]{1,0:T(8,128)(2,1)S(1)} %get-tuple-element.49), channel_id=1, source_target_pairs={{0,96},{8,104},{16,112},{24,120},{32,0},{40,8},{48,16},{56,24},{64... | collective-permute-start | bytes 983048 | tf_op jit(solution)/shard_map/ppermute | solution.py:429
  90.3 9.9 %collective-permute-start.14 = (bf16[128,1152]{1,0:T(8,128)(2,1)S(1)}, bf16[128,1152]{1,0:T(8,128)(2,1)S(1)}, u32[]{:S(2)}, u32[]{:S(2)}) collective-permute-start(bf16[128,1152]{1,0:T(8,128)(2,1)S(1)} %get-tuple-element.58), channel_id=1, source_target_pairs={{0,8},{8,0},{16,24},{24,16},{32,40},{40,32},{48,56},{56,48},{64,72... | collective-permute-start | bytes 884744 | tf_op jit(solution)/shard_map/ppermute | solution.py:429
  90.3 9.8 %collective-permute-start.15 = (bf16[128,1152]{1,0:T(8,128)(2,1)S(1)}, bf16[128,1152]{1,0:T(8,128)(2,1)S(1)}, u32[]{:S(2)}, u32[]{:S(2)}) collective-permute-start(bf16[128,1152]{1,0:T(8,128)(2,1)S(1)} %get-tuple-element.59), channel_id=1, source_target_pairs={{8,16},{16,8},{24,32},{32,24},{40,48},{48,40},{56,64},{64,56},{72,... | collective-permute-start | bytes 884744 | tf_op jit(solution)/shard_map/ppermute | solution.py:429
  93.0 22.3 %collective-permute-start.19 = (bf16[144,1152]{1,0:T(8,128)(2,1)S(1)}, bf16[144,1152]{1,0:T(8,128)(2,1)S(1)}, u32[]{:S(2)}, u32[]{:S(2)}) collective-permute-start(bf16[144,1152]{1,0:T(8,128)(2,1)S(1)} %get-tuple-element.72), channel_id=1, source_target_pairs={{0,8},{8,0},{16,24},{24,16},{32,40},{40,32},{48,56},{56,48},{64,72... | collective-permute-start | bytes 995336 | tf_op jit(solution)/shard_map/ppermute | solution.py:429
  102.0 8.1 %collective-permute-start.16 = (bf16[80,1152]{1,0:T(8,128)(2,1)S(1)}, bf16[80,1152]{1,0:T(8,128)(2,1)S(1)}, u32[]{:S(2)}, u32[]{:S(2)}) collective-permute-start(bf16[80,1152]{1,0:T(8,128)(2,1)S(1)} %get-tuple-element.60), channel_id=1, source_target_pairs={{0,8},{8,0},{16,24},{24,16},{32,40},{40,32},{48,56},{56,48},{64,72... | collective-permute-start | bytes 552968 | tf_op jit(solution)/shard_map/ppermute | solution.py:429
  103.8 6.3 %collective-permute-start.17 = (bf16[80,1152]{1,0:T(8,128)(2,1)S(1)}, bf16[80,1152]{1,0:T(8,128)(2,1)S(1)}, u32[]{:S(2)}, u32[]{:S(2)}) collective-permute-start(bf16[80,1152]{1,0:T(8,128)(2,1)S(1)} %get-tuple-element.61), channel_id=1, source_target_pairs={{8,16},{16,8},{24,32},{32,24},{40,48},{48,40},{56,64},{64,56},{72,... | collective-permute-start | bytes 552968 | tf_op jit(solution)/shard_map/ppermute | solution.py:429
  104.5 10.9 %collective-permute-start.18 = (bf16[80,1152]{1,0:T(8,128)(2,1)S(1)}, bf16[80,1152]{1,0:T(8,128)(2,1)S(1)}, u32[]{:S(2)}, u32[]{:S(2)}) collective-permute-start(bf16[80,1152]{1,0:T(8,128)(2,1)S(1)} %get-tuple-element.62), channel_id=1, source_target_pairs={{8,24},{16,0},{24,40},{32,16},{40,56},{48,32},{56,72},{64,48},{72,... | collective-permute-start | bytes 552968 | tf_op jit(solution)/shard_map/ppermute | solution.py:429

commit v5 on v4

--- a/solution.py
+++ b/solution.py
@@ -103,7 +103,7 @@
             out_specs=out_specs,
         ),
         out_shape=out_shape,
-        compiler_params=params(60),
+        compiler_params=params(56 if flip is None else 60),
         cost_estimate=cost(2 * 2 * 512 * part * tok, 2 * (tok * (part + 512) + 512 * part) * 2),
         name="gradient_pieces" if flip is None else "gradient_to_send",
     )(spot, *([inputs] * 4), *([cotangent] * tiles))
@@ -156,7 +156,7 @@
         in_specs=[pair_spec(part, g) for g in (groups[0], groups[1], 0, 0, 1, 1)],
         out_specs=[pl.BlockSpec((BLK, part), lambda s: (0, 0))] * 4,
         out_shape=[jax.ShapeDtypeStruct((BLK, part), BF)] * 4,
-        compiler_params=params(48),
+        compiler_params=params(52),
         cost_estimate=cost(8 * BLK * part, 16 * BLK * part * 2),
         name="long_sums",
     )(rest, rest, fwd2, bwd2, fwd, bwd)

time: 170 us -> 170 us (level)
  Pallas kernels: 46.4 us -> 44.3 us
  local copies, waits for them, and re-layouts: 3.9 us -> 5.61 us
    pallas_call x2, Pallas kernels: 3.73 us -> 1.55 us  [relay(): pl.pallas_call(relay_body, grid=(1,), in_specs=[pair_spec(part, g) for g...]
    unnamed x21 -> x29, local copies, waits for them, and re-layouts: 3.83 us -> 5.54 us
  transfers between devices with their start and end apart: 20 -> 20, of which waited for: 8 -> 9; matrix products, arithmetic and copies ran while one was open for 1% -> 1% of each run, Pallas kernels for 21% -> 20%
where the time goes in v5:
time: 170 us; the launch traced here: 169 us
  blocking collectives  50.7 us (30%)
  Pallas kernels  44.3 us (26%)
  starting transfers between devices  33.1 us (19%)
  waiting for transfers between devices  30.8 us (18%)
  local copies, waits for them, and re-layouts  5.61 us (3%)
  between operations  2.79 us (2%)
  other arithmetic  1.87 us (1%)
    ppermute x20, starting transfers between devices, send(): return lax.ppermute(v, ('yh', 'yl', 'x'), pairs)  33.1 us
    ppermute x20, waiting for transfers between devices, send(): return lax.ppermute(v, ('yh', 'yl', 'x'), pairs)  30.8 us
    all_to_all x1, blocking collectives, shards(): lax.all_to_all(out, ('z', 'core', 'yh'), split_axis=0, concat_axis=0, til...  27.6 us
    pallas_call x4, Pallas kernels, mm(): pl.pallas_call(mm_rest_body if flip is None else functools.partial(mm_sen...  27 us
    all_to_all x1, blocking collectives, shards(): lax.all_to_all(got, ('yh', 'yl', 'x'), split_axis=0, concat_axis=0, tiled...  23.1 us
    unnamed x29, local copies, waits for them, and re-layouts  5.54 us
    pallas_call x2, Pallas kernels, long_sum(): pl.pallas_call(long_sum_body, grid=(1,), in_specs=[pair_spec(part, g) for...  4.54 us
    pallas_call x1, Pallas kernels, update_state(): pl.pallas_call(state_body, grid_spec=pltpu.PrefetchScalarGridSpec(num_sca...  4.27 us
  transfers between devices with their start and end apart: 20, of which 9 were waited for; matrix products, arithmetic and copies ran while one was open for 1% of the time, Pallas kernels for 20%

profile of v5, /device:TPU:0, one launch (start us, length us, event | category | flops | bytes accessed | tf_op | source)
XLA Modules:
  0.0 169.3 jit_solution(15684164373871046134)
XLA Ops:
  0.7 0.6 pad_add_fusion.1.spot
  1.3 7.1 %gradient_to_send.2 = (bf16[4,128,1280]{2,1,0:T(8,128)(2,1)}, bf16[4,128,1280]{2,1,0:T(8,128)(2,1)}) custom-call(s32[2]{0:T(128)} %pad_add_fusion.1.spot, bf16[1024,1024]{1,0:T(8,128)(2,1)} %refs_3_.7, bf16[1024,1024]{1,0:T(8,128)(2,1)} %refs_3_.7, bf16[1024,1024]{1,0:T(8,128)(2,1)} %refs_3_.7, bf16[1024,1024]{1,0:T(8,128)(2,1)} %refs_3_.7, ...), custom_call_target="tpu_custom_call" | custom-call | flops 2684354560 | bytes 9961472 | tf_op jit(solution)/shard_map/gradient_to_send/pallas_call | solution.py:97
  8.4 1.6 collective-permute-start
  10.0 1.7 collective-permute-start.1
  11.6 6.2 %gradient_to_send.3 = (bf16[4,128,1024]{2,1,0:T(8,128)(2,1)}, bf16[4,128,1024]{2,1,0:T(8,128)(2,1)}) custom-call(s32[2]{0:T(128)} %pad_add_fusion.1.spot, bf16[1024,1024]{1,0:T(8,128)(2,1)} %refs_3_.7, bf16[1024,1024]{1,0:T(8,128)(2,1)} %refs_3_.7, bf16[1024,1024]{1,0:T(8,128)(2,1)} %refs_3_.7, bf16[1024,1024]{1,0:T(8,128)(2,1)} %refs_3_.7, ...), custom_call_target="tpu_custom_call" | custom-call | flops 2147483648 | bytes 8388608 | tf_op jit(solution)/shard_map/gradient_to_send/pallas_call | solution.py:97
  17.9 1.7 collective-permute-start.7
  19.5 1.6 collective-permute-start.8
  21.1 6.3 %gradient_pieces.3.refs_0_.to_fwd.to_bwd.own_even.own_odd = bf16[8,128,1024]{2,1,0:T(8,128)(2,1)} custom-call(s32[2]{0:T(128)} %pad_add_fusion.1.spot, bf16[1024,1024]{1,0:T(8,128)(2,1)} %refs_3_.7, bf16[1024,1024]{1,0:T(8,128)(2,1)} %refs_3_.7, bf16[1024,1024]{1,0:T(8,128)(2,1)} %refs_3_.7, bf16[1024,1024]{1,0:T(8,128)(2,1)} %refs_3_.7, ...), custom_call_target="tpu_custom_call" | custom-call | flops 2147483648 | bytes 8388608 | tf_op jit(solution)/shard_map/gradient_pieces/pallas_call | solution.py:97
  27.4 7.3 %gradient_pieces.2.to_fwd.to_bwd.own_even.own_odd.refs_0_ = bf16[8,128,1280]{2,1,0:T(8,128)(2,1)} custom-call(s32[2]{0:T(128)} %pad_add_fusion.1.spot, bf16[1024,1024]{1,0:T(8,128)(2,1)} %refs_3_.7, bf16[1024,1024]{1,0:T(8,128)(2,1)} %refs_3_.7, bf16[1024,1024]{1,0:T(8,128)(2,1)} %refs_3_.7, bf16[1024,1024]{1,0:T(8,128)(2,1)} %refs_3_.7, ...), custom_call_target="tpu_custom_call" | custom-call | flops 2684354560 | bytes 9961472 | tf_op jit(solution)/shard_map/gradient_pieces/pallas_call | solution.py:97
  34.7 9.1 %collective-permute-done.7.fwd = bf16[4,128,1024]{2,1,0:T(8,128)(2,1)S(1)} collective-permute-done((bf16[4,128,1024]{2,1,0:T(8,128)(2,1)}, bf16[4,128,1024]{2,1,0:T(8,128)(2,1)S(1)}, u32[]{:S(2)}, u32[]{:S(2)}) %collective-permute-start.7) | collective-permute-done | bytes 1048608 | tf_op jit(solution)/shard_map/ppermute | solution.py:429
  43.8 0.0 collective-permute-done.8.bwd
  43.8 2.1 %copy-done = bf16[8,128,1280]{2,1,0:T(8,128)(2,1)S(1)} copy-done((bf16[8,128,1280]{2,1,0:T(8,128)(2,1)S(1)}, bf16[8,128,1280]{2,1,0:T(8,128)(2,1)}, u32[]{:S(2)}) %copy-start) | copy-done | bytes 2621464
  45.9 0.2 relay_sums.3
  46.2 0.7 copy-done.8
  46.9 1.2 collective-permute-start.9
  48.1 2.0 %collective-permute-start.10 = (bf16[2,128,1024]{2,1,0:T(8,128)(2,1)S(1)}, bf16[2,128,1024]{2,1,0:T(8,128)(2,1)S(1)}, u32[]{:S(2)}, u32[]{:S(2)}) collective-permute-start(bf16[2,128,1024]{2,1,0:T(8,128)(2,1)S(1)} %get-tuple-element.53), channel_id=1, source_target_pairs={{0,96},{8,104},{16,112},{24,120},{32,0},{40,8},{48,16},{56,24},{64... | collective-permute-start | bytes 1572872 | tf_op jit(solution)/shard_map/ppermute | solution.py:429
  50.1 0.0 collective-permute-done.fwd
  50.1 0.0 copy-start.6
  50.1 1.3 relay_sums.2
  51.5 0.4 copy-done.6
  51.8 0.3 collective-permute-start.2
  52.1 3.0 %collective-permute-start.3 = (bf16[2,128,1280]{2,1,0:T(8,128)(2,1)S(1)}, bf16[2,128,1280]{2,1,0:T(8,128)(2,1)S(1)}, u32[]{:S(2)}, u32[]{:S(2)}) collective-permute-start(bf16[2,128,1280]{2,1,0:T(8,128)(2,1)S(1)} %get-tuple-element.45), channel_id=1, source_target_pairs={{0,24},{8,0},{16,8},{24,16},{32,56},{40,32},{48,40},{56,48},{64,88... | collective-permute-start | bytes 1966088 | tf_op jit(solution)/shard_map/ppermute | solution.py:429
  55.1 5.3 %collective-permute-done.9.fwd2 = bf16[2,128,1024]{2,1,0:T(8,128)(2,1)S(1)} collective-permute-done((bf16[2,128,1024]{2,1,0:T(8,128)(2,1)S(1)}, bf16[2,128,1024]{2,1,0:T(8,128)(2,1)S(1)}, u32[]{:S(2)}, u32[]{:S(2)}) %collective-permute-start.9) | collective-permute-done | bytes 524320 | tf_op jit(solution)/shard_map/ppermute | solution.py:429
  60.4 0.8 copy-done.10
  61.2 2.0 %long_sums.3 = (bf16[128,1024]{1,0:T(8,128)(2,1)S(1)}, bf16[128,1024]{1,0:T(8,128)(2,1)S(1)}, bf16[128,1024]{1,0:T(8,128)(2,1)S(1)}, bf16[128,1024]{1,0:T(8,128)(2,1)S(1)}) custom-call(bf16[8,128,1024]{2,1,0:T(8,128)(2,1)} %gradient_pieces.3.refs_0_.to_fwd.to_bwd.own_even.own_odd, ...), custom_call_target="tpu_custom_call" | custom-call | flops 1048576 | bytes 4194304 | tf_op jit(solution)/shard_map/long_sums/pallas_call | solution.py:153
  63.3 1.8 %collective-permute-start.11 = (bf16[128,1024]{1,0:T(8,128)(2,1)S(1)}, bf16[128,1024]{1,0:T(8,128)(2,1)S(1)}, u32[]{:S(2)}, u32[]{:S(2)}) collective-permute-start(bf16[128,1024]{1,0:T(8,128)(2,1)S(1)} %get-tuple-element.55), channel_id=1, source_target_pairs={{0,16},{8,24},{16,0},{24,8},{32,48},{40,56},{48,32},{56,40},{64,80... | collective-permute-start | bytes 786440 | tf_op jit(solution)/shard_map/ppermute | solution.py:429
  65.1 0.1 slice.3
  65.1 0.7 fusion.1
  67.8 0.7 collective-permute-start.12
  68.5 2.6 %collective-permute-start.13 = (bf16[128,1024]{1,0:T(8,128)(2,1)S(1)}, bf16[128,1024]{1,0:T(8,128)(2,1)S(1)}, u32[]{:S(2)}, u32[]{:S(2)}) collective-permute-start(bf16[128,1024]{1,0:T(8,128)(2,1)S(1)} %get-tuple-element.57), channel_id=1, source_target_pairs={{0,24},{8,0},{16,8},{24,16},{32,56},{40,32},{48,40},{56,48},{64,88... | collective-permute-start | bytes 786440 | tf_op jit(solution)/shard_map/ppermute | solution.py:429
  71.1 1.7 %collective-permute-done.2.fwd2 = bf16[2,128,1280]{2,1,0:T(8,128)(2,1)S(1)} collective-permute-done((bf16[2,128,1280]{2,1,0:T(8,128)(2,1)}, bf16[2,128,1280]{2,1,0:T(8,128)(2,1)S(1)}, u32[]{:S(2)}, u32[]{:S(2)}) %collective-permute-start.2) | collective-permute-done | bytes 655392 | tf_op jit(solution)/shard_map/ppermute | solution.py:429
  72.8 0.7 collective-permute-done.3.bwd2
  73.5 0.8 copy-done.9
  74.3 2.5 %long_sums.2 = (bf16[128,1280]{1,0:T(8,128)(2,1)S(1)}, bf16[128,1280]{1,0:T(8,128)(2,1)S(1)}, bf16[128,1280]{1,0:T(8,128)(2,1)S(1)}, bf16[128,1280]{1,0:T(8,128)(2,1)S(1)}) custom-call(bf16[8,128,1280]{2,1,0:T(8,128)(2,1)} %gradient_pieces.2.to_fwd.to_bwd.own_even.own_odd.refs_0_, ...), custom_call_target="tpu_custom_call" | custom-call | flops 1310720 | bytes 5242880 | tf_op jit(solution)/shard_map/long_sums/pallas_call | solution.py:153
  76.8 0.0 copy-start.2
  76.9 0.9 collective-permute-start.4
  77.8 0.6 collective-permute-start.5
  78.4 2.7 %collective-permute-start.6 = (bf16[128,1280]{1,0:T(8,128)(2,1)S(1)}, bf16[128,1280]{1,0:T(8,128)(2,1)S(1)}, u32[]{:S(2)}, u32[]{:S(2)}) collective-permute-start(bf16[128,1280]{1,0:T(8,128)(2,1)S(1)} %get-tuple-element.49), channel_id=1, source_target_pairs={{0,96},{8,104},{16,112},{24,120},{32,0},{40,8},{48,16},{56,24},{64... | collective-permute-start | bytes 983048 | tf_op jit(solution)/shard_map/ppermute | solution.py:429
  81.0 0.1 pad_add_fusion.info
  81.1 0.2 convert_reduce_fusion
  81.3 0.1 select_reduce_fusion.1
  81.4 0.0 collective-permute-done.12.refs_6_
  81.4 4.6 %collective-permute-done.4.refs_1_ = bf16[128,1280]{1,0:T(8,128)(2,1)S(1)} collective-permute-done((bf16[128,1280]{1,0:T(8,128)(2,1)S(1)}, bf16[128,1280]{1,0:T(8,128)(2,1)S(1)}, u32[]{:S(2)}, u32[]{:S(2)}) %collective-permute-start.4) | collective-permute-done | bytes 327712 | tf_op jit(solution)/shard_map/ppermute | solution.py:429
  86.0 3.4 %collective-permute-done.5.refs_2_ = bf16[128,1280]{1,0:T(8,128)(2,1)S(1)} collective-permute-done((bf16[128,1280]{1,0:T(8,128)(2,1)S(1)}, bf16[128,1280]{1,0:T(8,128)(2,1)S(1)}, u32[]{:S(2)}, u32[]{:S(2)}) %collective-permute-start.5) | collective-permute-done | bytes 327712 | tf_op jit(solution)/shard_map/ppermute | solution.py:429
  89.3 0.1 collective-permute-done.6.refs_3_
  89.4 0.9 slices.1
  90.3 0.1 collective-permute-start.14
  90.4 0.7 collective-permute-start.15
  91.1 0.1 select_reduce_fusion
  91.2 1.9 %codes_of_own.1 = (bf16[144,1152]{1,0:T(8,128)(2,1)S(1)}, bf16[144,1152]{1,0:T(8,128)(2,1)S(1)}) custom-call(s32[3]{0:T(128)S(1)} %pad_add_fusion.info, bf16[128,1152]{1,0:T(8,128)(2,1)S(1)} %get-tuple-element.63.front.a, bf16[128,1152]{1,0:T(8,128)(2,1)S(1)} %get-tuple-element.64.back.b, f32[1,36,128,128]{3,2,1,0:T(8,128)S(1)} %copy-done.2, ...), custom_call_target="tpu_custom_call" | custom-call | flops 8847360 | bytes 7077888 | tf_op jit(solution)/shard_map/codes_of_own/pallas_call | solution.py:267
  93.1 6.3 %collective-permute-start.19 = (bf16[144,1152]{1,0:T(8,128)(2,1)S(1)}, bf16[144,1152]{1,0:T(8,128)(2,1)S(1)}, u32[]{:S(2)}, u32[]{:S(2)}) collective-permute-start(bf16[144,1152]{1,0:T(8,128)(2,1)S(1)} %get-tuple-element.72), channel_id=1, source_target_pairs={{0,8},{8,0},{16,24},{24,16},{32,40},{40,32},{48,56},{56,48},{64,72... | collective-permute-start | bytes 995336 | tf_op jit(solution)/shard_map/ppermute | solution.py:429
  99.4 0.8 collective-permute-done.14.inside
  100.2 1.9 %codes_of_halo.1 = (bf16[80,1152]{1,0:T(8,128)(2,1)S(1)}, bf16[80,1152]{1,0:T(8,128)(2,1)S(1)}, bf16[80,1152]{1,0:T(8,128)(2,1)S(1)}, bf16[80,1152]{1,0:T(8,128)(2,1)S(1)}) custom-call(s32[3]{0:T(128)S(1)} %pad_add_fusion.info, bf16[128,1152]{1,0:T(8,128)(2,1)S(1)} %collective-permute-done.14.inside, bf16[128,1152]{1,0:T(8,128)(2,1)S(1)} %collective-permute-done.15.cross, ...), custom_call_target="tpu_custom_call" | custom-call | flops 8847360 | bytes 7077888 | tf_op jit(solution)/shard_map/codes_of_halo/pallas_call | solution.py:267
  102.1 1.9 %collective-permute-start.16 = (bf16[80,1152]{1,0:T(8,128)(2,1)S(1)}, bf16[80,1152]{1,0:T(8,128)(2,1)S(1)}, u32[]{:S(2)}, u32[]{:S(2)}) collective-permute-start(bf16[80,1152]{1,0:T(8,128)(2,1)S(1)} %get-tuple-element.60), channel_id=1, source_target_pairs={{0,8},{8,0},{16,24},{24,16},{32,40},{40,32},{48,56},{56,48},{64,72... | collective-permute-start | bytes 552968 | tf_op jit(solution)/shard_map/ppermute | solution.py:429
  104.0 0.7 collective-permute-start.17
  104.6 1.3 collective-permute-start.18
  105.9 0.1 pad_add_fusion.2.info
  106.0 4.3 %update_state.1 = (f32[1,36,128,128]{3,2,1,0:T(8,128)}, f32[1,36,128,128]{3,2,1,0:T(8,128)}, f32[1,36,128,128]{3,2,1,0:T(8,128)}) custom-call(s32[3]{0:T(128)S(1)} %pad_add_fusion.info, bf16[128,1152]{1,0:T(8,128)(2,1)S(1)} %collective-permute-done.14.inside, bf16[128,1152]{1,0:T(8,128)(2,1)S(1)} %get-tuple-element.63.front.a, ...), custom_call_target="tpu_custom_call" | custom-call | flops 11796480 | bytes 15335424 | tf_op jit(solution)/shard_map/update_state/pallas_call | solution.py:312
  110.3 5.2 %collective-permute-done.18.far = bf16[80,1152]{1,0:T(8,128)(2,1)S(1)} collective-permute-done((bf16[80,1152]{1,0:T(8,128)(2,1)S(1)}, bf16[80,1152]{1,0:T(8,128)(2,1)S(1)}, u32[]{:S(2)}, u32[]{:S(2)}) %collective-permute-start.18) | collective-permute-done | bytes 184352 | tf_op jit(solution)/shard_map/ppermute | solution.py:429
  115.5 1.3 pack_by_owner.1
  116.8 27.6 %all_to_all.10 = bf16[16,304,128]{2,1,0:T(8,128)(2,1)S(1)} all-to-all(bf16[16,304,128]{2,1,0:T(8,128)(2,1)S(1)} %pack_by_owner.1), channel_id=1, replica_groups=mesh['yh'=2,'yl'=2,'x'=4,'z'=4,'core'=2] {'z','core','yh'}, dimensions={0} | all-to-all | bytes 2490368 | tf_op jit(solution)/shard_map/all_to_all | solution.py:514
  144.4 23.1 %all_to_all.11.got = bf16[16,304,128]{2,1,0:T(8,128)(2,1)S(1)} all-to-all(bf16[16,304,128]{2,1,0:T(8,128)(2,1)S(1)} %all_to_all.10), channel_id=1, replica_groups=mesh['yh'=2,'yl'=2,'x'=4,'z'=4,'core'=2] {'yh','yl','x'}, dimensions={0} | all-to-all | bytes 2490368 | tf_op jit(solution)/shard_map/all_to_all | solution.py:515
  167.5 1.1 place_served.1
  168.6 0.7 copy.14
  (32 shorter events, 0.1 us)
Async XLA Ops:
  8.4 41.7 %collective-permute-start = (bf16[4,128,1280]{2,1,0:T(8,128)(2,1)}, bf16[4,128,1280]{2,1,0:T(8,128)(2,1)S(1)}, u32[]{:S(2)}, u32[]{:S(2)}) collective-permute-start(bf16[4,128,1280]{2,1,0:T(8,128)(2,1)} %get-tuple-element.42), channel_id=1, source_target_pairs={{0,8},{8,16},{16,24},{24,0},{32,40},{40,48},{48,56},{56,32},{64,72... | collective-permute-start | bytes 3932168 | tf_op jit(solution)/shard_map/ppermute | solution.py:429
  10.0 40.2 %collective-permute-start.1 = (bf16[4,128,1280]{2,1,0:T(8,128)(2,1)}, bf16[4,128,1280]{2,1,0:T(8,128)(2,1)S(1)}, u32[]{:S(2)}, u32[]{:S(2)}) collective-permute-start(bf16[4,128,1280]{2,1,0:T(8,128)(2,1)} %get-tuple-element.43), channel_id=1, source_target_pairs={{0,24},{8,0},{16,8},{24,16},{32,56},{40,32},{48,40},{56,48},{64,88... | collective-permute-start | bytes 3932168 | tf_op jit(solution)/shard_map/ppermute | solution.py:429
  17.9 25.9 %collective-permute-start.7 = (bf16[4,128,1024]{2,1,0:T(8,128)(2,1)}, bf16[4,128,1024]{2,1,0:T(8,128)(2,1)S(1)}, u32[]{:S(2)}, u32[]{:S(2)}) collective-permute-start(bf16[4,128,1024]{2,1,0:T(8,128)(2,1)} %get-tuple-element.50), channel_id=1, source_target_pairs={{0,32},{8,40},{16,48},{24,56},{32,64},{40,72},{48,80},{56,88},{64,... | collective-permute-start | bytes 3145736 | tf_op jit(solution)/shard_map/ppermute | solution.py:429
  19.5 24.3 %collective-permute-start.8 = (bf16[4,128,1024]{2,1,0:T(8,128)(2,1)}, bf16[4,128,1024]{2,1,0:T(8,128)(2,1)S(1)}, u32[]{:S(2)}, u32[]{:S(2)}) collective-permute-start(bf16[4,128,1024]{2,1,0:T(8,128)(2,1)} %get-tuple-element.51), channel_id=1, source_target_pairs={{0,96},{8,104},{16,112},{24,120},{32,0},{40,8},{48,16},{56,24},{64... | collective-permute-start | bytes 3145736 | tf_op jit(solution)/shard_map/ppermute | solution.py:429
  27.4 16.4 %copy-start.1 = (bf16[8,128,1024]{2,1,0:T(8,128)(2,1)S(1)}, bf16[8,128,1024]{2,1,0:T(8,128)(2,1)}, u32[]{:S(2)}) copy-start(bf16[8,128,1024]{2,1,0:T(8,128)(2,1)} %gradient_pieces.3.refs_0_.to_fwd.to_bwd.own_even.own_odd) | copy-start | bytes 6291460
  43.8 2.4 %copy-start.7 = (bf16[4,128,1024]{2,1,0:T(8,128)(2,1)}, bf16[4,128,1024]{2,1,0:T(8,128)(2,1)S(1)}, u32[]{:S(2)}) copy-start(bf16[4,128,1024]{2,1,0:T(8,128)(2,1)S(1)} %collective-permute-done.7.fwd) | copy-start | bytes 3145732
  43.8 2.1 %copy-start = (bf16[8,128,1280]{2,1,0:T(8,128)(2,1)S(1)}, bf16[8,128,1280]{2,1,0:T(8,128)(2,1)}, u32[]{:S(2)}) copy-start(bf16[8,128,1280]{2,1,0:T(8,128)(2,1)} %gradient_pieces.2.to_fwd.to_bwd.own_even.own_odd.refs_0_) | copy-start | bytes 7864324
  45.9 1.0 copy-start.8
  46.9 13.5 %collective-permute-start.9 = (bf16[2,128,1024]{2,1,0:T(8,128)(2,1)S(1)}, bf16[2,128,1024]{2,1,0:T(8,128)(2,1)S(1)}, u32[]{:S(2)}, u32[]{:S(2)}) collective-permute-start(bf16[2,128,1024]{2,1,0:T(8,128)(2,1)S(1)} %get-tuple-element.52), channel_id=1, source_target_pairs={{0,32},{8,40},{16,48},{24,56},{32,64},{40,72},{48,80},{56,88},{64,... | collective-permute-start | bytes 1572872 | tf_op jit(solution)/shard_map/ppermute | solution.py:429
  48.1 12.3 %collective-permute-start.10 = (bf16[2,128,1024]{2,1,0:T(8,128)(2,1)S(1)}, bf16[2,128,1024]{2,1,0:T(8,128)(2,1)S(1)}, u32[]{:S(2)}, u32[]{:S(2)}) collective-permute-start(bf16[2,128,1024]{2,1,0:T(8,128)(2,1)S(1)} %get-tuple-element.53), channel_id=1, source_target_pairs={{0,96},{8,104},{16,112},{24,120},{32,0},{40,8},{48,16},{56,24},{64... | collective-permute-start | bytes 1572872 | tf_op jit(solution)/shard_map/ppermute | solution.py:429
  50.1 1.3 copy-start.5
  50.1 1.7 %copy-start.6 = (bf16[4,128,1280]{2,1,0:T(8,128)(2,1)}, bf16[4,128,1280]{2,1,0:T(8,128)(2,1)S(1)}, u32[]{:S(2)}) copy-start(bf16[4,128,1280]{2,1,0:T(8,128)(2,1)S(1)} %collective-permute-done.1.bwd) | copy-start | bytes 3932164
  51.8 21.0 %collective-permute-start.2 = (bf16[2,128,1280]{2,1,0:T(8,128)(2,1)}, bf16[2,128,1280]{2,1,0:T(8,128)(2,1)S(1)}, u32[]{:S(2)}, u32[]{:S(2)}) collective-permute-start(bf16[2,128,1280]{2,1,0:T(8,128)(2,1)} %get-tuple-element.44), channel_id=1, source_target_pairs={{0,8},{8,16},{16,24},{24,0},{32,40},{40,48},{48,56},{56,32},{64,72... | collective-permute-start | bytes 1966088 | tf_op jit(solution)/shard_map/ppermute | solution.py:429
  52.1 12.9 %copy-start.12 = (s32[16]{0:T(128)S(1)}, s32[16]{0:T(128)}, u32[]{:S(2)}) copy-start(s32[16]{0:T(128)} %param.13) | copy-start | bytes 196
  52.1 21.4 %collective-permute-start.3 = (bf16[2,128,1280]{2,1,0:T(8,128)(2,1)S(1)}, bf16[2,128,1280]{2,1,0:T(8,128)(2,1)S(1)}, u32[]{:S(2)}, u32[]{:S(2)}) collective-permute-start(bf16[2,128,1280]{2,1,0:T(8,128)(2,1)S(1)} %get-tuple-element.45), channel_id=1, source_target_pairs={{0,24},{8,0},{16,8},{24,16},{32,56},{40,32},{48,40},{56,48},{64,88... | collective-permute-start | bytes 1966088 | tf_op jit(solution)/shard_map/ppermute | solution.py:429
  60.4 0.8 copy-start.10
  63.3 15.1 %collective-permute-start.11 = (bf16[128,1024]{1,0:T(8,128)(2,1)S(1)}, bf16[128,1024]{1,0:T(8,128)(2,1)S(1)}, u32[]{:S(2)}, u32[]{:S(2)}) collective-permute-start(bf16[128,1024]{1,0:T(8,128)(2,1)S(1)} %get-tuple-element.55), channel_id=1, source_target_pairs={{0,16},{8,24},{16,0},{24,8},{32,48},{40,56},{48,32},{56,40},{64,80... | collective-permute-start | bytes 786440 | tf_op jit(solution)/shard_map/ppermute | solution.py:429
  67.8 13.6 %collective-permute-start.12 = (bf16[128,1024]{1,0:T(8,128)(2,1)S(1)}, bf16[128,1024]{1,0:T(8,128)(2,1)S(1)}, u32[]{:S(2)}, u32[]{:S(2)}) collective-permute-start(bf16[128,1024]{1,0:T(8,128)(2,1)S(1)} %get-tuple-element.56), channel_id=1, source_target_pairs={{0,8},{8,16},{16,24},{24,0},{32,40},{40,48},{48,56},{56,32},{64,72... | collective-permute-start | bytes 786440 | tf_op jit(solution)/shard_map/ppermute | solution.py:429
  68.5 12.6 %copy-start.11 = (s32[36]{0:T(128)S(1)}, s32[36]{0:T(128)}, u32[]{:S(2)}) copy-start(s32[36]{0:T(128)} %param.14) | copy-start | bytes 436
  68.5 12.8 %copy-start.13 = (s32[32]{0:T(128)S(1)}, s32[32]{0:T(128)}, u32[]{:S(2)}) copy-start(s32[32]{0:T(128)} %param.15) | copy-start | bytes 388
  68.5 12.9 %collective-permute-start.13 = (bf16[128,1024]{1,0:T(8,128)(2,1)S(1)}, bf16[128,1024]{1,0:T(8,128)(2,1)S(1)}, u32[]{:S(2)}, u32[]{:S(2)}) collective-permute-start(bf16[128,1024]{1,0:T(8,128)(2,1)S(1)} %get-tuple-element.57), channel_id=1, source_target_pairs={{0,24},{8,0},{16,8},{24,16},{32,56},{40,32},{48,40},{56,48},{64,88... | collective-permute-start | bytes 786440 | tf_op jit(solution)/shard_map/ppermute | solution.py:429
  73.5 0.8 copy-start.9
  74.3 16.9 %copy-start.3 = (f32[1,36,128,128]{3,2,1,0:T(8,128)S(1)}, f32[1,36,128,128]{3,2,1,0:T(8,128)}, u32[]{:S(2)}) copy-start(f32[1,36,128,128]{3,2,1,0:T(8,128)} %moment.5) | copy-start | bytes 7077892
  74.3 16.9 %copy-start.4 = (f32[1,36,128,128]{3,2,1,0:T(8,128)S(1)}, f32[1,36,128,128]{3,2,1,0:T(8,128)}, u32[]{:S(2)}) copy-start(f32[1,36,128,128]{3,2,1,0:T(8,128)} %variance.5) | copy-start | bytes 7077892
  76.8 14.4 %copy-start.2 = (f32[1,36,128,128]{3,2,1,0:T(8,128)S(1)}, f32[1,36,128,128]{3,2,1,0:T(8,128)}, u32[]{:S(2)}) copy-start(f32[1,36,128,128]{3,2,1,0:T(8,128)} %master.5) | copy-start | bytes 7077892
  76.9 9.1 %collective-permute-start.4 = (bf16[128,1280]{1,0:T(8,128)(2,1)S(1)}, bf16[128,1280]{1,0:T(8,128)(2,1)S(1)}, u32[]{:S(2)}, u32[]{:S(2)}) collective-permute-start(bf16[128,1280]{1,0:T(8,128)(2,1)S(1)} %get-tuple-element.47), channel_id=1, source_target_pairs={{0,64},{8,72},{16,80},{24,88},{32,96},{40,104},{48,112},{56,120},{... | collective-permute-start | bytes 983048 | tf_op jit(solution)/shard_map/ppermute | solution.py:429
  77.8 11.5 %collective-permute-start.5 = (bf16[128,1280]{1,0:T(8,128)(2,1)S(1)}, bf16[128,1280]{1,0:T(8,128)(2,1)S(1)}, u32[]{:S(2)}, u32[]{:S(2)}) collective-permute-start(bf16[128,1280]{1,0:T(8,128)(2,1)S(1)} %get-tuple-element.48), channel_id=1, source_target_pairs={{0,32},{8,40},{16,48},{24,56},{32,64},{40,72},{48,80},{56,88},{64,... | collective-permute-start | bytes 983048 | tf_op jit(solution)/shard_map/ppermute | solution.py:429
  78.4 11.0 %collective-permute-start.6 = (bf16[128,1280]{1,0:T(8,128)(2,1)S(1)}, bf16[128,1280]{1,0:T(8,128)(2,1)S(1)}, u32[]{:S(2)}, u32[]{:S(2)}) collective-permute-start(bf16[128,1280]{1,0:T(8,128)(2,1)S(1)} %get-tuple-element.49), channel_id=1, source_target_pairs={{0,96},{8,104},{16,112},{24,120},{32,0},{40,8},{48,16},{56,24},{64... | collective-permute-start | bytes 983048 | tf_op jit(solution)/shard_map/ppermute | solution.py:429
  90.3 9.9 %collective-permute-start.14 = (bf16[128,1152]{1,0:T(8,128)(2,1)S(1)}, bf16[128,1152]{1,0:T(8,128)(2,1)S(1)}, u32[]{:S(2)}, u32[]{:S(2)}) collective-permute-start(bf16[128,1152]{1,0:T(8,128)(2,1)S(1)} %get-tuple-element.58), channel_id=1, source_target_pairs={{0,8},{8,0},{16,24},{24,16},{32,40},{40,32},{48,56},{56,48},{64,72... | collective-permute-start | bytes 884744 | tf_op jit(solution)/shard_map/ppermute | solution.py:429
  90.4 9.8 %collective-permute-start.15 = (bf16[128,1152]{1,0:T(8,128)(2,1)S(1)}, bf16[128,1152]{1,0:T(8,128)(2,1)S(1)}, u32[]{:S(2)}, u32[]{:S(2)}) collective-permute-start(bf16[128,1152]{1,0:T(8,128)(2,1)S(1)} %get-tuple-element.59), channel_id=1, source_target_pairs={{8,16},{16,8},{24,32},{32,24},{40,48},{48,40},{56,64},{64,56},{72,... | collective-permute-start | bytes 884744 | tf_op jit(solution)/shard_map/ppermute | solution.py:429
  93.1 22.4 %collective-permute-start.19 = (bf16[144,1152]{1,0:T(8,128)(2,1)S(1)}, bf16[144,1152]{1,0:T(8,128)(2,1)S(1)}, u32[]{:S(2)}, u32[]{:S(2)}) collective-permute-start(bf16[144,1152]{1,0:T(8,128)(2,1)S(1)} %get-tuple-element.72), channel_id=1, source_target_pairs={{0,8},{8,0},{16,24},{24,16},{32,40},{40,32},{48,56},{56,48},{64,72... | collective-permute-start | bytes 995336 | tf_op jit(solution)/shard_map/ppermute | solution.py:429
  102.1 8.2 %collective-permute-start.16 = (bf16[80,1152]{1,0:T(8,128)(2,1)S(1)}, bf16[80,1152]{1,0:T(8,128)(2,1)S(1)}, u32[]{:S(2)}, u32[]{:S(2)}) collective-permute-start(bf16[80,1152]{1,0:T(8,128)(2,1)S(1)} %get-tuple-element.60), channel_id=1, source_target_pairs={{0,8},{8,0},{16,24},{24,16},{32,40},{40,32},{48,56},{56,48},{64,72... | collective-permute-start | bytes 552968 | tf_op jit(solution)/shard_map/ppermute | solution.py:429
  104.0 6.3 %collective-permute-start.17 = (bf16[80,1152]{1,0:T(8,128)(2,1)S(1)}, bf16[80,1152]{1,0:T(8,128)(2,1)S(1)}, u32[]{:S(2)}, u32[]{:S(2)}) collective-permute-start(bf16[80,1152]{1,0:T(8,128)(2,1)S(1)} %get-tuple-element.61), channel_id=1, source_target_pairs={{8,16},{16,8},{24,32},{32,24},{40,48},{48,40},{56,64},{64,56},{72,... | collective-permute-start | bytes 552968 | tf_op jit(solution)/shard_map/ppermute | solution.py:429
  104.6 10.9 %collective-permute-start.18 = (bf16[80,1152]{1,0:T(8,128)(2,1)S(1)}, bf16[80,1152]{1,0:T(8,128)(2,1)S(1)}, u32[]{:S(2)}, u32[]{:S(2)}) collective-permute-start(bf16[80,1152]{1,0:T(8,128)(2,1)S(1)} %get-tuple-element.62), channel_id=1, source_target_pairs={{8,24},{16,0},{24,40},{32,16},{40,56},{48,32},{56,72},{64,48},{72,... | collective-permute-start | bytes 552968 | tf_op jit(solution)/shard_map/ppermute | solution.py:429
